TPU v7x, 256 devices: a whole 4x4x8 slice. The times are simulated.
256 devices in a mesh: queue: 128 (over z, y, x), seq: 2 (over core).
Axes of the slice: x: 4, y: 4, z: 8, core: 2. Of those that a mesh axis runs over, the one named last changes fastest.
Arguments:
- latents: bfloat16 [128, 256, 3072], P('queue', 'seq'), may hold values from -6 to 6
- fresh_noise: bfloat16 [2, 256, 3072], P(None, 'seq'), may hold values from -6 to 6
- levels: int32 [128], replicated, may hold values from 0 to 49
- pattern: int32 [4, 12], replicated, may hold values 0 or 1
- entry: int32 [2], replicated, may hold values from 0 to 127
- level_scale: float32 [50, 3072], replicated, may hold values from -1.5 to 1.5
- level_shift: float32 [50, 3072], replicated, may hold values from -3 to 3
- step_size: float32 [50], replicated, may hold values from 0.2 to 1
- qk_gain: float32 [2, 64], replicated, may hold values from 0.5 to 2
- wq: bfloat16 [3072, 1536], P(None, 'seq'), may hold values from -0.109375 to 0.109375
- wk: bfloat16 [3072, 1536], P(None, 'seq'), may hold values from -0.109375 to 0.109375
- wv: bfloat16 [3072, 1536], P(None, 'seq'), may hold values from -0.109375 to 0.109375
- wo: bfloat16 [1536, 3072], P('seq'), may hold values from -0.15625 to 0.15625
Outputs:
- result: bfloat16 [128, 256, 3072], P('queue', 'seq')
All inputs are finite; a program needn't handle non-finite values.
Results may differ from a plain program's by a relative error of at most 0.012.
Values may be sent and summed in bfloat16 or wider, within the bound.
No kernel may reach another device: no remote copies, remote signals or barrier semaphores. Data moves between devices by JAX's collectives and lax.ppermute only.
A program may use at most 128 MiB of HBM per device.

v0:
```python
import math

import jax
import jax.numpy as jnp
from jax import lax
from jax.sharding import PartitionSpec as P

HD = 64
FRAMES = 4
ITERS = 2


def shifted(shard, axis, by):
    count = lax.axis_size(axis)
    pairs = [(i, i + by) for i in range(count) if 0 <= i + by < count]
    return lax.ppermute(shard, axis, pairs)


def shifted_2(block, axis, distance):
    devices = range(lax.axis_size(axis))
    route = [((i - distance) % len(devices), i) for i in devices]
    return lax.ppermute(block, axis, route)


def modulate(slot_state, scale_row, shift_row):
    values = slot_state.astype(jnp.float32)
    normed = values * lax.rsqrt(jnp.mean(values * values, axis=-1, keepdims=True) + 1e-06)
    return (normed * (1.0 + scale_row) + shift_row).astype(jnp.bfloat16)


def head_norm(values, gain):
    return (
        values * lax.rsqrt(jnp.mean(values * values, axis=-1, keepdims=True) + 1e-06) * gain
    ).astype(jnp.bfloat16)


def allowed_keys(pattern, logical, queue_count, token_count):
    frame_tokens = token_count // FRAMES
    block_index = jnp.arange(3 * FRAMES, dtype=jnp.int32) // FRAMES
    present = (
        (block_index == 1)
        | (block_index == 0) & (logical > 0)
        | (block_index == 2) & (logical < queue_count - 1)
    )
    own_frame = (
        jnp.arange(3 * FRAMES, dtype=jnp.int32)[None, :]
        == (FRAMES + jnp.arange(FRAMES, dtype=jnp.int32))[:, None]
    )
    frame_table = ((pattern == 1) | own_frame) & present[None, :]
    return jnp.repeat(jnp.repeat(frame_table, frame_tokens, axis=0), frame_tokens, axis=1)


def attend(query, keys, values, allowed):
    scale = 1.0 / math.sqrt(HD)

    def one_head(operands):
        query_head, key_head, value_head = operands
        scores = jnp.dot(query_head, key_head.T, preferred_element_type=jnp.float32) * scale
        scores = jnp.where(allowed, scores, -1e30)
        highest = jnp.max(scores, axis=-1, keepdims=True)
        expo = jnp.exp(scores - highest)
        weights = (expo / jnp.sum(expo, axis=-1, keepdims=True)).astype(jnp.bfloat16)
        return jnp.dot(weights, value_head, preferred_element_type=jnp.float32).astype(jnp.bfloat16)

    heads = lax.map(
        one_head, (query.transpose(1, 0, 2), keys.transpose(1, 0, 2), values.transpose(1, 0, 2))
    )
    return heads.transpose(1, 0, 2)


def on_device(
    latents,
    fresh_noise,
    levels,
    pattern,
    entry,
    level_scale,
    level_shift,
    step_size,
    qk_gain,
    wq,
    wk,
    wv,
    wo,
):
    queue_count = lax.axis_size("queue")
    place = lax.axis_index("queue")
    state = latents[0]
    for step_index in range(ITERS):
        level_now = levels[place]
        modulated = modulate(state, level_scale[level_now], level_shift[level_now])
        whole = lax.all_gather(modulated, "seq", axis=0, tiled=True)
        token_count = whole.shape[0]
        width = wq.shape[1]
        local_heads = width // HD
        query = head_norm(
            jnp.dot(whole, wq, preferred_element_type=jnp.float32).reshape(
                token_count, local_heads, HD
            ),
            qk_gain[0],
        )
        keys = head_norm(
            jnp.dot(whole, wk, preferred_element_type=jnp.float32).reshape(
                token_count, local_heads, HD
            ),
            qk_gain[1],
        )
        values = (
            jnp.dot(whole, wv, preferred_element_type=jnp.float32)
            .astype(jnp.bfloat16)
            .reshape(token_count, local_heads, HD)
        )
        before = shifted((keys, values), "queue", 1)
        after = shifted((keys, values), "queue", -1)
        key_window = jnp.concatenate([before[0], keys, after[0]], axis=0)
        value_window = jnp.concatenate([before[1], values, after[1]], axis=0)
        allowed = allowed_keys(pattern, place, queue_count, token_count)
        attended = attend(query, key_window, value_window, allowed).reshape(token_count, width)
        velocity = lax.psum_scatter(
            jnp.dot(attended, wo, preferred_element_type=jnp.float32).astype(jnp.bfloat16),
            "seq",
            scatter_dimension=0,
            tiled=True,
        ).astype(jnp.float32)
        updated = (state.astype(jnp.float32) + step_size[level_now] * velocity).astype(jnp.bfloat16)
        moved = shifted_2(updated, "queue", 1)
        state = jnp.where(place == entry[step_index], fresh_noise[step_index], moved)
    return state[None]


def solution(mesh):
    return jax.shard_map(
        on_device,
        mesh=mesh,
        in_specs=(
            P("queue", "seq", None),
            P(None, "seq", None),
            P(),
            P(),
            P(),
            P(),
            P(),
            P(),
            P(),
            P(None, "seq"),
            P(None, "seq"),
            P(None, "seq"),
            P("seq", None),
        ),
        out_specs=P("queue", "seq", None),
        check_vma=False,
    )
```

profile of v0, /device:TPU:1, one launch (start us, length us, event | category | flops | bytes accessed | tf_op | source)
XLA Modules:
  0.0 279.0 jit_solution(13647552570094393578)
XLA Ops:
  9.1 1.4 fusion.33
  12.7 2.3 fusion.36
  15.6 19.3 %all-gather.3.cloned.1.call-done = bf16[256,3072]{1,0:T(8,128)(2,1)} async-done(((bf16[128,3072]{1,0:T(8,128)(2,1)}), bf16[256,3072]{1,0:T(8,128)(2,1)}) %all-gather.3.cloned.1.call-update) | async-done | bytes 1572880 | tf_op jit(solution)/shard_map/all_gather | solution.py:92
  34.9 4.8 %fusion.47 = f32[256,768]{0,1:T(8,128)S(1)} fusion(bf16[256,3072]{1,0:T(8,128)(2,1)} %all-gather.3.cloned.1.call-done, bf16[3072,768]{1,0:T(8,128)(2,1)} %param.27), kind=kOutput, calls=%fused_computation.94 | convolution fusion | flops 1207959552 | bytes 7077888 | tf_op jit(solution)/shard_map/dot_general | solution.py:103
  40.0 1.4 collective-permute-start.1
  41.4 4.0 %collective-permute-start = (bf16[256,12,64]{0,2,1:T(8,128)(2,1)S(1)}, bf16[256,12,64]{0,2,1:T(8,128)(2,1)S(1)}, u32[]{:S(2)}, u32[]{:S(2)}) collective-permute-start(bf16[256,12,64]{0,2,1:T(8,128)(2,1)S(1)} %multiply_convert_fusion.2), channel_id=1, source_target_pairs={{0,2},{2,4},{4,6},{6,8},{8,10},{10,12},{12,14},{14,16},{16,18},{18... | collective-permute-start | bytes 1179656 | tf_op jit(solution)/shard_map/ppermute | solution.py:16
  45.4 3.7 %convolution_convert_fusion.5 = bf16[256,768]{1,0:T(8,128)(2,1)S(1)} fusion(bf16[256,3072]{1,0:T(8,128)(2,1)S(1)} %copy-done.12, bf16[3072,768]{1,0:T(8,128)(2,1)} %param.28), kind=kOutput, calls=%fused_computation.53 | convolution fusion | flops 1208156160 | bytes 6684672 | tf_op jit(solution)/shard_map/dot_general | solution.py:109
  49.3 1.3 collective-permute-start.3
  50.6 4.0 %collective-permute-start.2 = (bf16[256,12,64]{0,2,1:T(8,128)(2,1)S(1)}, bf16[256,12,64]{0,2,1:T(8,128)(2,1)S(1)}, u32[]{:S(2)}, u32[]{:S(2)}) collective-permute-start(bf16[256,12,64]{0,2,1:T(8,128)(2,1)S(1)} %bitcast.141), channel_id=1, source_target_pairs={{0,2},{2,4},{4,6},{6,8},{8,10},{10,12},{12,14},{14,16},{16,18},{18... | collective-permute-start | bytes 1179656 | tf_op jit(solution)/shard_map/ppermute | solution.py:16
  54.6 4.8 %fusion.46 = f32[256,768]{0,1:T(8,128)S(1)} fusion(bf16[256,3072]{1,0:T(8,128)(2,1)} %all-gather.3.cloned.1.call-done, bf16[3072,768]{1,0:T(8,128)(2,1)} %param.26), kind=kOutput, calls=%fused_computation.93 | convolution fusion | flops 1207959552 | bytes 7077888 | tf_op jit(solution)/shard_map/dot_general | solution.py:97
  59.8 1.3 collective-permute-done.3
  62.1 17.2 %while.22 = (s32[]{:T(128)}, bf16[12,256,64]{1,2,0:T(8,128)(2,1)S(1)}, bf16[12,256,64]{1,2,0:T(8,128)(2,1)S(1)}, bf16[12,768,64]{1,2,0:T(8,128)(2,1)S(1)}, bf16[...) while((s32[]{:T(128)}, bf16[12,256,64]{1,2,0:T(8,128)(2,1)S(1)}, ...), condition=%wide.region_6.7_spmd.clone, body=%wide.region_3.6_spmd.clone.sunk | while | flops 51920384 | bytes 3418197 | solution.py:65
  79.2 4.9 %convolution_convert_fusion.3 = bf16[256,3072]{1,0:T(8,128)(2,1)} fusion(bf16[256,768]{0,1:T(8,128)(2,1)S(1)} %bitcast.139, bf16[768,3072]{1,0:T(8,128)(2,1)} %param.29), kind=kOutput, calls=%fused_computation.35 | convolution fusion | flops 1208745984 | bytes 6684672 | tf_op jit(solution)/shard_map/dot_general | solution.py:120
  85.5 27.5 %reduce-scatter.3.cloned.1.call-done = bf16[128,3072]{1,0:T(8,128)(2,1)} async-done(((bf16[256,3072]{1,0:T(8,128)(2,1)}), bf16[128,3072]{1,0:T(8,128)(2,1)}) %reduce-scatter.3.cloned.1.call-update) | async-done | bytes 786448 | tf_op jit(solution)/shard_map/reduce_scatter | solution.py:119
  113.0 2.0 fusion.37
  117.2 22.7 %collective-permute-done.4 = bf16[128,3072]{1,0:T(8,128)(2,1)} collective-permute-done((bf16[128,3072]{1,0:T(8,128)(2,1)S(1)}, bf16[128,3072]{1,0:T(8,128)(2,1)}, u32[]{:S(2)}, u32[]{:S(2)}) %collective-permute-start.4) | collective-permute-done | bytes 786464 | tf_op jit(solution)/shard_map/ppermute | solution.py:22
  140.0 1.5 fusion.28
  143.0 11.9 %all-gather.5.cloned.1.call-done = bf16[256,3072]{1,0:T(8,128)(2,1)} async-done(((bf16[128,3072]{1,0:T(8,128)(2,1)}), bf16[256,3072]{1,0:T(8,128)(2,1)}) %all-gather.5.cloned.1.call-update) | async-done | bytes 1572880 | tf_op jit(solution)/shard_map/all_gather | solution.py:92
  154.8 4.8 %fusion.49 = f32[256,768]{0,1:T(8,128)S(1)} fusion(bf16[256,3072]{1,0:T(8,128)(2,1)} %all-gather.5.cloned.1.call-done, bf16[3072,768]{1,0:T(8,128)(2,1)} %param.27), kind=kOutput, calls=%fused_computation.96 | convolution fusion | flops 1207959552 | bytes 7077888 | tf_op jit(solution)/shard_map/dot_general | solution.py:103
  159.9 1.4 collective-permute-start.6
  161.4 4.7 %collective-permute-start.5 = (bf16[256,12,64]{0,2,1:T(8,128)(2,1)S(1)}, bf16[256,12,64]{0,2,1:T(8,128)(2,1)}, u32[]{:S(2)}, u32[]{:S(2)}) collective-permute-start(bf16[256,12,64]{0,2,1:T(8,128)(2,1)S(1)} %multiply_convert_fusion), channel_id=1, source_target_pairs={{0,2},{2,4},{4,6},{6,8},{8,10},{10,12},{12,14},{14,16},{16,18},{18... | collective-permute-start | bytes 1179656 | tf_op jit(solution)/shard_map/ppermute | solution.py:16
  166.1 3.7 %convolution_convert_fusion.4 = bf16[256,768]{1,0:T(8,128)(2,1)S(1)} fusion(bf16[256,3072]{1,0:T(8,128)(2,1)S(1)} %copy-done.13, bf16[3072,768]{1,0:T(8,128)(2,1)} %param.28), kind=kOutput, calls=%fused_computation.52 | convolution fusion | flops 1208156160 | bytes 6684672 | tf_op jit(solution)/shard_map/dot_general | solution.py:109
  170.0 1.3 collective-permute-start.8
  171.3 4.0 %collective-permute-start.7 = (bf16[256,12,64]{0,2,1:T(8,128)(2,1)S(1)}, bf16[256,12,64]{0,2,1:T(8,128)(2,1)S(1)}, u32[]{:S(2)}, u32[]{:S(2)}) collective-permute-start(bf16[256,12,64]{0,2,1:T(8,128)(2,1)S(1)} %bitcast.144), channel_id=1, source_target_pairs={{0,2},{2,4},{4,6},{6,8},{8,10},{10,12},{12,14},{14,16},{16,18},{18... | collective-permute-start | bytes 1179656 | tf_op jit(solution)/shard_map/ppermute | solution.py:16
  175.3 4.8 %fusion.48 = f32[256,768]{0,1:T(8,128)S(1)} fusion(bf16[256,3072]{1,0:T(8,128)(2,1)} %all-gather.5.cloned.1.call-done, bf16[3072,768]{1,0:T(8,128)(2,1)} %param.26), kind=kOutput, calls=%fused_computation.95 | convolution fusion | flops 1207959552 | bytes 7077888 | tf_op jit(solution)/shard_map/dot_general | solution.py:97
  183.8 27.8 %while.23 = (s32[]{:T(128)}, bf16[12,256,64]{1,2,0:T(8,128)(2,1)S(1)}, bf16[12,256,64]{1,2,0:T(8,128)(2,1)S(1)}, bf16[12,768,64]{1,2,0:T(8,128)(2,1)S(1)}, bf16[...) while((s32[]{:T(128)}, bf16[12,256,64]{1,2,0:T(8,128)(2,1)S(1)}, ...), condition=%wide.region_14.15_spmd.clone, body=%wide.region_11.14_spmd.clone.sunk | while | flops 51920384 | bytes 3418197 | solution.py:65
  184.8 1.3 fusion.81
  187.1 1.3 fusion.81
  211.5 4.9 %convolution_convert_fusion.2 = bf16[256,3072]{1,0:T(8,128)(2,1)} fusion(bf16[256,768]{0,1:T(8,128)(2,1)S(1)} %bitcast.138, bf16[768,3072]{1,0:T(8,128)(2,1)} %param.29), kind=kOutput, calls=%fused_computation.34 | convolution fusion | flops 1208745984 | bytes 6684672 | tf_op jit(solution)/shard_map/dot_general | solution.py:120
  216.5 28.0 %reduce-scatter.5.cloned.1.call-done = bf16[128,3072]{1,0:T(8,128)(2,1)} async-done(((bf16[256,3072]{1,0:T(8,128)(2,1)}), bf16[128,3072]{1,0:T(8,128)(2,1)}) %reduce-scatter.5.cloned.1.call-update) | async-done | bytes 786448 | tf_op jit(solution)/shard_map/reduce_scatter | solution.py:119
  244.6 2.0 fusion.32
  248.2 23.3 %collective-permute-done.9 = bf16[128,3072]{1,0:T(8,128)(2,1)S(1)} collective-permute-done((bf16[128,3072]{1,0:T(8,128)(2,1)S(1)}, bf16[128,3072]{1,0:T(8,128)(2,1)S(1)}, u32[]{:S(2)}, u32[]{:S(2)}) %collective-permute-start.9) | collective-permute-done | bytes 786464 | tf_op jit(solution)/shard_map/ppermute | solution.py:22
  (200 shorter events, 57.4 us)
Async XLA Ops:
  6.5 28.3 %all-gather.3.cloned.1.call-start = ((), (), s32[]{:S(2)}) async-start(), calls=%async_computation.2 | async-start | bytes 2359296 | tf_op jit(solution)/shard_map/all_gather | solution.py:92
  9.1 6.1 %copy-start.9 = (s32[4,12]{1,0:T(4,128)S(1)}, s32[4,12]{1,0:T(4,128)}, u32[]{:S(2)}) copy-start(s32[4,12]{1,0:T(4,128)} %param.20) | copy-start | bytes 580
  9.1 6.4 %copy-start.11 = (f32[2,64]{1,0:T(2,128)S(1)}, f32[2,64]{1,0:T(2,128)}, u32[]{:S(2)}) copy-start(f32[2,64]{1,0:T(2,128)} %param.25) | copy-start | bytes 1540
  12.1 0.6 copy-start.3
  15.1 97.9 %reduce-scatter.3.cloned.1.call-start = ((), (), s32[]{:S(2)}) async-start(), calls=%async_computation.3 | async-start | bytes 2359296 | tf_op jit(solution)/shard_map/reduce_scatter | solution.py:119
  15.5 24.2 %copy-start.7 = (f32[64]{0:T(128)}, f32[64]{0:T(128)S(1)}, u32[]{:S(2)}) copy-start(f32[64]{0:T(128)S(1)} %get-tuple-element.143) | copy-start | bytes 772
  15.5 44.0 %copy-start.5 = (f32[64]{0:T(128)}, f32[64]{0:T(128)S(1)}, u32[]{:S(2)}) copy-start(f32[64]{0:T(128)S(1)} %get-tuple-element.144) | copy-start | bytes 772
  39.6 5.8 %copy-start.12 = (bf16[256,3072]{1,0:T(8,128)(2,1)S(1)}, bf16[256,3072]{1,0:T(8,128)(2,1)}, u32[]{:S(2)}) copy-start(bf16[256,3072]{1,0:T(8,128)(2,1)} %all-gather.3.cloned.1.call-done) | copy-start | bytes 4718596
  40.0 19.8 %collective-permute-start.1 = (bf16[256,12,64]{0,2,1:T(8,128)(2,1)S(1)}, bf16[256,12,64]{0,2,1:T(8,128)(2,1)S(1)}, u32[]{:S(2)}, u32[]{:S(2)}) collective-permute-start(bf16[256,12,64]{0,2,1:T(8,128)(2,1)S(1)} %multiply_convert_fusion.2), channel_id=1, source_target_pairs={{2,0},{4,2},{6,4},{8,6},{10,8},{12,10},{14,12},{16,14},{18,16},{20... | collective-permute-start | bytes 1179656 | tf_op jit(solution)/shard_map/ppermute | solution.py:16
  41.4 18.3 %collective-permute-start = (bf16[256,12,64]{0,2,1:T(8,128)(2,1)S(1)}, bf16[256,12,64]{0,2,1:T(8,128)(2,1)S(1)}, u32[]{:S(2)}, u32[]{:S(2)}) collective-permute-start(bf16[256,12,64]{0,2,1:T(8,128)(2,1)S(1)} %multiply_convert_fusion.2), channel_id=1, source_target_pairs={{0,2},{2,4},{4,6},{6,8},{8,10},{10,12},{12,14},{14,16},{16,18},{18... | collective-permute-start | bytes 1179656 | tf_op jit(solution)/shard_map/ppermute | solution.py:16
  49.3 11.8 %collective-permute-start.3 = (bf16[256,12,64]{0,2,1:T(8,128)(2,1)S(1)}, bf16[256,12,64]{0,2,1:T(8,128)(2,1)S(1)}, u32[]{:S(2)}, u32[]{:S(2)}) collective-permute-start(bf16[256,12,64]{0,2,1:T(8,128)(2,1)S(1)} %bitcast.140), channel_id=1, source_target_pairs={{2,0},{4,2},{6,4},{8,6},{10,8},{12,10},{14,12},{16,14},{18,16},{20... | collective-permute-start | bytes 1179656 | tf_op jit(solution)/shard_map/ppermute | solution.py:16
  50.6 11.3 %collective-permute-start.2 = (bf16[256,12,64]{0,2,1:T(8,128)(2,1)S(1)}, bf16[256,12,64]{0,2,1:T(8,128)(2,1)S(1)}, u32[]{:S(2)}, u32[]{:S(2)}) collective-permute-start(bf16[256,12,64]{0,2,1:T(8,128)(2,1)S(1)} %bitcast.141), channel_id=1, source_target_pairs={{0,2},{2,4},{4,6},{6,8},{8,10},{10,12},{12,14},{14,16},{16,18},{18... | collective-permute-start | bytes 1179656 | tf_op jit(solution)/shard_map/ppermute | solution.py:16
  84.2 0.7 copy-start.14
  84.2 28.8 %copy-start = (bf16[1,128,3072]{2,1,0:T(8,128)(2,1)S(1)}, bf16[1,128,3072]{2,1,0:T(8,128)(2,1)}, u32[]{:S(2)}) copy-start(bf16[1,128,3072]{2,1,0:T(8,128)(2,1)} %param.17) | copy-start | bytes 2359300
  84.2 31.8 %copy-start.10 = (s32[2]{0:T(128)S(1)}, s32[2]{0:T(128)}, u32[]{:S(2)}) copy-start(s32[2]{0:T(128)} %param.21) | copy-start | bytes 28
  84.2 55.8 %copy-start.1 = (bf16[2,128,3072]{2,1,0:T(8,128)(2,1)S(1)}, bf16[2,128,3072]{2,1,0:T(8,128)(2,1)}, u32[]{:S(2)}) copy-start(bf16[2,128,3072]{2,1,0:T(8,128)(2,1)} %param.18) | copy-start | bytes 4718596
  84.2 70.6 %all-gather.5.cloned.1.call-start = ((), (), s32[]{:S(2)}) async-start(), calls=%async_computation.4 | async-start | bytes 2359296 | tf_op jit(solution)/shard_map/all_gather | solution.py:92
  114.9 26.6 %copy-start.4 = (f32[1,3072]{1,0:T(1,128)S(1)}, f32[1,3072]{1,0:T(1,128)}, u32[]{:S(2)}) copy-start(f32[1,3072]{1,0:T(1,128)} %copy-done.3) | copy-start | bytes 36868
  115.0 25.0 %collective-permute-start.4 = (bf16[128,3072]{1,0:T(8,128)(2,1)S(1)}, bf16[128,3072]{1,0:T(8,128)(2,1)}, u32[]{:S(2)}, u32[]{:S(2)}) collective-permute-start(bf16[128,3072]{1,0:T(8,128)(2,1)S(1)} %fusion.37), channel_id=1, source_target_pairs={{254,0},{0,2},{2,4},{4,6},{6,8},{8,10},{10,12},{12,14},{14,16},{16... | collective-permute-start | bytes 2359304 | tf_op jit(solution)/shard_map/ppermute | solution.py:22
  142.7 17.0 %copy-start.8 = (f32[64]{0:T(128)S(1)}, f32[64]{0:T(128)}, u32[]{:S(2)}) copy-start(f32[64]{0:T(128)} %copy-done.7) | copy-start | bytes 772
  142.7 101.8 %reduce-scatter.5.cloned.1.call-start = ((), (), s32[]{:S(2)}) async-start(), calls=%async_computation.5 | async-start | bytes 2359296 | tf_op jit(solution)/shard_map/reduce_scatter | solution.py:119
  159.6 6.5 %copy-start.13 = (bf16[256,3072]{1,0:T(8,128)(2,1)S(1)}, bf16[256,3072]{1,0:T(8,128)(2,1)}, u32[]{:S(2)}) copy-start(bf16[256,3072]{1,0:T(8,128)(2,1)} %all-gather.5.cloned.1.call-done) | copy-start | bytes 4718596
  159.9 20.5 %collective-permute-start.6 = (bf16[256,12,64]{0,2,1:T(8,128)(2,1)S(1)}, bf16[256,12,64]{0,2,1:T(8,128)(2,1)S(1)}, u32[]{:S(2)}, u32[]{:S(2)}) collective-permute-start(bf16[256,12,64]{0,2,1:T(8,128)(2,1)S(1)} %multiply_convert_fusion), channel_id=1, source_target_pairs={{2,0},{4,2},{6,4},{8,6},{10,8},{12,10},{14,12},{16,14},{18,16},{20... | collective-permute-start | bytes 1179656 | tf_op jit(solution)/shard_map/ppermute | solution.py:16
  161.4 19.1 %collective-permute-start.5 = (bf16[256,12,64]{0,2,1:T(8,128)(2,1)S(1)}, bf16[256,12,64]{0,2,1:T(8,128)(2,1)}, u32[]{:S(2)}, u32[]{:S(2)}) collective-permute-start(bf16[256,12,64]{0,2,1:T(8,128)(2,1)S(1)} %multiply_convert_fusion), channel_id=1, source_target_pairs={{0,2},{2,4},{4,6},{6,8},{8,10},{10,12},{12,14},{14,16},{16,18},{18... | collective-permute-start | bytes 1179656 | tf_op jit(solution)/shard_map/ppermute | solution.py:16
  170.0 10.2 %copy-start.6 = (f32[64]{0:T(128)S(1)}, f32[64]{0:T(128)}, u32[]{:S(2)}) copy-start(f32[64]{0:T(128)} %copy-done.5) | copy-start | bytes 772
  170.0 11.8 %collective-permute-start.8 = (bf16[256,12,64]{0,2,1:T(8,128)(2,1)S(1)}, bf16[256,12,64]{0,2,1:T(8,128)(2,1)S(1)}, u32[]{:S(2)}, u32[]{:S(2)}) collective-permute-start(bf16[256,12,64]{0,2,1:T(8,128)(2,1)S(1)} %bitcast.143), channel_id=1, source_target_pairs={{2,0},{4,2},{6,4},{8,6},{10,8},{12,10},{14,12},{16,14},{18,16},{20... | collective-permute-start | bytes 1179656 | tf_op jit(solution)/shard_map/ppermute | solution.py:16
  171.3 11.3 %collective-permute-start.7 = (bf16[256,12,64]{0,2,1:T(8,128)(2,1)S(1)}, bf16[256,12,64]{0,2,1:T(8,128)(2,1)S(1)}, u32[]{:S(2)}, u32[]{:S(2)}) collective-permute-start(bf16[256,12,64]{0,2,1:T(8,128)(2,1)S(1)} %bitcast.144), channel_id=1, source_target_pairs={{0,2},{2,4},{4,6},{6,8},{8,10},{10,12},{12,14},{14,16},{16,18},{18... | collective-permute-start | bytes 1179656 | tf_op jit(solution)/shard_map/ppermute | solution.py:16
  216.5 55.0 %copy-start.2 = (bf16[2,128,3072]{2,1,0:T(8,128)(2,1)S(1)}, bf16[2,128,3072]{2,1,0:T(8,128)(2,1)}, u32[]{:S(2)}) copy-start(bf16[2,128,3072]{2,1,0:T(8,128)(2,1)} %param.18) | copy-start | bytes 4718596
  246.5 25.0 %collective-permute-start.9 = (bf16[128,3072]{1,0:T(8,128)(2,1)S(1)}, bf16[128,3072]{1,0:T(8,128)(2,1)S(1)}, u32[]{:S(2)}, u32[]{:S(2)}) collective-permute-start(bf16[128,3072]{1,0:T(8,128)(2,1)S(1)} %fusion.32), channel_id=1, source_target_pairs={{254,0},{0,2},{2,4},{4,6},{6,8},{8,10},{10,12},{12,14},{14,16},{16... | collective-permute-start | bytes 2359304 | tf_op jit(solution)/shard_map/ppermute | solution.py:22
Sparse Core Ops, SparseCore 0:
  15.2 19.6 all-gather.2
  84.3 28.5 reduce-scatter.2
  142.8 11.9 all-gather.4
  216.6 27.8 reduce-scatter.4
where the time goes:
time: 280 us; the launch traced here: 279 us
  waiting for transfers between devices  136 us (49%)
  matrix products  65.2 us (23%)
  starting transfers between devices  24.6 us (9%)
  other arithmetic  22.6 us (8%)
  between operations  16.9 us (6%)
  local copies, waits for them, and re-layouts  13.2 us (5%)
    reduce_scatter x2, waiting for transfers between devices, on_device(): lax.psum_scatter(jnp.dot(attended, wo, preferred_element_type=jnp.float32...  55.6 us
    ppermute x2, waiting for transfers between devices, shifted_2(): return lax.ppermute(block, axis, route)  46 us
    all_gather x2, waiting for transfers between devices, on_device(): whole = lax.all_gather(modulated, 'seq', axis=0, tiled=True)  31.2 us
    ppermute x8, starting transfers between devices, shifted(): return lax.ppermute(shard, axis, pairs)  22.2 us
    dot_general x24, matrix products, one_head(): jnp.dot(weights, value_head, preferred_element_type=jnp.float32)  19.4 us
    dot_general x2, matrix products, on_device(): jnp.dot(attended, wo, preferred_element_type=jnp.float32)  9.88 us
    dot_general x2, matrix products, on_device(): jnp.dot(whole, wq, preferred_element_type=jnp.float32)  9.52 us
    dot_general x2, matrix products, on_device(): jnp.dot(whole, wk, preferred_element_type=jnp.float32)  9.51 us
  transfers between devices with their start and end apart: 14, of which 10 were waited for; matrix products, arithmetic and copies ran while one was open for 7% of the time, Pallas kernels for 0%

commit v1 on v0

v1 whole, which is shorter than its diff:
```python
import math

import jax
import jax.numpy as jnp
from jax import lax
from jax.sharding import PartitionSpec as P

HD = 64
FRAMES = 4
ITERS = 2


def swap_cores(block):
    return lax.ppermute(block, "seq", [(0, 1), (1, 0)])


def modulate(slot_state, scale_row, shift_row):
    values = slot_state.astype(jnp.float32)
    normed = values * lax.rsqrt(jnp.mean(values * values, axis=-1, keepdims=True) + 1e-06)
    return (normed * (1.0 + scale_row) + shift_row).astype(jnp.bfloat16)


def head_norm(values, gain):
    return (
        values * lax.rsqrt(jnp.mean(values * values, axis=-1, keepdims=True) + 1e-06) * gain
    ).astype(jnp.bfloat16)


def frame_table(pattern, slot, count, core):
    block = jnp.arange(3 * FRAMES, dtype=jnp.int32) // FRAMES
    present = (block == 1) | (block == 0) & (slot > 0) | (block == 2) & (slot < count - 1)
    own = (
        jnp.arange(3 * FRAMES, dtype=jnp.int32)[None, :]
        == (FRAMES + jnp.arange(FRAMES, dtype=jnp.int32))[:, None]
    )
    table = ((pattern == 1) | own) & present[None, :]
    half = FRAMES // 2
    turned = table.reshape(2, half, 3, 2, half)[::-1, :, :, ::-1].reshape(FRAMES, 3 * FRAMES)
    return jnp.where(core == 0, table, turned)


def attend(query, keys, values, allowed):
    scale = 1.0 / math.sqrt(HD)

    def one_head(operands):
        query_head, key_head, value_head = operands
        scores = jnp.dot(query_head, key_head.T, preferred_element_type=jnp.float32) * scale
        scores = jnp.where(allowed, scores, -1e30)
        highest = jnp.max(scores, axis=-1, keepdims=True)
        expo = jnp.exp(scores - highest)
        weights = (expo / jnp.sum(expo, axis=-1, keepdims=True)).astype(jnp.bfloat16)
        return jnp.dot(weights, value_head, preferred_element_type=jnp.float32).astype(jnp.bfloat16)

    heads = lax.map(
        one_head, (query.transpose(1, 0, 2), keys.transpose(1, 0, 2), values.transpose(1, 0, 2))
    )
    return heads.transpose(1, 0, 2)


def on_device(
    latents, fresh_noise, levels, pattern, entry, level_scale, level_shift, step_size, qk_gain, wq, wk, wv, wo
):
    count = lax.axis_size("queue")
    place = lax.axis_index("queue")
    core = lax.axis_index("seq")
    state = latents[0]
    half, _ = state.shape
    tokens, width = 2 * half, wq.shape[1]
    heads = width // HD
    forward = [(i, (i + 1) % count) for i in range(count)]
    backward = [((i + 1) % count, i) for i in range(count)]
    for step in range(ITERS):
        slot = (place + step) % count
        level = levels[slot]
        modulated = modulate(state, level_scale[level], level_shift[level])
        whole = jnp.concatenate([modulated, swap_cores(modulated)], axis=0)
        keys = head_norm(
            jnp.dot(whole, wk, preferred_element_type=jnp.float32).reshape(tokens, heads, HD), qk_gain[1]
        )
        values = (
            jnp.dot(whole, wv, preferred_element_type=jnp.float32)
            .astype(jnp.bfloat16)
            .reshape(tokens, heads, HD)
        )
        pair = jnp.stack([keys.reshape(tokens, width), values.reshape(tokens, width)])
        before = lax.ppermute(pair, "queue", forward)
        after = lax.ppermute(pair, "queue", backward)
        query = head_norm(
            jnp.dot(whole, wq, preferred_element_type=jnp.float32).reshape(tokens, heads, HD), qk_gain[0]
        )
        window = jnp.concatenate([before, pair, after], axis=1).reshape(2, 3 * tokens, heads, HD)
        table = frame_table(pattern, slot, count, core)
        per_frame = tokens // FRAMES
        allowed = jnp.repeat(jnp.repeat(table, per_frame, axis=0), per_frame, axis=1)
        attended = attend(query, window[0], window[1], allowed).reshape(tokens, width)
        term = jnp.dot(attended, wo, preferred_element_type=jnp.float32).astype(jnp.bfloat16)
        other = swap_cores(term[half:])
        velocity = term[:half].astype(jnp.float32) + other.astype(jnp.float32)
        updated = (state.astype(jnp.float32) + step_size[level] * velocity).astype(jnp.bfloat16)
        state = jnp.where((slot + 1) % count == entry[step], fresh_noise[step], updated)
    route = [(i, (i + ITERS) % count) for i in range(count)]
    return lax.ppermute(state, "queue", route)[None]


def solution(mesh):
    return jax.shard_map(
        on_device,
        mesh=mesh,
        in_specs=(
            P("queue", "seq", None),
            P(None, "seq", None),
            P(),
            P(),
            P(),
            P(),
            P(),
            P(),
            P(),
            P(None, "seq"),
            P(None, "seq"),
            P(None, "seq"),
            P("seq", None),
        ),
        out_specs=P("queue", "seq", None),
        check_vma=False,
    )
```

time: 280 us -> 203 us (0.72)
  waiting for transfers between devices: 136 us -> 68.3 us
  between operations: 16.9 us -> 5.66 us
  local copies, waits for them, and re-layouts: 13.2 us -> 21.1 us
  starting transfers between devices: 24.6 us -> 17.3 us
  matrix products: 65.2 us -> 69.4 us
    reduce_scatter x2 -> x0, waiting for transfers between devices: 55.6 us -> none  [on_device(): lax.psum_scatter(jnp.dot(attended, wo, preferred_element_type=jnp.float32...]
    all_gather x2 -> x0, waiting for transfers between devices: 31.2 us -> none  [on_device(): whole = lax.all_gather(modulated, 'seq', axis=0, tiled=True)]
    dot_general x24, matrix products: 9.41 us -> 30.8 us  [one_head(): jnp.dot(query_head, key_head.T, preferred_element_type=jnp.float32) * scale]
    ppermute x10 -> x9, waiting for transfers between devices: 49.3 us -> 68.3 us  [the longest x2 28.1 us: on_device(): after = lax.ppermute(pair, 'queue', backward)]
    dot_general x24, matrix products: 19.4 us -> 8.85 us  [one_head(): jnp.dot(weights, value_head, preferred_element_type=jnp.float32)]
    ppermute x10 -> x9, starting transfers between devices: 24.3 us -> 17.3 us  [the longest x2 8.64 us: on_device(): after = lax.ppermute(pair, 'queue', backward)]
    slice x1 -> x9, local copies, waits for them, and re-layouts: 0.59 us -> 5.22 us  [the longest x2 2.93 us: on_device(): window[0]]
    dot_general x2, matrix products: 9.52 us -> 5.11 us  [on_device(): jnp.dot(whole, wq, preferred_element_type=jnp.float32)]
  transfers between devices with their start and end apart: 14 -> 9, of which waited for: 10 -> 9; matrix products, arithmetic and copies ran while one was open for 7% -> 5% of each run, Pallas kernels for 0% -> 0%
where the time goes in v1:
time: 203 us; the launch traced here: 202 us
  matrix products  69.4 us (34%)
  waiting for transfers between devices  68.3 us (34%)
  local copies, waits for them, and re-layouts  21.1 us (10%)
  other arithmetic  19.9 us (10%)
  starting transfers between devices  17.3 us (9%)
  between operations  5.66 us (3%)
    dot_general x24, matrix products, one_head(): jnp.dot(query_head, key_head.T, preferred_element_type=jnp.float32) * scale  30.8 us
    ppermute x2, waiting for transfers between devices, on_device(): after = lax.ppermute(pair, 'queue', backward)  28.1 us
    ppermute x1, waiting for transfers between devices, on_device(): return lax.ppermute(state, 'queue', route)[None]  24.5 us
    ppermute x2, waiting for transfers between devices, on_device(): before = lax.ppermute(pair, 'queue', forward)  12.6 us
    dot_general x24, matrix products, one_head(): jnp.dot(weights, value_head, preferred_element_type=jnp.float32)  8.85 us
    dot_general x2, matrix products, on_device(): jnp.dot(whole, wk, preferred_element_type=jnp.float32)  8.84 us
    ppermute x2, starting transfers between devices, on_device(): after = lax.ppermute(pair, 'queue', backward)  8.64 us
    dot_general x2, matrix products, on_device(): jnp.dot(whole, wv, preferred_element_type=jnp.float32).astype(jnp.bfloat16)  8.14 us
  transfers between devices with their start and end apart: 9, of which 9 were waited for; matrix products, arithmetic and copies ran while one was open for 5% of the time, Pallas kernels for 0%

profile of v1, /device:TPU:1, one launch (start us, length us, event | category | flops | bytes accessed | tf_op | source)
XLA Modules:
  0.0 202.1 jit_solution(9307569768797771015)
XLA Ops:
  0.0 1.3 fusion.65
  3.9 1.4 fusion.33
  6.6 1.7 dynamic-slice_add_fusion
  8.3 1.4 fusion.36
  9.7 3.3 %collective-permute-start = (bf16[128,3072]{1,0:T(8,128)(2,1)S(1)}, bf16[128,3072]{1,0:T(8,128)(2,1)S(1)}, u32[]{:S(2)}, u32[]{:S(2)}) collective-permute-start(bf16[128,3072]{1,0:T(8,128)(2,1)S(1)} %fusion.36), channel_id=1, source_target_pairs={{0,1},{1,0},{2,3},{3,2},{4,5},{5,4},{6,7},{7,6},{8,9},{9,8},{10,11... | collective-permute-start | bytes 2359304 | tf_op jit(solution)/shard_map/ppermute | solution.py:14
  14.9 4.0 %fusion.66 = (f32[256,768]{1,0:T(8,128)S(1)}, f32[256,768]{1,0:T(8,128)S(1)}) fusion(bf16[3072,768]{1,0:T(8,128)(2,1)} %param.27, bf16[128,3072]{1,0:T(8,128)(2,1)S(1)} %collective-permute-done, bf16[128,3072]{1,0:T(8,128)(2,1)S(1)} %fusion.36), kind=kOutput, calls=%fused_computation.116 | convolution fusion | flops 1211301888 | bytes 7864320 | tf_op jit(solution)/shard_map/dot_general | solution.py:78
  20.8 4.1 %fusion.38 = bf16[1,256,768]{2,1,0:T(8,128)(2,1)S(1)} fusion(bf16[3072,768]{1,0:T(8,128)(2,1)} %param.28, bf16[128,3072]{1,0:T(8,128)(2,1)S(1)} %copy-done.12, bf16[128,3072]{1,0:T(8,128)(2,1)S(1)} %fusion.36), kind=kOutput, calls=%fused_computation.58 | convolution fusion | flops 1211301888 | bytes 6684672 | tf_op jit(solution)/shard_map/dot_general | solution.py:81
  25.0 8.6 %collective-permute-start.2 = (bf16[2,256,768]{2,1,0:T(8,128)(2,1)S(1)}, bf16[2,256,768]{2,1,0:T(8,128)(2,1)S(1)}, u32[]{:S(2)}, u32[]{:S(2)}) collective-permute-start(bf16[2,256,768]{2,1,0:T(8,128)(2,1)S(1)} %pad_maximum_fusion.4), channel_id=1, source_target_pairs={{2,0},{4,2},{6,4},{8,6},{10,8},{12,10},{14,12},{16,14},{18,16},{20... | collective-permute-start | bytes 2359304 | tf_op jit(solution)/shard_map/ppermute | solution.py:87
  33.6 1.9 fusion.45
  35.8 14.3 %collective-permute-done.2 = bf16[2,256,768]{2,1,0:T(8,128)(2,1)S(1)} collective-permute-done((bf16[2,256,768]{2,1,0:T(8,128)(2,1)S(1)}, bf16[2,256,768]{2,1,0:T(8,128)(2,1)S(1)}, u32[]{:S(2)}, u32[]{:S(2)}) %collective-permute-start.2) | collective-permute-done | bytes 786464 | tf_op jit(solution)/shard_map/ppermute | solution.py:87
  50.1 7.3 %collective-permute-done.1 = bf16[2,256,768]{2,1,0:T(8,128)(2,1)S(1)} collective-permute-done((bf16[2,256,768]{2,1,0:T(8,128)(2,1)S(1)}, bf16[2,256,768]{2,1,0:T(8,128)(2,1)S(1)}, u32[]{:S(2)}, u32[]{:S(2)}) %collective-permute-start.1) | collective-permute-done | bytes 786464 | tf_op jit(solution)/shard_map/ppermute | solution.py:86
  57.7 1.5 copy.27
  59.9 27.8 %while.22 = (s32[]{:T(128)}, bf16[12,256,64]{1,2,0:T(8,128)(2,1)S(1)}, bf16[12,256,64]{1,2,0:T(8,128)(2,1)S(1)}, bf16[12,768,64]{1,2,0:T(8,128)(2,1)}, bf16[12,7...) while((s32[]{:T(128)}, bf16[12,256,64]{1,2,0:T(8,128)(2,1)S(1)}, ...), condition=%wide.region_6.7_spmd.clone, body=%wide.region_3.6_spmd.clone.sunk | while | flops 51920384 | bytes 3418197 | solution.py:54
  87.7 3.8 %convolution_convert_fusion.3 = bf16[256,3072]{1,0:T(8,128)(2,1)S(1)} fusion(bf16[256,768]{0,1:T(8,128)(2,1)S(1)} %bitcast.149, bf16[768,3072]{1,0:T(8,128)(2,1)} %param.29), kind=kOutput, calls=%fused_computation.35 | convolution fusion | flops 1208745984 | bytes 6684672 | tf_op jit(solution)/shard_map/dot_general | solution.py:96
  91.6 1.8 collective-permute-start.3
  95.4 2.6 %fusion.28 = (f32[128]{0:T(128)S(1)}, bf16[128,3072]{1,0:T(8,128)(2,1)S(1)}) fusion(bf16[128,3072]{1,0:T(8,128)(2,1)} %collective-permute-done.3, bf16[256,3072]{1,0:T(8,128)(2,1)S(1)} %convolution_convert_fusion.3, f32[]{:T(128)} %bitcast.6, bf16[1,128,3072]{2,1,0:T(8,128)(2,1)S(1)} %copy-done, bf16[2,128,3072]{2,1,0:T(8,128)(2,1)} %param.18, pred[]{:T(512)S(6)} %eq.79), kind=kLoop, calls=%fused_computation.44 | loop fusion | flops 4325248 | bytes 3932677 | tf_op jit(solution)/shard_map/reduce_sum | solution.py:19
  99.4 1.5 collective-permute-done.4
  100.9 4.8 %fusion.67 = (f32[256,768]{1,0:T(8,128)S(1)}, f32[256,768]{1,0:T(8,128)}) fusion(bf16[3072,768]{1,0:T(8,128)(2,1)} %param.27, bf16[128,3072]{1,0:T(8,128)(2,1)} %collective-permute-done.4, bf16[128,3072]{1,0:T(8,128)(2,1)S(1)} %fusion.31), kind=kOutput, calls=%fused_computation.117 | convolution fusion | flops 1211301888 | bytes 7864320 | tf_op jit(solution)/shard_map/dot_general | solution.py:78
  106.7 1.4 fusion.49
  108.1 4.1 %fusion.39 = bf16[1,256,768]{2,1,0:T(8,128)(2,1)S(1)} fusion(bf16[3072,768]{1,0:T(8,128)(2,1)} %param.28, bf16[128,3072]{1,0:T(8,128)(2,1)} %collective-permute-done.4, bf16[128,3072]{1,0:T(8,128)(2,1)S(1)} %fusion.31), kind=kOutput, calls=%fused_computation.59 | convolution fusion | flops 1211301888 | bytes 6684672 | tf_op jit(solution)/shard_map/dot_general | solution.py:81
  112.4 1.5 collective-permute-start.5
  113.8 3.2 %fusion.43 = f32[256,768]{0,1:T(8,128)S(1)} fusion(bf16[3072,768]{1,0:T(8,128)(2,1)S(1)} %bitcast.162, bf16[128,3072]{1,0:T(8,128)(2,1)} %collective-permute-done.4, bf16[128,3072]{1,0:T(8,128)(2,1)S(1)} %fusion.31), kind=kOutput, calls=%fused_computation.71 | convolution fusion | flops 1211105280 | bytes 7077888 | tf_op jit(solution)/shard_map/dot_general | solution.py:89
  117.3 13.8 %collective-permute-done.6 = bf16[2,256,768]{2,1,0:T(8,128)(2,1)S(1)} collective-permute-done((bf16[2,256,768]{2,1,0:T(8,128)(2,1)S(1)}, bf16[2,256,768]{2,1,0:T(8,128)(2,1)S(1)}, u32[]{:S(2)}, u32[]{:S(2)}) %collective-permute-start.6) | collective-permute-done | bytes 786464 | tf_op jit(solution)/shard_map/ppermute | solution.py:87
  131.1 5.3 %collective-permute-done.5 = bf16[2,256,768]{2,1,0:T(8,128)(2,1)S(1)} collective-permute-done((bf16[2,256,768]{2,1,0:T(8,128)(2,1)S(1)}, bf16[2,256,768]{2,1,0:T(8,128)(2,1)S(1)}, u32[]{:S(2)}, u32[]{:S(2)}) %collective-permute-start.5) | collective-permute-done | bytes 786464 | tf_op jit(solution)/shard_map/ppermute | solution.py:86
  136.7 1.5 copy.36
  138.9 27.9 %while.23 = (s32[]{:T(128)}, bf16[12,256,64]{1,2,0:T(8,128)(2,1)S(1)}, bf16[12,256,64]{1,2,0:T(8,128)(2,1)S(1)}, bf16[12,768,64]{1,2,0:T(8,128)(2,1)}, bf16[12,7...) while((s32[]{:T(128)}, bf16[12,256,64]{1,2,0:T(8,128)(2,1)S(1)}, ...), condition=%wide.region_13.14_spmd.clone, body=%wide.region_10.13_spmd.clone.sunk | while | flops 51920384 | bytes 3418197 | solution.py:54
  141.5 1.3 fusion.91
  166.7 3.8 %convolution_convert_fusion.2 = bf16[256,3072]{1,0:T(8,128)(2,1)S(1)} fusion(bf16[256,768]{0,1:T(8,128)(2,1)S(1)} %bitcast.148, bf16[768,3072]{1,0:T(8,128)(2,1)} %param.29), kind=kOutput, calls=%fused_computation.34 | convolution fusion | flops 1208745984 | bytes 6684672 | tf_op jit(solution)/shard_map/dot_general | solution.py:96
  170.6 1.5 collective-permute-start.7
  172.7 1.4 collective-permute-done.7
  174.1 2.5 %fusion.41 = bf16[128,3072]{1,0:T(8,128)(2,1)S(1)} fusion(bf16[128,3072]{1,0:T(8,128)(2,1)} %collective-permute-done.7, bf16[128,3072]{1,0:T(8,128)(2,1)S(1)} %get-tuple-element.140, bf16[256,3072]{1,0:T(8,128)(2,1)S(1)} %convolution_convert_fusion.2, f32[]{:T(128)} %bitcast.25, bf16[2,128,3072]{2,1,0:T(8,128)(2,1)} %param.18, pred[]{:T(512)S(6)} %eq.78), kind=kLoop, calls=%fused_computation.61 | loop fusion | flops 3145728 | bytes 3932165 | tf_op jit(solution)/shard_map/jit(_where)/select_n | solution.py:100
  176.7 24.5 %collective-permute-done.8 = bf16[128,3072]{1,0:T(8,128)(2,1)S(1)} collective-permute-done((bf16[128,3072]{1,0:T(8,128)(2,1)S(1)}, bf16[128,3072]{1,0:T(8,128)(2,1)S(1)}, u32[]{:S(2)}, u32[]{:S(2)}) %collective-permute-start.8) | collective-permute-done | bytes 786464 | tf_op jit(solution)/shard_map/ppermute | solution.py:102
  (217 shorter events, 65.1 us)
Async XLA Ops:
  0.0 13.0 %copy-start.10 = (f32[2,64]{1,0:T(2,128)S(1)}, f32[2,64]{1,0:T(2,128)}, u32[]{:S(2)}) copy-start(f32[2,64]{1,0:T(2,128)} %param.25) | copy-start | bytes 1540
  0.0 13.7 %copy-start.8 = (s32[4,12]{1,0:T(4,128)S(1)}, s32[4,12]{1,0:T(4,128)}, u32[]{:S(2)}) copy-start(s32[4,12]{1,0:T(4,128)} %param.20) | copy-start | bytes 580
  9.7 5.2 %collective-permute-start = (bf16[128,3072]{1,0:T(8,128)(2,1)S(1)}, bf16[128,3072]{1,0:T(8,128)(2,1)S(1)}, u32[]{:S(2)}, u32[]{:S(2)}) collective-permute-start(bf16[128,3072]{1,0:T(8,128)(2,1)S(1)} %fusion.36), channel_id=1, source_target_pairs={{0,1},{1,0},{2,3},{3,2},{4,5},{5,4},{6,7},{7,6},{8,9},{9,8},{10,11... | collective-permute-start | bytes 2359304 | tf_op jit(solution)/shard_map/ppermute | solution.py:14
  13.7 6.0 %copy-start.2 = (f32[768]{0:T(1024)}, f32[768]{0:T(1024)S(1)}, u32[]{:S(2)}) copy-start(f32[768]{0:T(1024)S(1)} %mul.178) | copy-start | bytes 9220
  14.9 4.0 %copy-start.11 = (bf16[128,3072]{1,0:T(8,128)(2,1)}, bf16[128,3072]{1,0:T(8,128)(2,1)S(1)}, u32[]{:S(2)}) copy-start(bf16[128,3072]{1,0:T(8,128)(2,1)S(1)} %collective-permute-done) | copy-start | bytes 2359300
  19.7 1.1 copy-start.12
  19.7 13.8 %slice-start = ((s8[4718592]{0:T(1024)(128)(4,1)}), s8[4194304]{0:T(1024)(128)(4,1)S(1)}, s32[]{:S(2)}) async-start(s8[4718592]{0:T(1024)(128)(4,1)} %bitcast.159), calls=%async_computation | async-start | bytes 8388608
  20.8 12.7 %slice-start.1 = ((s8[4718592]{0:T(1024)(128)(4,1)}), s8[524288]{0:T(1024)(128)(4,1)S(1)}, s32[]{:S(2)}) async-start(s8[4718592]{0:T(1024)(128)(4,1)} %bitcast.159), calls=%async_computation.1 | async-start | bytes 1048576
  25.0 10.6 %copy-start.4 = (f32[64]{0:T(128)S(1)}, f32[64]{0:T(128)}, u32[]{:S(2)}) copy-start(f32[64]{0:T(128)} %get-tuple-element.154) | copy-start | bytes 772
  25.0 25.1 %collective-permute-start.2 = (bf16[2,256,768]{2,1,0:T(8,128)(2,1)S(1)}, bf16[2,256,768]{2,1,0:T(8,128)(2,1)S(1)}, u32[]{:S(2)}, u32[]{:S(2)}) collective-permute-start(bf16[2,256,768]{2,1,0:T(8,128)(2,1)S(1)} %pad_maximum_fusion.4), channel_id=1, source_target_pairs={{2,0},{4,2},{6,4},{8,6},{10,8},{12,10},{14,12},{16,14},{18,16},{20... | collective-permute-start | bytes 2359304 | tf_op jit(solution)/shard_map/ppermute | solution.py:87
  33.5 23.9 %collective-permute-start.1 = (bf16[2,256,768]{2,1,0:T(8,128)(2,1)S(1)}, bf16[2,256,768]{2,1,0:T(8,128)(2,1)S(1)}, u32[]{:S(2)}, u32[]{:S(2)}) collective-permute-start(bf16[2,256,768]{2,1,0:T(8,128)(2,1)S(1)} %pad_maximum_fusion.4), channel_id=1, source_target_pairs={{0,2},{2,4},{4,6},{6,8},{8,10},{10,12},{12,14},{14,16},{16,18},{18... | collective-permute-start | bytes 2359304 | tf_op jit(solution)/shard_map/ppermute | solution.py:86
  91.5 1.9 copy-start.9
  91.5 3.1 %copy-start.7 = (f32[50]{0:T(128)S(1)}, f32[50]{0:T(128)}, u32[]{:S(2)}) copy-start(f32[50]{0:T(128)} %param.24) | copy-start | bytes 604
  91.5 3.9 %copy-start = (bf16[1,128,3072]{2,1,0:T(8,128)(2,1)S(1)}, bf16[1,128,3072]{2,1,0:T(8,128)(2,1)}, u32[]{:S(2)}) copy-start(bf16[1,128,3072]{2,1,0:T(8,128)(2,1)} %param.17) | copy-start | bytes 2359300
  91.6 3.8 %collective-permute-start.3 = (bf16[128,3072]{1,0:T(8,128)(2,1)S(1)}, bf16[128,3072]{1,0:T(8,128)(2,1)}, u32[]{:S(2)}, u32[]{:S(2)}) collective-permute-start(bf16[128,3072]{1,0:T(8,128)(2,1)S(1)} %slice.65), channel_id=1, source_target_pairs={{0,1},{1,0},{2,3},{3,2},{4,5},{5,4},{6,7},{7,6},{8,9},{9,8},{10,11... | collective-permute-start | bytes 2359304 | tf_op jit(solution)/shard_map/ppermute | solution.py:14
  95.4 2.7 %copy-start.1 = (f32[1,3072]{1,0:T(1,128)S(1)}, f32[1,3072]{1,0:T(1,128)}, u32[]{:S(2)}) copy-start(f32[1,3072]{1,0:T(1,128)} %get-tuple-element.168) | copy-start | bytes 36868
  98.1 0.8 copy-start.6
  98.4 2.5 %collective-permute-start.4 = (bf16[128,3072]{1,0:T(8,128)(2,1)S(1)}, bf16[128,3072]{1,0:T(8,128)(2,1)}, u32[]{:S(2)}, u32[]{:S(2)}) collective-permute-start(bf16[128,3072]{1,0:T(8,128)(2,1)S(1)} %fusion.31), channel_id=1, source_target_pairs={{0,1},{1,0},{2,3},{3,2},{4,5},{5,4},{6,7},{7,6},{8,9},{9,8},{10,11... | collective-permute-start | bytes 2359304 | tf_op jit(solution)/shard_map/ppermute | solution.py:14
  106.0 0.7 copy-start.3
  106.7 7.1 %slice-start.2 = ((s8[4718592]{0:T(1024)(128)(4,1)}), s8[4194304]{0:T(1024)(128)(4,1)S(1)}, s32[]{:S(2)}) async-start(s8[4718592]{0:T(1024)(128)(4,1)} %bitcast.161), calls=%async_computation.2 | async-start | bytes 8388608
  108.1 5.7 %slice-start.3 = ((s8[4718592]{0:T(1024)(128)(4,1)}), s8[524288]{0:T(1024)(128)(4,1)S(1)}, s32[]{:S(2)}) async-start(s8[4718592]{0:T(1024)(128)(4,1)} %bitcast.161), calls=%async_computation.3 | async-start | bytes 1048576
  112.3 4.8 %copy-start.5 = (f32[64]{0:T(128)S(1)}, f32[64]{0:T(128)}, u32[]{:S(2)}) copy-start(f32[64]{0:T(128)} %get-tuple-element.154) | copy-start | bytes 772
  112.3 18.8 %collective-permute-start.6 = (bf16[2,256,768]{2,1,0:T(8,128)(2,1)S(1)}, bf16[2,256,768]{2,1,0:T(8,128)(2,1)S(1)}, u32[]{:S(2)}, u32[]{:S(2)}) collective-permute-start(bf16[2,256,768]{2,1,0:T(8,128)(2,1)S(1)} %pad_maximum_fusion.5), channel_id=1, source_target_pairs={{2,0},{4,2},{6,4},{8,6},{10,8},{12,10},{14,12},{16,14},{18,16},{20... | collective-permute-start | bytes 2359304 | tf_op jit(solution)/shard_map/ppermute | solution.py:87
  112.4 24.0 %collective-permute-start.5 = (bf16[2,256,768]{2,1,0:T(8,128)(2,1)S(1)}, bf16[2,256,768]{2,1,0:T(8,128)(2,1)S(1)}, u32[]{:S(2)}, u32[]{:S(2)}) collective-permute-start(bf16[2,256,768]{2,1,0:T(8,128)(2,1)S(1)} %pad_maximum_fusion.5), channel_id=1, source_target_pairs={{0,2},{2,4},{4,6},{6,8},{8,10},{10,12},{12,14},{14,16},{16,18},{18... | collective-permute-start | bytes 2359304 | tf_op jit(solution)/shard_map/ppermute | solution.py:86
  170.6 3.6 %collective-permute-start.7 = (bf16[128,3072]{1,0:T(8,128)(2,1)S(1)}, bf16[128,3072]{1,0:T(8,128)(2,1)}, u32[]{:S(2)}, u32[]{:S(2)}) collective-permute-start(bf16[128,3072]{1,0:T(8,128)(2,1)S(1)} %slice.69), channel_id=1, source_target_pairs={{0,1},{1,0},{2,3},{3,2},{4,5},{5,4},{6,7},{7,6},{8,9},{9,8},{10,11... | collective-permute-start | bytes 2359304 | tf_op jit(solution)/shard_map/ppermute | solution.py:14
  176.6 24.6 %collective-permute-start.8 = (bf16[128,3072]{1,0:T(8,128)(2,1)S(1)}, bf16[128,3072]{1,0:T(8,128)(2,1)S(1)}, u32[]{:S(2)}, u32[]{:S(2)}) collective-permute-start(bf16[128,3072]{1,0:T(8,128)(2,1)S(1)} %fusion.41), channel_id=1, source_target_pairs={{0,4},{2,6},{4,8},{6,10},{8,12},{10,14},{12,16},{14,18},{16,20},{1... | collective-permute-start | bytes 2359304 | tf_op jit(solution)/shard_map/ppermute | solution.py:102

commit v2 on v1

v2 whole, which is shorter than its diff:
```python
import math

import jax
import jax.numpy as jnp
from jax import lax
from jax.experimental import pallas as pl
from jax.experimental.pallas import tpu as pltpu
from jax.sharding import PartitionSpec as P

HD = 64
FRAMES = 4
ITERS = 2
LANES = 128
EPS = 1e-06
CLOSED = -30000.0
BLOCK = 256
OUT_BLOCK = 768
MIB = 1 << 20
F32 = jnp.float32
BF16 = jnp.bfloat16

SMEM = pl.BlockSpec(memory_space=pltpu.SMEM)
VMEM = pl.BlockSpec(memory_space=pltpu.VMEM)
ANY = pl.BlockSpec(memory_space=pl.ANY)


def swap_cores(block):
    return lax.ppermute(block, "seq", [(0, 1), (1, 0)])


def params(mib):
    return pltpu.CompilerParams(vmem_limit_bytes=mib * MIB)


def slot_of(step):
    return lax.rem(lax.axis_index("queue") + step, lax.axis_size("queue"))


def modulated_rows(values, scale_row, shift_row):
    normed = values * lax.rsqrt(jnp.mean(values * values, axis=-1, keepdims=True) + EPS)
    return (normed * (1.0 + scale_row) + shift_row).astype(BF16)


def modulate(state, levels, level_scale, level_shift):
    def kernel(levels_ref, state_ref, scale_ref, shift_ref, out_ref):
        row = pl.ds(levels_ref[slot_of(0)], 1)
        out_ref[...] = modulated_rows(state_ref[...].astype(F32), scale_ref[row, :], shift_ref[row, :])

    return pl.pallas_call(
        kernel,
        out_shape=jax.ShapeDtypeStruct(state.shape, BF16),
        in_specs=[SMEM, VMEM, VMEM, VMEM],
        out_specs=VMEM,
        compiler_params=params(16),
    )(levels, state, level_scale, level_shift)


def head_normed(values, gain_row):
    width = values.shape[1]
    squares = values * values
    high = squares.astype(BF16)
    low = (squares - high.astype(F32)).astype(BF16)
    row = lax.broadcasted_iota(jnp.int32, (2 * width, width), 0)
    column = lax.broadcasted_iota(jnp.int32, (2 * width, width), 1)
    row = jnp.where(row >= width, row - width, row)
    same = (row // HD == column // HD).astype(BF16)
    sums = jnp.dot(jnp.concatenate([high, low], axis=1), same, preferred_element_type=F32)
    return values * lax.rsqrt(sums * (1.0 / HD) + EPS) * gain_row


def keys_values(mine, other, qk_gain, wk, wv):
    half, depth = mine.shape
    width = wk.shape[1]
    blocks = width // BLOCK

    def kernel(gain_ref, mine_ref, other_ref, wk_ref, wv_ref, out_ref, whole):
        step = pl.program_id(0)

        @pl.when(step == 0)
        def _():
            whole[:half, :] = mine_ref[...]
            whole[half:, :] = other_ref[...]

        @pl.when(step < blocks)
        def _():
            keys = jnp.dot(whole[...], wk_ref[...], preferred_element_type=F32)
            gain = jnp.concatenate([gain_ref[1:2, :]] * (BLOCK // HD), axis=1)
            out_ref[0] = head_normed(keys, gain).astype(BF16)

        @pl.when(step >= blocks)
        def _():
            out_ref[0] = jnp.dot(whole[...], wv_ref[...], preferred_element_type=F32).astype(BF16)

    return pl.pallas_call(
        kernel,
        grid=(2 * blocks,),
        out_shape=jax.ShapeDtypeStruct((2, 2 * half, width), BF16),
        in_specs=[
            pl.BlockSpec((2, HD), lambda i: (0, 0)),
            pl.BlockSpec((half, depth), lambda i: (0, 0)),
            pl.BlockSpec((half, depth), lambda i: (0, 0)),
            pl.BlockSpec((depth, BLOCK), lambda i: (0, jnp.minimum(i, blocks - 1))),
            pl.BlockSpec((depth, BLOCK), lambda i: (0, jnp.maximum(i - blocks, 0))),
        ],
        out_specs=pl.BlockSpec((1, 2 * half, BLOCK), lambda i: (i // blocks, 0, i % blocks)),
        scratch_shapes=[pltpu.VMEM((2 * half, depth), BF16)],
        compiler_params=params(32),
    )(qk_gain, mine, other, wk, wv)


def queries(mine, other, qk_gain, wq):
    half, depth = mine.shape
    width = wq.shape[1]
    blocks = width // BLOCK
    scale = math.log2(math.e) / math.sqrt(HD)

    def kernel(gain_ref, mine_ref, other_ref, wq_ref, out_ref, whole):
        @pl.when(pl.program_id(0) == 0)
        def _():
            whole[:half, :] = mine_ref[...]
            whole[half:, :] = other_ref[...]

        query = jnp.dot(whole[...], wq_ref[...], preferred_element_type=F32)
        gain = jnp.concatenate([gain_ref[0:1, :] * scale] * (BLOCK // HD), axis=1)
        out_ref[...] = head_normed(query, gain).astype(BF16)

    return pl.pallas_call(
        kernel,
        grid=(blocks,),
        out_shape=jax.ShapeDtypeStruct((2 * half, width), BF16),
        in_specs=[
            pl.BlockSpec((2, HD), lambda i: (0, 0)),
            pl.BlockSpec((half, depth), lambda i: (0, 0)),
            pl.BlockSpec((half, depth), lambda i: (0, 0)),
            pl.BlockSpec((depth, BLOCK), lambda i: (0, i)),
        ],
        out_specs=pl.BlockSpec((2 * half, BLOCK), lambda i: (0, i)),
        scratch_shapes=[pltpu.VMEM((2 * half, depth), BF16)],
        compiler_params=params(32),
    )(qk_gain, mine, other, wq)


def window_bias(pattern_ref, bias_ref, slot, count, core, frame_rows):
    lane = lax.broadcasted_iota(jnp.int32, (1, LANES), 1)
    half = FRAMES // 2
    for block in range(3):
        absent = (slot == 0) if block == 0 else (slot == count - 1)
        for at in range(FRAMES):
            key_frame = lax.rem(at + half * core, FRAMES)
            row = jnp.zeros((1, LANES), F32)
            for f in range(FRAMES):
                if block == 1 and f == at:
                    continue
                closed = pattern_ref[lax.rem(f + half * core, FRAMES), block * FRAMES + key_frame] != 1
                if block != 1:
                    closed = jnp.logical_or(closed, absent)
                row = row + jnp.where(lane == f, jnp.where(closed, CLOSED, 0.0), 0.0)
            first = (block * FRAMES + at) * frame_rows
            bias_ref[first : first + frame_rows, :] = jnp.broadcast_to(row, (frame_rows, LANES)).astype(BF16)


def attend_project(step, query, before, own, after, pattern, wo):
    tokens, width = query.shape
    half = tokens // 2
    out_width = wo.shape[1]
    pairs = width // LANES

    def kernel(pattern_ref, query_ref, before_ref, own_ref, after_ref, wo_ref, keep_ref, send_ref, bias, key_all, value_all, attended, wo_all, sem):
        copy = pltpu.make_async_copy(wo_ref, wo_all, sem)
        copy.start()
        window_bias(
            pattern_ref, bias, slot_of(step), lax.axis_size("queue"), lax.axis_index("seq"), tokens // FRAMES
        )
        lane = lax.broadcasted_iota(jnp.int32, (tokens, LANES), 1)
        frame = lax.broadcasted_iota(jnp.int32, (tokens, LANES), 0) // (tokens // FRAMES)
        frame_of = (lane == frame).astype(BF16)
        first = lane < HD
        key_all[:, LANES:] = bias[...]
        value_all[:, LANES:] = jnp.ones((3 * tokens, LANES), BF16)
        for pair in range(pairs):
            columns = slice(pair * LANES, (pair + 1) * LANES)
            for i, ref in enumerate((before_ref, own_ref, after_ref)):
                rows = slice(i * tokens, (i + 1) * tokens)
                key_all[rows, :LANES] = ref[0, :, columns]
                value_all[rows, :LANES] = ref[1, :, columns]
            query_pair = query_ref[:, columns]
            outs = []
            for which in (first, jnp.logical_not(first)):
                one = jnp.where(which, query_pair, jnp.zeros_like(query_pair))
                one = jnp.concatenate([one, frame_of], axis=1)
                scores = lax.dot_general(
                    one, key_all[...], (((1,), (1,)), ((), ())), preferred_element_type=F32
                )
                weights = jnp.exp2(scores).astype(BF16)
                both = jnp.dot(weights, value_all[...], preferred_element_type=F32)
                outs.append(both[:, :LANES] / both[:, LANES:])
            attended[:, columns] = jnp.where(first, outs[0], outs[1]).astype(BF16)
        copy.wait()
        for block in range(out_width // OUT_BLOCK):
            columns = slice(block * OUT_BLOCK, (block + 1) * OUT_BLOCK)
            term = jnp.dot(attended[...], wo_all[:, columns], preferred_element_type=F32).astype(BF16)
            keep_ref[:, columns] = term[:half]
            send_ref[:, columns] = term[half:]

    out = jax.ShapeDtypeStruct((half, out_width), BF16)
    return pl.pallas_call(
        kernel,
        out_shape=(out, out),
        in_specs=[SMEM, VMEM, VMEM, VMEM, VMEM, ANY],
        out_specs=(VMEM, VMEM),
        scratch_shapes=[
            pltpu.VMEM((3 * tokens, LANES), BF16),
            pltpu.VMEM((3 * tokens, 2 * LANES), BF16),
            pltpu.VMEM((3 * tokens, 2 * LANES), BF16),
            pltpu.VMEM((tokens, width), BF16),
            pltpu.VMEM(wo.shape, BF16),
            pltpu.SemaphoreType.DMA(()),
        ],
        compiler_params=params(40),
    )(pattern, query, before, own, after, wo)


def update(step, state, kept, received, fresh_noise, levels, entry, step_size, level_scale, level_shift):
    last = step == ITERS - 1

    def kernel(levels_ref, entry_ref, size_ref, state_ref, kept_ref, received_ref, noise_ref, scale_ref, shift_ref, *rest):
        out_ref, sem = rest[0], rest[-1]
        count = lax.axis_size("queue")
        slot = slot_of(step)
        next_slot = lax.rem(slot + 1, count)
        velocity = kept_ref[...].astype(F32) + received_ref[...].astype(F32)
        out_ref[...] = (state_ref[...].astype(F32) + size_ref[levels_ref[slot]] * velocity).astype(BF16)

        @pl.when(next_slot == entry_ref[step])
        def _():
            copy = pltpu.make_async_copy(noise_ref.at[step], out_ref, sem)
            copy.start()
            copy.wait()

        if not last:
            row = pl.ds(levels_ref[next_slot], 1)
            rest[1][...] = modulated_rows(out_ref[...].astype(F32), scale_ref[row, :], shift_ref[row, :])

    out = jax.ShapeDtypeStruct(state.shape, BF16)
    return pl.pallas_call(
        kernel,
        out_shape=(out,) if last else (out, out),
        in_specs=[SMEM, SMEM, SMEM, VMEM, VMEM, VMEM, ANY, VMEM, VMEM],
        out_specs=(VMEM,) if last else (VMEM, VMEM),
        scratch_shapes=[pltpu.SemaphoreType.DMA(())],
        compiler_params=params(24),
    )(levels, entry, step_size, state, kept, received, fresh_noise, level_scale, level_shift)


def on_device(
    latents, fresh_noise, levels, pattern, entry, level_scale, level_shift, step_size, qk_gain, wq, wk, wv, wo
):
    count = lax.axis_size("queue")
    forward = [(i, (i + 1) % count) for i in range(count)]
    backward = [((i + 1) % count, i) for i in range(count)]
    state = latents[0]
    modulated = modulate(state, levels, level_scale, level_shift)
    for step in range(ITERS):
        other = swap_cores(modulated)
        own = keys_values(modulated, other, qk_gain, wk, wv)
        before = lax.ppermute(own, "queue", forward)
        after = lax.ppermute(own, "queue", backward)
        query = queries(modulated, other, qk_gain, wq)
        kept, sent = attend_project(step, query, before, own, after, pattern, wo)
        received = swap_cores(sent)
        state, *rest = update(
            step, state, kept, received, fresh_noise, levels, entry, step_size, level_scale, level_shift
        )
        if rest:
            modulated = rest[0]
    route = [(i, (i + ITERS) % count) for i in range(count)]
    return lax.ppermute(state, "queue", route)[None]


def solution(mesh):
    return jax.shard_map(
        on_device,
        mesh=mesh,
        in_specs=(
            P("queue", "seq", None),
            P(None, "seq", None),
            P(),
            P(),
            P(),
            P(),
            P(),
            P(),
            P(),
            P(None, "seq"),
            P(None, "seq"),
            P(None, "seq"),
            P("seq", None),
        ),
        out_specs=P("queue", "seq", None),
        check_vma=False,
    )
```

time: 203 us -> 140 us (0.69)
  matrix products: 69.4 us -> 0 us
  Pallas kernels: 0 us -> 30.9 us
  other arithmetic: 19.9 us -> 0.01 us
  between operations: 5.66 us -> 0.26 us
  waiting for transfers between devices: 68.3 us -> 72.2 us
  local copies, waits for them, and re-layouts: 21.1 us -> 18.8 us
    dot_general x56 -> x0, matrix products: 69.4 us -> none  [the longest x24 30.8 us: one_head(): jnp.dot(query_head, key_head.T, preferred_element_type=jnp.float32) * scale]
    pallas_call x0 -> x9, Pallas kernels: none -> 30.9 us  [the longest x2 10.9 us: keys_values(): pl.pallas_call(kernel, grid=(2 * blocks,), out_shape=jax.ShapeDtypeStruct...]
    unnamed x35 -> x65, local copies, waits for them, and re-layouts: 2.2 us -> 18.8 us
    reduce_sum x30 -> x0, other arithmetic: 11 us -> none  [the longest x24 6.73 us: one_head(): jnp.sum(expo, axis=-1, keepdims=True)]
    reshape x30 -> x0, local copies, waits for them, and re-layouts: 7.23 us -> none  [the longest x24 6.7 us: on_device(): jnp.repeat(jnp.repeat(table, per_frame, axis=0), per_frame, axis=1)]
    slice x9 -> x0, local copies, waits for them, and re-layouts: 5.22 us -> none  [the longest x2 2.93 us: on_device(): window[0]]
    ppermute x4, waiting for transfers between devices: 3.14 us -> 7.65 us  [swap_cores(): return lax.ppermute(block, 'seq', [(0, 1), (1, 0)])]
    convert_element_type x4 -> x0, other arithmetic: 3.2 us -> none  [the longest x2 1.73 us: modulate(): return (normed * (1.0 + scale_row) + shift_row).astype(jnp.bfloat16)]
  transfers between devices with their start and end apart: 9 -> 9, of which waited for: 9 -> 9; matrix products, arithmetic and copies ran while one was open for 5% -> 0% of each run, Pallas kernels for 0% -> 4%
where the time goes in v2:
time: 140 us
  waiting for transfers between devices  72.2 us (52%)
  Pallas kernels  30.9 us (22%)
  local copies, waits for them, and re-layouts  18.8 us (13%)
  starting transfers between devices  17.4 us (12%)
    ppermute x2, waiting for transfers between devices, on_device(): after = lax.ppermute(own, 'queue', backward)  27.7 us
    ppermute x1, waiting for transfers between devices, on_device(): return lax.ppermute(state, 'queue', route)[None]  24.5 us
    unnamed x65, local copies, waits for them, and re-layouts  18.8 us
    ppermute x2, waiting for transfers between devices, on_device(): before = lax.ppermute(own, 'queue', forward)  12.4 us
    pallas_call x2, Pallas kernels, keys_values(): pl.pallas_call(kernel, grid=(2 * blocks,), out_shape=jax.ShapeDtypeStruct...  10.9 us
    pallas_call x2, Pallas kernels, attend_project(): pl.pallas_call(kernel, out_shape=(out, out), in_specs=[SMEM, VMEM, VMEM,...  10.6 us
    ppermute x2, starting transfers between devices, on_device(): after = lax.ppermute(own, 'queue', backward)  9.54 us
    ppermute x4, waiting for transfers between devices, swap_cores(): return lax.ppermute(block, 'seq', [(0, 1), (1, 0)])  7.65 us
  transfers between devices with their start and end apart: 9, of which 9 were waited for; matrix products, arithmetic and copies ran while one was open for 0% of the time, Pallas kernels for 4%

profile of v2, /device:TPU:1, one launch (start us, length us, event | category | flops | bytes accessed | tf_op | source)
XLA Modules:
  0.0 139.6 jit_solution(10105015364713962766)
XLA Ops:
  0.0 1.1 copy-done.5
  1.1 1.1 copy-done.8
  2.2 1.1 copy-done.11
  4.0 1.1 shard_map.127.mine_ref
  5.1 3.3 %collective-permute-start = (bf16[128,3072]{1,0:T(8,128)(2,1)S(1)}, bf16[128,3072]{1,0:T(8,128)(2,1)S(1)}, u32[]{:S(2)}, u32[]{:S(2)}) collective-permute-start(bf16[128,3072]{1,0:T(8,128)(2,1)S(1)} %shard_map.127.mine_ref), channel_id=1, source_target_pairs={{0,1},{1,0},{2,3},{3,2},{4,5},{5,4},{6,7},{7,6},{8,9},{9,8},{10,11... | collective-permute-start | bytes 2359304 | tf_op jit(solution)/shard_map/ppermute | solution.py:28
  8.4 1.9 %collective-permute-done.other_ref = bf16[128,3072]{1,0:T(8,128)(2,1)S(1)} collective-permute-done((bf16[128,3072]{1,0:T(8,128)(2,1)S(1)}, bf16[128,3072]{1,0:T(8,128)(2,1)S(1)}, u32[]{:S(2)}, u32[]{:S(2)}) %collective-permute-start) | collective-permute-done | bytes 786464 | tf_op jit(solution)/shard_map/ppermute | solution.py:28
  10.3 2.3 %copy-done = bf16[3072,768]{1,0:T(8,128)(2,1)S(1)} copy-done((bf16[3072,768]{1,0:T(8,128)(2,1)S(1)}, bf16[3072,768]{1,0:T(8,128)(2,1)}, u32[]{:S(2)}) %copy-start) | copy-done | bytes 4718616
  12.6 2.3 %copy-done.1 = bf16[3072,768]{1,0:T(8,128)(2,1)S(1)} copy-done((bf16[3072,768]{1,0:T(8,128)(2,1)S(1)}, bf16[3072,768]{1,0:T(8,128)(2,1)}, u32[]{:S(2)}) %copy-start.1) | copy-done | bytes 4718616
  15.7 5.4 %shard_map.129.own_ref = bf16[2,256,768]{2,1,0:T(8,128)(2,1)S(1)} custom-call(f32[2,64]{1,0:T(2,128)S(1)} %copy-done.19, bf16[128,3072]{1,0:T(8,128)(2,1)S(1)} %shard_map.127.mine_ref, bf16[128,3072]{1,0:T(8,128)(2,1)S(1)} %collective-permute-done.other_ref, bf16[3072,768]{1,0:T(8,128)(2,1)S(1)} %copy-done, bf16[3072,768]{1,0:T(8,128)(2,1)S(1)} %copy-done.1), custom_call_target="tpu_custom_call" | custom-call | tf_op jit(solution)/shard_map/pallas_call | solution.py:94
  21.2 8.6 %collective-permute-start.2 = (bf16[2,256,768]{2,1,0:T(8,128)(2,1)S(1)}, bf16[2,256,768]{2,1,0:T(8,128)(2,1)S(1)}, u32[]{:S(2)}, u32[]{:S(2)}) collective-permute-start(bf16[2,256,768]{2,1,0:T(8,128)(2,1)S(1)} %shard_map.129.own_ref), channel_id=1, source_target_pairs={{2,0},{4,2},{6,4},{8,6},{10,8},{12,10},{14,12},{16,14},{18,16},{20... | collective-permute-start | bytes 2359304 | tf_op jit(solution)/shard_map/ppermute | solution.py:267
  29.8 3.0 %shard_map.128.query_ref = bf16[256,768]{1,0:T(8,128)(2,1)S(1)} custom-call(f32[2,64]{1,0:T(2,128)S(1)} %copy-done.19, bf16[128,3072]{1,0:T(8,128)(2,1)S(1)} %shard_map.127.mine_ref, bf16[128,3072]{1,0:T(8,128)(2,1)S(1)} %collective-permute-done.other_ref, bf16[3072,768]{1,0:T(8,128)(2,1)S(1)} %copy-done.3), custom_call_target="tpu_custom_call" | custom-call | tf_op jit(solution)/shard_map/pallas_call | solution.py:127
  32.8 13.5 %collective-permute-done.2.after_ref = bf16[2,256,768]{2,1,0:T(8,128)(2,1)S(1)} collective-permute-done((bf16[2,256,768]{2,1,0:T(8,128)(2,1)S(1)}, bf16[2,256,768]{2,1,0:T(8,128)(2,1)S(1)}, u32[]{:S(2)}, u32[]{:S(2)}) %collective-permute-start.2) | collective-permute-done | bytes 786464 | tf_op jit(solution)/shard_map/ppermute | solution.py:267
  47.2 6.4 %collective-permute-done.1.before_ref = bf16[2,256,768]{2,1,0:T(8,128)(2,1)S(1)} collective-permute-done((bf16[2,256,768]{2,1,0:T(8,128)(2,1)S(1)}, bf16[2,256,768]{2,1,0:T(8,128)(2,1)S(1)}, u32[]{:S(2)}, u32[]{:S(2)}) %collective-permute-start.1) | collective-permute-done | bytes 786464 | tf_op jit(solution)/shard_map/ppermute | solution.py:266
  54.5 1.1 copy-done.14
  55.6 1.1 copy-done.16
  56.8 1.1 copy-done.18
  57.9 5.3 %shard_map.130 = (bf16[128,3072]{1,0:T(8,128)(2,1)S(1)}, bf16[128,3072]{1,0:T(8,128)(2,1)S(1)}) custom-call(s32[4,12]{1,0:T(4,128)S(1)} %copy-done.21, bf16[256,768]{1,0:T(8,128)(2,1)S(1)} %shard_map.128.query_ref, bf16[2,256,768]{2,1,0:T(8,128)(2,1)S(1)} %copy-done.18, bf16[2,256,768]{2,1,0:T(8,128)(2,1)S(1)} %copy-done.14, ...), custom_call_target="tpu_custom_call" | custom-call | tf_op jit(solution)/shard_map/pallas_call | solution.py:206
  63.2 1.6 %collective-permute-start.3 = (bf16[128,3072]{1,0:T(8,128)(2,1)S(1)}, bf16[128,3072]{1,0:T(8,128)(2,1)S(1)}, u32[]{:S(2)}, u32[]{:S(2)}) collective-permute-start(bf16[128,3072]{1,0:T(8,128)(2,1)S(1)} %get-tuple-element.12), channel_id=1, source_target_pairs={{0,1},{1,0},{2,3},{3,2},{4,5},{5,4},{6,7},{7,6},{8,9},{9,8},{10,11... | collective-permute-start | bytes 2359304 | tf_op jit(solution)/shard_map/ppermute | solution.py:28
  64.8 1.9 %collective-permute-done.3.received_ref = bf16[128,3072]{1,0:T(8,128)(2,1)S(1)} collective-permute-done((bf16[128,3072]{1,0:T(8,128)(2,1)S(1)}, bf16[128,3072]{1,0:T(8,128)(2,1)S(1)}, u32[]{:S(2)}, u32[]{:S(2)}) %collective-permute-start.3) | collective-permute-done | bytes 786464 | tf_op jit(solution)/shard_map/ppermute | solution.py:28
  66.7 1.1 copy-done.6
  67.8 1.1 copy-done.9
  68.9 1.1 copy-done.12
  70.0 1.4 %shard_map.131 = (bf16[128,3072]{1,0:T(8,128)(2,1)S(1)}, bf16[128,3072]{1,0:T(8,128)(2,1)S(1)}) custom-call(s32[128]{0:T(128)S(1)} %copy-done.23, s32[2]{0:T(128)S(1)} %copy-done.24, f32[50]{0:T(128)S(1)} %copy-done.25, bf16[128,3072]{1,0:T(8,128)(2,1)S(1)} %bitcast.9, bf16[128,3072]{1,0:T(8,128)(2,1)S(1)} %get-tuple-element.11.kept_ref, ...), custom_call_target="tpu_custom_call" | custom-call | tf_op jit(solution)/shard_map/pallas_call | solution.py:245
  72.1 1.9 %collective-permute-done.4.other_ref = bf16[128,3072]{1,0:T(8,128)(2,1)S(1)} collective-permute-done((bf16[128,3072]{1,0:T(8,128)(2,1)S(1)}, bf16[128,3072]{1,0:T(8,128)(2,1)S(1)}, u32[]{:S(2)}, u32[]{:S(2)}) %collective-permute-start.4) | collective-permute-done | bytes 786464 | tf_op jit(solution)/shard_map/ppermute | solution.py:28
  74.1 5.4 %shard_map.133.own_ref = bf16[2,256,768]{2,1,0:T(8,128)(2,1)S(1)} custom-call(f32[2,64]{1,0:T(2,128)S(1)} %copy-done.20, bf16[128,3072]{1,0:T(8,128)(2,1)S(1)} %get-tuple-element.14.mine_ref, bf16[128,3072]{1,0:T(8,128)(2,1)S(1)} %collective-permute-done.4.other_ref, bf16[3072,768]{1,0:T(8,128)(2,1)S(1)} %bitcast.3, bf16[3072,768]{1,0:T(8,128)(2,1)S(1)} %bitcast.5), custom_call_target="tpu_custom_call" | custom-call | tf_op jit(solution)/shard_map/pallas_call | solution.py:94
  81.1 3.0 %shard_map.132.query_ref = bf16[256,768]{1,0:T(8,128)(2,1)S(1)} custom-call(f32[2,64]{1,0:T(2,128)S(1)} %copy-done.20, bf16[128,3072]{1,0:T(8,128)(2,1)S(1)} %get-tuple-element.14.mine_ref, bf16[128,3072]{1,0:T(8,128)(2,1)S(1)} %collective-permute-done.4.other_ref, bf16[3072,768]{1,0:T(8,128)(2,1)S(1)} %bitcast.7), custom_call_target="tpu_custom_call" | custom-call | tf_op jit(solution)/shard_map/pallas_call | solution.py:127
  84.1 14.2 %collective-permute-done.6.after_ref = bf16[2,256,768]{2,1,0:T(8,128)(2,1)S(1)} collective-permute-done((bf16[2,256,768]{2,1,0:T(8,128)(2,1)S(1)}, bf16[2,256,768]{2,1,0:T(8,128)(2,1)S(1)}, u32[]{:S(2)}, u32[]{:S(2)}) %collective-permute-start.6) | collective-permute-done | bytes 786464 | tf_op jit(solution)/shard_map/ppermute | solution.py:267
  98.4 6.0 %collective-permute-done.5.before_ref = bf16[2,256,768]{2,1,0:T(8,128)(2,1)S(1)} collective-permute-done((bf16[2,256,768]{2,1,0:T(8,128)(2,1)S(1)}, bf16[2,256,768]{2,1,0:T(8,128)(2,1)S(1)}, u32[]{:S(2)}, u32[]{:S(2)}) %collective-permute-start.5) | collective-permute-done | bytes 786464 | tf_op jit(solution)/shard_map/ppermute | solution.py:266
  104.4 5.3 %shard_map.134 = (bf16[128,3072]{1,0:T(8,128)(2,1)S(1)}, bf16[128,3072]{1,0:T(8,128)(2,1)S(1)}) custom-call(s32[4,12]{1,0:T(4,128)S(1)} %copy-done.21, bf16[256,768]{1,0:T(8,128)(2,1)S(1)} %shard_map.132.query_ref, bf16[2,256,768]{2,1,0:T(8,128)(2,1)S(1)} %collective-permute-done.5.before_ref, bf16[2,256,768]{2,1,0:T(8,128)(2,1)S(1)} %shard_map.133.own_ref, ...), custom_call_target="tpu_custom_call" | custom-call | tf_op jit(solution)/shard_map/pallas_call | solution.py:206
  109.7 1.6 %collective-permute-start.7 = (bf16[128,3072]{1,0:T(8,128)(2,1)S(1)}, bf16[128,3072]{1,0:T(8,128)(2,1)S(1)}, u32[]{:S(2)}, u32[]{:S(2)}) collective-permute-start(bf16[128,3072]{1,0:T(8,128)(2,1)S(1)} %get-tuple-element.16), channel_id=1, source_target_pairs={{0,1},{1,0},{2,3},{3,2},{4,5},{5,4},{6,7},{7,6},{8,9},{9,8},{10,11... | collective-permute-start | bytes 2359304 | tf_op jit(solution)/shard_map/ppermute | solution.py:28
  111.3 1.9 %collective-permute-done.7.received_ref = bf16[128,3072]{1,0:T(8,128)(2,1)S(1)} collective-permute-done((bf16[128,3072]{1,0:T(8,128)(2,1)S(1)}, bf16[128,3072]{1,0:T(8,128)(2,1)S(1)}, u32[]{:S(2)}, u32[]{:S(2)}) %collective-permute-start.7) | collective-permute-done | bytes 786464 | tf_op jit(solution)/shard_map/ppermute | solution.py:28
  114.2 24.5 %collective-permute-done.8 = bf16[128,3072]{1,0:T(8,128)(2,1)S(1)} collective-permute-done((bf16[128,3072]{1,0:T(8,128)(2,1)S(1)}, bf16[128,3072]{1,0:T(8,128)(2,1)S(1)}, u32[]{:S(2)}, u32[]{:S(2)}) %collective-permute-start.8) | collective-permute-done | bytes 786464 | tf_op jit(solution)/shard_map/ppermute | solution.py:277
  (63 shorter events, 7.3 us)
Async XLA Ops:
  2.2 1.1 copy-start.11
  5.1 5.2 %collective-permute-start = (bf16[128,3072]{1,0:T(8,128)(2,1)S(1)}, bf16[128,3072]{1,0:T(8,128)(2,1)S(1)}, u32[]{:S(2)}, u32[]{:S(2)}) collective-permute-start(bf16[128,3072]{1,0:T(8,128)(2,1)S(1)} %shard_map.127.mine_ref), channel_id=1, source_target_pairs={{0,1},{1,0},{2,3},{3,2},{4,5},{5,4},{6,7},{7,6},{8,9},{9,8},{10,11... | collective-permute-start | bytes 2359304 | tf_op jit(solution)/shard_map/ppermute | solution.py:28
  10.3 2.3 %copy-start = (bf16[3072,768]{1,0:T(8,128)(2,1)S(1)}, bf16[3072,768]{1,0:T(8,128)(2,1)}, u32[]{:S(2)}) copy-start(bf16[3072,768]{1,0:T(8,128)(2,1)} %wk_ref.3) | copy-start | bytes 14155780
  12.6 2.3 %copy-start.1 = (bf16[3072,768]{1,0:T(8,128)(2,1)S(1)}, bf16[3072,768]{1,0:T(8,128)(2,1)}, u32[]{:S(2)}) copy-start(bf16[3072,768]{1,0:T(8,128)(2,1)} %wv_ref.3) | copy-start | bytes 14155780
  15.7 14.1 %copy-start.3 = (bf16[3072,768]{1,0:T(8,128)(2,1)S(1)}, bf16[3072,768]{1,0:T(8,128)(2,1)}, u32[]{:S(2)}) copy-start(bf16[3072,768]{1,0:T(8,128)(2,1)} %wq_ref.3) | copy-start | bytes 14155780
  15.7 38.8 %copy-start.21 = (s32[4,12]{1,0:T(4,128)S(1)}, s32[4,12]{1,0:T(4,128)}, u32[]{:S(2)}) copy-start(s32[4,12]{1,0:T(4,128)} %pattern_ref.3) | copy-start | bytes 580
  15.7 51.0 %copy-start.23 = (s32[128]{0:T(128)S(1)}, s32[128]{0:T(128)}, u32[]{:S(2)}) copy-start(s32[128]{0:T(128)} %levels_ref.5) | copy-start | bytes 1540
  15.7 51.0 %copy-start.24 = (s32[2]{0:T(128)S(1)}, s32[2]{0:T(128)}, u32[]{:S(2)}) copy-start(s32[2]{0:T(128)} %entry_ref.3) | copy-start | bytes 28
  15.7 51.0 %copy-start.25 = (f32[50]{0:T(128)S(1)}, f32[50]{0:T(128)}, u32[]{:S(2)}) copy-start(f32[50]{0:T(128)} %size_ref.3) | copy-start | bytes 604
  15.7 58.4 %copy-start.20 = (f32[2,64]{1,0:T(2,128)S(1)}, f32[2,64]{1,0:T(2,128)}, u32[]{:S(2)}) copy-start(f32[2,64]{1,0:T(2,128)} %gain_ref.7) | copy-start | bytes 1540
  21.1 11.7 %copy-start.13 = (bf16[2,256,768]{2,1,0:T(8,128)(2,1)}, bf16[2,256,768]{2,1,0:T(8,128)(2,1)S(1)}, u32[]{:S(2)}) copy-start(bf16[2,256,768]{2,1,0:T(8,128)(2,1)S(1)} %shard_map.129.own_ref) | copy-start | bytes 2359300
  21.1 33.3 %copy-start.2 = (bf16[768,3072]{1,0:T(8,128)(2,1)S(1)}, bf16[768,3072]{1,0:T(8,128)(2,1)}, u32[]{:S(2)}) copy-start(bf16[768,3072]{1,0:T(8,128)(2,1)} %wo_ref.3) | copy-start | bytes 14155780
  21.2 25.1 %collective-permute-start.2 = (bf16[2,256,768]{2,1,0:T(8,128)(2,1)S(1)}, bf16[2,256,768]{2,1,0:T(8,128)(2,1)S(1)}, u32[]{:S(2)}, u32[]{:S(2)}) collective-permute-start(bf16[2,256,768]{2,1,0:T(8,128)(2,1)S(1)} %shard_map.129.own_ref), channel_id=1, source_target_pairs={{2,0},{4,2},{6,4},{8,6},{10,8},{12,10},{14,12},{16,14},{18,16},{20... | collective-permute-start | bytes 2359304 | tf_op jit(solution)/shard_map/ppermute | solution.py:267
  29.7 37.0 %copy-start.4 = (bf16[2,128,3072]{2,1,0:T(8,128)(2,1)S(1)}, bf16[2,128,3072]{2,1,0:T(8,128)(2,1)}, u32[]{:S(2)}) copy-start(bf16[2,128,3072]{2,1,0:T(8,128)(2,1)} %noise_ref.3) | copy-start | bytes 4718596
  29.7 23.9 %collective-permute-start.1 = (bf16[2,256,768]{2,1,0:T(8,128)(2,1)S(1)}, bf16[2,256,768]{2,1,0:T(8,128)(2,1)S(1)}, u32[]{:S(2)}, u32[]{:S(2)}) collective-permute-start(bf16[2,256,768]{2,1,0:T(8,128)(2,1)S(1)} %shard_map.129.own_ref), channel_id=1, source_target_pairs={{0,2},{2,4},{4,6},{6,8},{8,10},{10,12},{12,14},{14,16},{16,18},{18... | collective-permute-start | bytes 2359304 | tf_op jit(solution)/shard_map/ppermute | solution.py:266
  29.7 44.3 %slice-start = ((s8[4718592]{0:T(1024)(128)(4,1)}), s8[4194304]{0:T(1024)(128)(4,1)S(1)}, s32[]{:S(2)}) async-start(s8[4718592]{0:T(1024)(128)(4,1)} %bitcast.2), calls=%async_computation | async-start | bytes 8388608
  29.7 44.3 %slice-start.2 = ((s8[4718592]{0:T(1024)(128)(4,1)}), s8[4194304]{0:T(1024)(128)(4,1)S(1)}, s32[]{:S(2)}) async-start(s8[4718592]{0:T(1024)(128)(4,1)} %bitcast.4), calls=%async_computation.2 | async-start | bytes 8388608
  32.8 41.3 %slice-start.1 = ((s8[4718592]{0:T(1024)(128)(4,1)}), s8[524288]{0:T(1024)(128)(4,1)S(1)}, s32[]{:S(2)}) async-start(s8[4718592]{0:T(1024)(128)(4,1)} %bitcast.2), calls=%async_computation.1 | async-start | bytes 1048576
  32.8 41.3 %slice-start.3 = ((s8[4718592]{0:T(1024)(128)(4,1)}), s8[524288]{0:T(1024)(128)(4,1)S(1)}, s32[]{:S(2)}) async-start(s8[4718592]{0:T(1024)(128)(4,1)} %bitcast.4), calls=%async_computation.3 | async-start | bytes 1048576
  54.5 1.1 copy-start.14
  55.6 1.1 copy-start.16
  63.2 3.5 %collective-permute-start.3 = (bf16[128,3072]{1,0:T(8,128)(2,1)S(1)}, bf16[128,3072]{1,0:T(8,128)(2,1)S(1)}, u32[]{:S(2)}, u32[]{:S(2)}) collective-permute-start(bf16[128,3072]{1,0:T(8,128)(2,1)S(1)} %get-tuple-element.12), channel_id=1, source_target_pairs={{0,1},{1,0},{2,3},{3,2},{4,5},{5,4},{6,7},{7,6},{8,9},{9,8},{10,11... | collective-permute-start | bytes 2359304 | tf_op jit(solution)/shard_map/ppermute | solution.py:28
  68.9 1.1 copy-start.12
  71.5 9.6 %slice-start.4 = ((s8[4718592]{0:T(1024)(128)(4,1)}), s8[4194304]{0:T(1024)(128)(4,1)S(1)}, s32[]{:S(2)}) async-start(s8[4718592]{0:T(1024)(128)(4,1)} %bitcast.6), calls=%async_computation.4 | async-start | bytes 8388608
  71.5 9.6 %slice-start.5 = ((s8[4718592]{0:T(1024)(128)(4,1)}), s8[524288]{0:T(1024)(128)(4,1)S(1)}, s32[]{:S(2)}) async-start(s8[4718592]{0:T(1024)(128)(4,1)} %bitcast.6), calls=%async_computation.5 | async-start | bytes 1048576
  71.5 2.6 %collective-permute-start.4 = (bf16[128,3072]{1,0:T(8,128)(2,1)S(1)}, bf16[128,3072]{1,0:T(8,128)(2,1)S(1)}, u32[]{:S(2)}, u32[]{:S(2)}) collective-permute-start(bf16[128,3072]{1,0:T(8,128)(2,1)S(1)} %get-tuple-element.14.mine_ref), channel_id=1, source_target_pairs={{0,1},{1,0},{2,3},{3,2},{4,5},{5,4},{6,7},{7,6},{8,9},{9,8},{10,11... | collective-permute-start | bytes 2359304 | tf_op jit(solution)/shard_map/ppermute | solution.py:28
  79.5 18.8 %collective-permute-start.6 = (bf16[2,256,768]{2,1,0:T(8,128)(2,1)S(1)}, bf16[2,256,768]{2,1,0:T(8,128)(2,1)S(1)}, u32[]{:S(2)}, u32[]{:S(2)}) collective-permute-start(bf16[2,256,768]{2,1,0:T(8,128)(2,1)S(1)} %shard_map.133.own_ref), channel_id=1, source_target_pairs={{2,0},{4,2},{6,4},{8,6},{10,8},{12,10},{14,12},{16,14},{18,16},{20... | collective-permute-start | bytes 2359304 | tf_op jit(solution)/shard_map/ppermute | solution.py:267
  80.5 23.9 %collective-permute-start.5 = (bf16[2,256,768]{2,1,0:T(8,128)(2,1)S(1)}, bf16[2,256,768]{2,1,0:T(8,128)(2,1)S(1)}, u32[]{:S(2)}, u32[]{:S(2)}) collective-permute-start(bf16[2,256,768]{2,1,0:T(8,128)(2,1)S(1)} %shard_map.133.own_ref), channel_id=1, source_target_pairs={{0,2},{2,4},{4,6},{6,8},{8,10},{10,12},{12,14},{14,16},{16,18},{18... | collective-permute-start | bytes 2359304 | tf_op jit(solution)/shard_map/ppermute | solution.py:266
  84.1 29.1 %copy-start.7 = (f32[50,3072]{1,0:T(8,128)S(1)}, f32[50,3072]{1,0:T(8,128)}, u32[]{:S(2)}) copy-start(f32[50,3072]{1,0:T(8,128)} %scale_ref.5) | copy-start | bytes 1843204
  84.1 29.1 %copy-start.10 = (f32[50,3072]{1,0:T(8,128)S(1)}, f32[50,3072]{1,0:T(8,128)}, u32[]{:S(2)}) copy-start(f32[50,3072]{1,0:T(8,128)} %shift_ref.5) | copy-start | bytes 1843204
  109.7 3.5 %collective-permute-start.7 = (bf16[128,3072]{1,0:T(8,128)(2,1)S(1)}, bf16[128,3072]{1,0:T(8,128)(2,1)S(1)}, u32[]{:S(2)}, u32[]{:S(2)}) collective-permute-start(bf16[128,3072]{1,0:T(8,128)(2,1)S(1)} %get-tuple-element.16), channel_id=1, source_target_pairs={{0,1},{1,0},{2,3},{3,2},{4,5},{5,4},{6,7},{7,6},{8,9},{9,8},{10,11... | collective-permute-start | bytes 2359304 | tf_op jit(solution)/shard_map/ppermute | solution.py:28
  114.1 24.6 %collective-permute-start.8 = (bf16[128,3072]{1,0:T(8,128)(2,1)S(1)}, bf16[128,3072]{1,0:T(8,128)(2,1)S(1)}, u32[]{:S(2)}, u32[]{:S(2)}) collective-permute-start(bf16[128,3072]{1,0:T(8,128)(2,1)S(1)} %shard_map.135), channel_id=1, source_target_pairs={{0,4},{2,6},{4,8},{6,10},{8,12},{10,14},{12,16},{14,18},{16,20},{1... | collective-permute-start | bytes 2359304 | tf_op jit(solution)/shard_map/ppermute | solution.py:277
  (9 other events, 8.6 us)

commit v3 on v2

v3 whole, which is shorter than its diff:
```python
import math

import jax
import jax.numpy as jnp
from jax import lax
from jax.experimental import pallas as pl
from jax.experimental.pallas import tpu as pltpu
from jax.sharding import PartitionSpec as P

HD = 64
FRAMES = 4
ITERS = 2
LANES = 128
EPS = 1e-06
CLOSED = -30000.0
BLOCK = 256
OUT_BLOCK = 768
MIB = 1 << 20
F32 = jnp.float32
BF16 = jnp.bfloat16

SMEM = pl.BlockSpec(memory_space=pltpu.SMEM)
VMEM = pl.BlockSpec(memory_space=pltpu.VMEM)
HBM = pl.BlockSpec(memory_space=pltpu.HBM)


def swap_cores(block):
    return lax.ppermute(block, "seq", [(0, 1), (1, 0)])


def in_hbm(*arrays):
    return tuple(pltpu.with_memory_space_constraint(array, pltpu.HBM) for array in arrays)


def params(mib):
    return pltpu.CompilerParams(vmem_limit_bytes=mib * MIB)


def slot_of(step):
    return lax.rem(lax.axis_index("queue") + step, lax.axis_size("queue"))


def modulated_rows(values, scale_row, shift_row):
    normed = values * lax.rsqrt(jnp.mean(values * values, axis=-1, keepdims=True) + EPS)
    return (normed * scale_row + shift_row).astype(BF16)


def head_normed(values, gain_row):
    width = values.shape[1]
    squares = values * values
    high = squares.astype(BF16)
    low = (squares - high.astype(F32)).astype(BF16)
    row = lax.broadcasted_iota(jnp.int32, (2 * width, width), 0)
    column = lax.broadcasted_iota(jnp.int32, (2 * width, width), 1)
    row = jnp.where(row >= width, row - width, row)
    same = (row // HD == column // HD).astype(BF16)
    sums = jnp.dot(jnp.concatenate([high, low], axis=1), same, preferred_element_type=F32)
    return values * lax.rsqrt(sums * (1.0 / HD) + EPS) * gain_row


def window_bias(pattern_ref, bias_ref, slot, frame_rows):
    count, core = lax.axis_size("queue"), lax.axis_index("seq")
    lane = lax.broadcasted_iota(jnp.int32, (1, LANES), 1)
    half = FRAMES // 2
    for block in range(3):
        absent = (slot == 0) if block == 0 else (slot == count - 1)
        for at in range(FRAMES):
            key_frame = lax.rem(at + half * core, FRAMES)
            row = jnp.zeros((1, LANES), F32)
            for f in range(FRAMES):
                if block == 1 and f == at:
                    continue
                closed = pattern_ref[lax.rem(f + half * core, FRAMES), block * FRAMES + key_frame] != 1
                if block != 1:
                    closed = jnp.logical_or(closed, absent)
                row = row + jnp.where(lane == f, jnp.where(closed, CLOSED, 0.0), 0.0)
            first = at * frame_rows
            bias_ref[block, first : first + frame_rows, :] = jnp.broadcast_to(row, (frame_rows, LANES)).astype(BF16)


def prepare(levels, level_scale, level_shift, wk, wv):
    depth = level_scale.shape[1]

    def kernel(levels_ref, scale_ref, shift_ref, wk_ref, wv_ref, rows_ref, wk_out, wv_out, held, levels_sm, sems):
        first = pltpu.make_async_copy(levels_ref, levels_sm, sems.at[0])
        first.start()
        weights = [
            pltpu.make_async_copy(wk_ref, wk_out, sems.at[1]),
            pltpu.make_async_copy(wv_ref, wv_out, sems.at[2]),
        ]
        tables = [
            pltpu.make_async_copy(scale_ref, held.at[0], sems.at[3]),
            pltpu.make_async_copy(shift_ref, held.at[1], sems.at[4]),
        ]
        for copy in tables + weights:
            copy.start()
        for copy in [first] + tables:
            copy.wait()
        for step in range(ITERS):
            row = pl.ds(levels_sm[slot_of(step)], 1)
            rows_ref[step, 0:1, :] = 1.0 + held[0, row, :]
            rows_ref[step, 1:2, :] = held[1, row, :]
        for copy in weights:
            copy.wait()

    return pl.pallas_call(
        kernel,
        out_shape=(
            jax.ShapeDtypeStruct((ITERS, 2, depth), F32),
            jax.ShapeDtypeStruct(wk.shape, BF16),
            jax.ShapeDtypeStruct(wv.shape, BF16),
        ),
        in_specs=[HBM] * 5,
        out_specs=(VMEM,) * 3,
        scratch_shapes=[
            pltpu.VMEM((2, *level_scale.shape), F32),
            pltpu.SMEM(levels.shape, jnp.int32),
            pltpu.SemaphoreType.DMA((5,)),
        ],
        compiler_params=params(8),
    )(*in_hbm(levels, level_scale, level_shift, wk, wv))


def project(step, whole, gain_ref, wk_ref, wv_ref, out_ref):
    width = wk_ref.shape[1]
    gain = jnp.concatenate([gain_ref[1:2, :]] * (BLOCK // HD), axis=1)
    for block in range(width // BLOCK):
        columns = slice(block * BLOCK, (block + 1) * BLOCK)
        keys = jnp.dot(whole[...], wk_ref[:, columns], preferred_element_type=F32)
        out_ref[0, :, columns] = head_normed(keys, gain).astype(BF16)
        values = jnp.dot(whole[...], wv_ref[:, columns], preferred_element_type=F32)
        out_ref[1, :, columns] = values.astype(BF16)


def first_keys_values(mine, other, rows, qk_gain, wk, wv):
    half, depth = mine.shape
    width = wk.shape[1]

    def kernel(mine_ref, other_ref, rows_ref, gain_ref, wk_ref, wv_ref, whole, out_ref):
        scale_row, shift_row = rows_ref[0, 0:1, :], rows_ref[0, 1:2, :]
        whole[:half, :] = modulated_rows(mine_ref[...].astype(F32), scale_row, shift_row)
        whole[half:, :] = modulated_rows(other_ref[...].astype(F32), scale_row, shift_row)
        project(0, whole, gain_ref, wk_ref, wv_ref, out_ref)

    return pl.pallas_call(
        kernel,
        out_shape=(
            jax.ShapeDtypeStruct((2 * half, depth), BF16),
            jax.ShapeDtypeStruct((2, 2 * half, width), BF16),
        ),
        in_specs=[VMEM] * 6,
        out_specs=(VMEM, VMEM),
        compiler_params=params(8),
    )(mine, other, rows, qk_gain, wk, wv)


def next_keys_values(step, mine, other, terms, received, rows, qk_gain, wk, wv, levels, entry, step_size):
    half, depth = mine.shape
    width = wk.shape[1]

    def kernel(levels_ref, entry_ref, size_ref, mine_ref, other_ref, term_mine, term_other, their_own, their_mine, rows_ref, gain_ref, wk_ref, wv_ref, state_ref, whole, out_ref):
        slot = slot_of(step - 1)
        fresh = slot_of(step) == entry_ref[step - 1]
        size = size_ref[levels_ref[slot]]
        scale_row, shift_row = rows_ref[step, 0:1, :], rows_ref[step, 1:2, :]

        def moved(state, term_a, term_b, noise):
            velocity = term_a[...].astype(F32) + term_b[...].astype(F32)
            updated = (state[...].astype(F32) + size * velocity).astype(BF16)
            return jnp.where(fresh, noise[...], updated)

        new = moved(mine_ref, term_mine, their_mine, term_mine)
        state_ref[...] = new
        whole[:half, :] = modulated_rows(new.astype(F32), scale_row, shift_row)
        new = moved(other_ref, term_other, their_own, their_own)
        whole[half:, :] = modulated_rows(new.astype(F32), scale_row, shift_row)
        project(step, whole, gain_ref, wk_ref, wv_ref, out_ref)

    return pl.pallas_call(
        kernel,
        out_shape=(
            jax.ShapeDtypeStruct((half, depth), BF16),
            jax.ShapeDtypeStruct((2 * half, depth), BF16),
            jax.ShapeDtypeStruct((2, 2 * half, width), BF16),
        ),
        in_specs=[SMEM] * 3 + [VMEM] * 10,
        out_specs=(VMEM,) * 3,
        compiler_params=params(8),
    )(levels, entry, step_size, mine, other, *terms, *received, rows, qk_gain, wk, wv)


def queries(step, whole, qk_gain, wq, pattern):
    tokens = whole.shape[0]
    width = wq.shape[1]
    scale = math.log2(math.e) / math.sqrt(HD)

    def kernel(pattern_ref, gain_ref, whole_ref, wq_ref, out_ref, bias_ref):
        window_bias(pattern_ref, bias_ref, slot_of(step), tokens // FRAMES)
        gain = jnp.concatenate([gain_ref[0:1, :] * scale] * (BLOCK // HD), axis=1)
        for block in range(width // BLOCK):
            columns = slice(block * BLOCK, (block + 1) * BLOCK)
            query = jnp.dot(whole_ref[...], wq_ref[:, columns], preferred_element_type=F32)
            out_ref[:, columns] = head_normed(query, gain).astype(BF16)

    return pl.pallas_call(
        kernel,
        out_shape=(
            jax.ShapeDtypeStruct((tokens, width), BF16),
            jax.ShapeDtypeStruct((3, tokens, LANES), BF16),
        ),
        in_specs=[SMEM, VMEM, VMEM, VMEM],
        out_specs=(VMEM, VMEM),
        compiler_params=params(8),
    )(pattern, qk_gain, whole, wq)


def attend_project(step, query, bias, before, own, after, wo, fresh_noise, entry):
    tokens, width = query.shape
    half = tokens // 2
    out_width = wo.shape[1]
    last = step == ITERS - 1

    def kernel(entry_ref, query_ref, bias_ref, before_ref, own_ref, after_ref, wo_ref, noise_ref, keep_ref, send_ref, attended, sem):
        lane = lax.broadcasted_iota(jnp.int32, (tokens, LANES), 1)
        frame = lax.broadcasted_iota(jnp.int32, (tokens, LANES), 0) // (tokens // FRAMES)
        frame_of = (lane == frame).astype(BF16)
        first = lane < HD
        ones = jnp.ones((tokens, LANES), BF16)
        for pair in range(width // LANES):
            columns = slice(pair * LANES, (pair + 1) * LANES)
            query_pair = query_ref[:, columns]
            outs = []
            for which in (first, jnp.logical_not(first)):
                one = jnp.where(which, query_pair, jnp.zeros_like(query_pair))
                one = jnp.concatenate([one, frame_of], axis=1)
                both = None
                for i, ref in enumerate((before_ref, own_ref, after_ref)):
                    key = jnp.concatenate([ref[0, :, columns], bias_ref[i]], axis=1)
                    value = jnp.concatenate([ref[1, :, columns], ones], axis=1)
                    scores = lax.dot_general(one, key, (((1,), (1,)), ((), ())), preferred_element_type=F32)
                    weights = jnp.exp2(scores).astype(BF16)
                    part = jnp.dot(weights, value, preferred_element_type=F32)
                    both = part if both is None else both + part
                outs.append(both[:, :LANES] / both[:, LANES:])
            attended[:, columns] = jnp.where(first, outs[0], outs[1]).astype(BF16)
        for block in range(out_width // OUT_BLOCK):
            columns = slice(block * OUT_BLOCK, (block + 1) * OUT_BLOCK)
            term = jnp.dot(attended[...], wo_ref[:, columns], preferred_element_type=F32).astype(BF16)
            keep_ref[:, columns] = term[:half]
            send_ref[:, columns] = term[half:]
        if not last:

            @pl.when(slot_of(step + 1) == entry_ref[step])
            def _():
                copy = pltpu.make_async_copy(noise_ref.at[step], keep_ref, sem)
                copy.start()
                copy.wait()

    out = jax.ShapeDtypeStruct((half, out_width), BF16)
    return pl.pallas_call(
        kernel,
        out_shape=(out, out),
        in_specs=[SMEM, VMEM, VMEM, VMEM, VMEM, VMEM, VMEM, HBM],
        out_specs=(VMEM, VMEM),
        scratch_shapes=[pltpu.VMEM((tokens, width), BF16), pltpu.SemaphoreType.DMA(())],
        compiler_params=params(8),
    )(entry, query, bias, before, own, after, wo, *in_hbm(fresh_noise))


def last_update(state, kept, received, fresh_noise, levels, entry, step_size):
    step = ITERS - 1

    def kernel(levels_ref, entry_ref, size_ref, state_ref, kept_ref, received_ref, noise_ref, out_ref, sem):
        velocity = kept_ref[...].astype(F32) + received_ref[...].astype(F32)
        size = size_ref[levels_ref[slot_of(step)]]
        out_ref[...] = (state_ref[...].astype(F32) + size * velocity).astype(BF16)

        @pl.when(slot_of(step + 1) == entry_ref[step])
        def _():
            copy = pltpu.make_async_copy(noise_ref.at[step], out_ref, sem)
            copy.start()
            copy.wait()

    return pl.pallas_call(
        kernel,
        out_shape=jax.ShapeDtypeStruct(state.shape, BF16),
        in_specs=[SMEM, SMEM, SMEM, VMEM, VMEM, VMEM, HBM],
        out_specs=VMEM,
        scratch_shapes=[pltpu.SemaphoreType.DMA(())],
        compiler_params=params(8),
    )(levels, entry, step_size, state, kept, received, *in_hbm(fresh_noise))


def on_device(
    latents, fresh_noise, levels, pattern, entry, level_scale, level_shift, step_size, qk_gain, wq, wk, wv, wo
):
    count = lax.axis_size("queue")
    mine = latents[0]
    other = swap_cores(mine)
    rows, wk, wv = prepare(levels, level_scale, level_shift, wk, wv)
    for step in range(ITERS):
        if step == 0:
            whole, own = first_keys_values(mine, other, rows, qk_gain, wk, wv)
        else:
            state, whole, own = next_keys_values(
                step, mine, other, terms, received, rows, qk_gain, wk, wv, levels, entry, step_size
            )
        links = [i for i in range(count) if (i + step) % count != count - 1]
        before = lax.ppermute(own, "queue", [(i, (i + 1) % count) for i in links])
        after = lax.ppermute(own, "queue", [((i + 1) % count, i) for i in links])
        query, bias = queries(step, whole, qk_gain, wq, pattern)
        terms = attend_project(step, query, bias, before, own, after, wo, fresh_noise, entry)
        if step < ITERS - 1:
            received = [swap_cores(term) for term in terms]
    state = last_update(state, terms[0], swap_cores(terms[1]), fresh_noise, levels, entry, step_size)
    route = [(i, (i + ITERS) % count) for i in range(count)]
    return lax.ppermute(state, "queue", route)[None]


def solution(mesh):
    return jax.shard_map(
        on_device,
        mesh=mesh,
        in_specs=(
            P("queue", "seq", None),
            P(None, "seq", None),
            P(),
            P(),
            P(),
            P(),
            P(),
            P(),
            P(),
            P(None, "seq"),
            P(None, "seq"),
            P(None, "seq"),
            P("seq", None),
        ),
        out_specs=P("queue", "seq", None),
        check_vma=False,
    )
```

time: 140 us -> 121 us (0.86)
  local copies, waits for them, and re-layouts: 18.8 us -> 0.94 us
  waiting for transfers between devices: 72.2 us -> 62.6 us
  starting transfers between devices: 17.4 us -> 25.4 us
    unnamed x65 -> x21, local copies, waits for them, and re-layouts: 18.8 us -> 0.94 us
    ppermute x4, starting transfers between devices: 10.1 us -> 19 us  [the longest x2 13 us: on_device(): after = lax.ppermute(own, 'queue', [((i + 1) % count, i) for i in links])]
    ppermute x4, waiting for transfers between devices: 40.1 us -> 33.5 us  [the longest x2 23.4 us: on_device(): after = lax.ppermute(own, 'queue', [((i + 1) % count, i) for i in links])]
    ppermute x4, waiting for transfers between devices: 7.65 us -> 4.67 us  [swap_cores(): return lax.ppermute(block, 'seq', [(0, 1), (1, 0)])]
    pallas_call x7 -> x6, Pallas kernels: 20.3 us -> 22.2 us  [the longest x2 6.84 us: queries(): pl.pallas_call(kernel, out_shape=(jax.ShapeDtypeStruct((tokens, width), B...]
  transfers between devices with their start and end apart: 9 -> 9, of which waited for: 9 -> 8; matrix products, arithmetic and copies ran while one was open for 0% -> 0% of each run, Pallas kernels for 4% -> 9%
where the time goes in v3:
time: 121 us
  waiting for transfers between devices  62.6 us (52%)
  Pallas kernels  31.6 us (26%)
  starting transfers between devices  25.4 us (21%)
    ppermute x1, waiting for transfers between devices, on_device(): return lax.ppermute(state, 'queue', route)[None]  24.5 us
    ppermute x2, waiting for transfers between devices, on_device(): after = lax.ppermute(own, 'queue', [((i + 1) % count, i) for i in links])  23.4 us
    ppermute x2, starting transfers between devices, on_device(): after = lax.ppermute(own, 'queue', [((i + 1) % count, i) for i in links])  13 us
    ppermute x2, waiting for transfers between devices, on_device(): before = lax.ppermute(own, 'queue', [(i, (i + 1) % count) for i in links])  10.1 us
    pallas_call x2, Pallas kernels, attend_project(): pl.pallas_call(kernel, out_shape=(out, out), in_specs=[SMEM, VMEM, VMEM,...  9.38 us
    pallas_call x2, Pallas kernels, queries(): pl.pallas_call(kernel, out_shape=(jax.ShapeDtypeStruct((tokens, width), B...  6.84 us
    ppermute x4, starting transfers between devices, swap_cores(): return lax.ppermute(block, 'seq', [(0, 1), (1, 0)])  6.34 us
    ppermute x2, starting transfers between devices, on_device(): before = lax.ppermute(own, 'queue', [(i, (i + 1) % count) for i in links])  5.96 us
  transfers between devices with their start and end apart: 9, of which 8 were waited for; matrix products, arithmetic and copies ran while one was open for 0% of the time, Pallas kernels for 9%

profile of v3, /device:TPU:1, one launch (start us, length us, event | category | flops | bytes accessed | tf_op | source)
XLA Modules:
  0.0 120.8 jit_solution(5056377711798242329)
XLA Ops:
  0.0 3.2 %collective-permute-start = (bf16[128,3072]{1,0:T(8,128)(2,1)}, bf16[128,3072]{1,0:T(8,128)(2,1)S(1)}, u32[]{:S(2)}, u32[]{:S(2)}) collective-permute-start(bf16[128,3072]{1,0:T(8,128)(2,1)} %bitcast.6), channel_id=1, source_target_pairs={{0,1},{1,0},{2,3},{3,2},{4,5},{5,4},{6,7},{7,6},{8,9},{9,8},{10,11... | collective-permute-start | bytes 2359304 | tf_op jit(solution)/shard_map/ppermute | solution.py:28
  3.2 4.3 %shard_map.127 = (f32[2,2,3072]{2,1,0:T(2,128)S(1)}, bf16[3072,768]{1,0:T(8,128)(2,1)S(1)}, bf16[3072,768]{1,0:T(8,128)(2,1)S(1)}) custom-call(s32[128]{0:T(128)} %levels_ref.5, f32[50,3072]{1,0:T(8,128)} %scale_ref.1, f32[50,3072]{1,0:T(8,128)} %shift_ref.1, bf16[3072,768]{1,0:T(8,128)(2,1)} %wk_ref.1, bf16[3072,768]{1,0:T(8,128)(2,1)} %wv_ref.1), custom_call_target="tpu_custom_call" | custom-call | tf_op jit(solution)/shard_map/pallas_call | solution.py:106
  7.6 0.0 slice-start.2
  7.6 0.0 slice-start.1
  7.6 0.0 copy-start.2
  7.6 4.5 %shard_map.128 = (bf16[256,3072]{1,0:T(8,128)(2,1)S(1)}, bf16[2,256,768]{2,1,0:T(8,128)(2,1)S(1)}) custom-call(bf16[128,3072]{1,0:T(8,128)(2,1)S(1)} %bitcast.7, bf16[128,3072]{1,0:T(8,128)(2,1)S(1)} %collective-permute-done.other_ref, f32[2,2,3072]{2,1,0:T(2,128)S(1)} %get-tuple-element.21.rows_ref, f32[2,64]{1,0:T(2,128)S(1)} %copy-done.1, ...), custom_call_target="tpu_custom_call" | custom-call | tf_op jit(solution)/shard_map/pallas_call | solution.py:145
  12.1 0.0 copy-start.3
  12.1 1.3 %collective-permute-start.2 = (bf16[2,256,768]{2,1,0:T(8,128)(2,1)S(1)}, bf16[2,256,768]{2,1,0:T(8,128)(2,1)S(1)}, u32[]{:S(2)}, u32[]{:S(2)}) collective-permute-start(bf16[2,256,768]{2,1,0:T(8,128)(2,1)S(1)} %get-tuple-element.27.own_ref), channel_id=1, source_target_pairs={{2,0},{4,2},{6,4},{8,6},{10,8},{12,10},{14,12},{16,14},{18,16},{20... | collective-permute-start | bytes 2359304 | tf_op jit(solution)/shard_map/ppermute | solution.py:310
  13.4 4.0 %collective-permute-start.1 = (bf16[2,256,768]{2,1,0:T(8,128)(2,1)S(1)}, bf16[2,256,768]{2,1,0:T(8,128)(2,1)S(1)}, u32[]{:S(2)}, u32[]{:S(2)}) collective-permute-start(bf16[2,256,768]{2,1,0:T(8,128)(2,1)S(1)} %get-tuple-element.27.own_ref), channel_id=1, source_target_pairs={{0,2},{2,4},{4,6},{6,8},{8,10},{10,12},{12,14},{14,16},{16,18},{18... | collective-permute-start | bytes 2359304 | tf_op jit(solution)/shard_map/ppermute | solution.py:309
  17.5 3.4 %shard_map.129 = (bf16[256,768]{1,0:T(8,128)(2,1)S(1)}, bf16[3,256,128]{2,1,0:T(8,128)(2,1)S(1)}) custom-call(s32[4,12]{1,0:T(4,128)S(1)} %copy-done.2, f32[2,64]{1,0:T(2,128)S(1)} %copy-done.1, bf16[256,3072]{1,0:T(8,128)(2,1)S(1)} %get-tuple-element.24.whole_ref, bf16[3072,768]{1,0:T(8,128)(2,1)S(1)} %bitcast.3), custom_call_target="tpu_custom_call" | custom-call | tf_op jit(solution)/shard_map/pallas_call | solution.py:205
  20.9 0.0 copy-start.4
  21.0 0.0 copy-start.5
  21.0 12.2 %collective-permute-done.2.after_ref = bf16[2,256,768]{2,1,0:T(8,128)(2,1)S(1)} collective-permute-done((bf16[2,256,768]{2,1,0:T(8,128)(2,1)S(1)}, bf16[2,256,768]{2,1,0:T(8,128)(2,1)S(1)}, u32[]{:S(2)}, u32[]{:S(2)}) %collective-permute-start.2) | collective-permute-done | bytes 786464 | tf_op jit(solution)/shard_map/ppermute | solution.py:310
  33.2 0.9 collective-permute-done.1.before_ref
  34.1 4.7 %shard_map.130 = (bf16[128,3072]{1,0:T(8,128)(2,1)S(1)}, bf16[128,3072]{1,0:T(8,128)(2,1)S(1)}) custom-call(s32[2]{0:T(128)S(1)} %copy-done.3, bf16[256,768]{1,0:T(8,128)(2,1)S(1)} %get-tuple-element.25.query_ref, bf16[3,256,128]{2,1,0:T(8,128)(2,1)S(1)} %get-tuple-element.26.bias_ref, bf16[2,256,768]{2,1,0:T(8,128)(2,1)S(1)} %collective-permute-done.1.before_ref, ...), custom_call_target="tpu_custom_call" | custom-call | tf_op jit(solution)/shard_map/pallas_call | solution.py:260
  38.7 1.2 collective-permute-start.3
  39.9 0.3 collective-permute-start.4
  40.2 1.6 %collective-permute-done.3.their_own = bf16[128,3072]{1,0:T(8,128)(2,1)S(1)} collective-permute-done((bf16[128,3072]{1,0:T(8,128)(2,1)S(1)}, bf16[128,3072]{1,0:T(8,128)(2,1)S(1)}, u32[]{:S(2)}, u32[]{:S(2)}) %collective-permute-start.3) | collective-permute-done | bytes 786464 | tf_op jit(solution)/shard_map/ppermute | solution.py:28
  41.9 1.1 collective-permute-done.4.their_mine
  43.0 5.7 %shard_map.131 = (bf16[128,3072]{1,0:T(8,128)(2,1)S(1)}, bf16[256,3072]{1,0:T(8,128)(2,1)S(1)}, bf16[2,256,768]{2,1,0:T(8,128)(2,1)S(1)}) custom-call(s32[128]{0:T(128)S(1)} %copy-done.4, s32[2]{0:T(128)S(1)} %copy-done.3, f32[50]{0:T(128)S(1)} %copy-done.5, bf16[128,3072]{1,0:T(8,128)(2,1)S(1)} %bitcast.8, ...), custom_call_target="tpu_custom_call" | custom-call | tf_op jit(solution)/shard_map/pallas_call | solution.py:179
  48.7 11.7 %collective-permute-start.6 = (bf16[2,256,768]{2,1,0:T(8,128)(2,1)S(1)}, bf16[2,256,768]{2,1,0:T(8,128)(2,1)S(1)}, u32[]{:S(2)}, u32[]{:S(2)}) collective-permute-start(bf16[2,256,768]{2,1,0:T(8,128)(2,1)S(1)} %get-tuple-element.34.own_ref), channel_id=1, source_target_pairs={{2,0},{4,2},{6,4},{8,6},{10,8},{12,10},{14,12},{16,14},{18,16},{20... | collective-permute-start | bytes 2359304 | tf_op jit(solution)/shard_map/ppermute | solution.py:310
  60.4 1.9 %collective-permute-start.5 = (bf16[2,256,768]{2,1,0:T(8,128)(2,1)S(1)}, bf16[2,256,768]{2,1,0:T(8,128)(2,1)S(1)}, u32[]{:S(2)}, u32[]{:S(2)}) collective-permute-start(bf16[2,256,768]{2,1,0:T(8,128)(2,1)S(1)} %get-tuple-element.34.own_ref), channel_id=1, source_target_pairs={{0,2},{2,4},{4,6},{6,8},{8,10},{10,12},{12,14},{14,16},{16,18},{18... | collective-permute-start | bytes 2359304 | tf_op jit(solution)/shard_map/ppermute | solution.py:309
  62.4 3.4 %shard_map.132 = (bf16[256,768]{1,0:T(8,128)(2,1)S(1)}, bf16[3,256,128]{2,1,0:T(8,128)(2,1)S(1)}) custom-call(s32[4,12]{1,0:T(4,128)S(1)} %copy-done.2, f32[2,64]{1,0:T(2,128)S(1)} %copy-done.1, bf16[256,3072]{1,0:T(8,128)(2,1)S(1)} %get-tuple-element.31.whole_ref, bf16[3072,768]{1,0:T(8,128)(2,1)S(1)} %bitcast.3), custom_call_target="tpu_custom_call" | custom-call | tf_op jit(solution)/shard_map/pallas_call | solution.py:205
  65.8 11.2 %collective-permute-done.6.after_ref = bf16[2,256,768]{2,1,0:T(8,128)(2,1)S(1)} collective-permute-done((bf16[2,256,768]{2,1,0:T(8,128)(2,1)S(1)}, bf16[2,256,768]{2,1,0:T(8,128)(2,1)S(1)}, u32[]{:S(2)}, u32[]{:S(2)}) %collective-permute-start.6) | collective-permute-done | bytes 786464 | tf_op jit(solution)/shard_map/ppermute | solution.py:310
  77.0 9.2 %collective-permute-done.5.before_ref = bf16[2,256,768]{2,1,0:T(8,128)(2,1)S(1)} collective-permute-done((bf16[2,256,768]{2,1,0:T(8,128)(2,1)S(1)}, bf16[2,256,768]{2,1,0:T(8,128)(2,1)S(1)}, u32[]{:S(2)}, u32[]{:S(2)}) %collective-permute-start.5) | collective-permute-done | bytes 786464 | tf_op jit(solution)/shard_map/ppermute | solution.py:309
  86.2 4.7 %shard_map.133 = (bf16[128,3072]{1,0:T(8,128)(2,1)S(1)}, bf16[128,3072]{1,0:T(8,128)(2,1)S(1)}) custom-call(s32[2]{0:T(128)S(1)} %copy-done.3, bf16[256,768]{1,0:T(8,128)(2,1)S(1)} %get-tuple-element.32.query_ref, bf16[3,256,128]{2,1,0:T(8,128)(2,1)S(1)} %get-tuple-element.33.bias_ref, bf16[2,256,768]{2,1,0:T(8,128)(2,1)S(1)} %collective-permute-done.5.before_ref, ...), custom_call_target="tpu_custom_call" | custom-call | tf_op jit(solution)/shard_map/pallas_call | solution.py:260
  90.9 1.6 %collective-permute-start.7 = (bf16[128,3072]{1,0:T(8,128)(2,1)S(1)}, bf16[128,3072]{1,0:T(8,128)(2,1)S(1)}, u32[]{:S(2)}, u32[]{:S(2)}) collective-permute-start(bf16[128,3072]{1,0:T(8,128)(2,1)S(1)} %get-tuple-element.36), channel_id=1, source_target_pairs={{0,1},{1,0},{2,3},{3,2},{4,5},{5,4},{6,7},{7,6},{8,9},{9,8},{10,11... | collective-permute-start | bytes 2359304 | tf_op jit(solution)/shard_map/ppermute | solution.py:28
  92.5 1.9 %collective-permute-done.7.received_ref = bf16[128,3072]{1,0:T(8,128)(2,1)S(1)} collective-permute-done((bf16[128,3072]{1,0:T(8,128)(2,1)S(1)}, bf16[128,3072]{1,0:T(8,128)(2,1)S(1)}, u32[]{:S(2)}, u32[]{:S(2)}) %collective-permute-start.7) | collective-permute-done | bytes 786464 | tf_op jit(solution)/shard_map/ppermute | solution.py:28
  94.4 0.9 shard_map.134
  95.3 0.1 collective-permute-start.8
  95.4 24.5 %collective-permute-done.8 = bf16[128,3072]{1,0:T(8,128)(2,1)S(1)} collective-permute-done((bf16[128,3072]{1,0:T(8,128)(2,1)S(1)}, bf16[128,3072]{1,0:T(8,128)(2,1)S(1)}, u32[]{:S(2)}, u32[]{:S(2)}) %collective-permute-start.8) | collective-permute-done | bytes 786464 | tf_op jit(solution)/shard_map/ppermute | solution.py:317
  119.9 0.9 copy.15
  (17 shorter events, 0.0 us)
Async XLA Ops:
  0.0 7.6 %copy-start = (bf16[1,128,3072]{2,1,0:T(8,128)(2,1)S(1)}, bf16[1,128,3072]{2,1,0:T(8,128)(2,1)}, u32[]{:S(2)}) copy-start(bf16[1,128,3072]{2,1,0:T(8,128)(2,1)} %param.13) | copy-start | bytes 2359300
  0.0 7.6 %copy-start.1 = (f32[2,64]{1,0:T(2,128)S(1)}, f32[2,64]{1,0:T(2,128)}, u32[]{:S(2)}) copy-start(f32[2,64]{1,0:T(2,128)} %gain_ref.7) | copy-start | bytes 1540
  0.0 7.6 %collective-permute-start = (bf16[128,3072]{1,0:T(8,128)(2,1)}, bf16[128,3072]{1,0:T(8,128)(2,1)S(1)}, u32[]{:S(2)}, u32[]{:S(2)}) collective-permute-start(bf16[128,3072]{1,0:T(8,128)(2,1)} %bitcast.6), channel_id=1, source_target_pairs={{0,1},{1,0},{2,3},{3,2},{4,5},{5,4},{6,7},{7,6},{8,9},{9,8},{10,11... | collective-permute-start | bytes 2359304 | tf_op jit(solution)/shard_map/ppermute | solution.py:28
  3.2 14.2 %slice-start = ((s8[4718592]{0:T(1024)(128)(4,1)}), s8[4194304]{0:T(1024)(128)(4,1)S(1)}, s32[]{:S(2)}) async-start(s8[4718592]{0:T(1024)(128)(4,1)} %bitcast.2), calls=%async_computation | async-start | bytes 8388608
  7.6 26.5 %slice-start.2 = ((s8[4718592]{0:T(1024)(128)(4,1)}), s8[4194304]{0:T(1024)(128)(4,1)S(1)}, s32[]{:S(2)}) async-start(s8[4718592]{0:T(1024)(128)(4,1)} %bitcast.4), calls=%async_computation.2 | async-start | bytes 8388608
  7.6 9.9 %slice-start.1 = ((s8[4718592]{0:T(1024)(128)(4,1)}), s8[524288]{0:T(1024)(128)(4,1)S(1)}, s32[]{:S(2)}) async-start(s8[4718592]{0:T(1024)(128)(4,1)} %bitcast.2), calls=%async_computation.1 | async-start | bytes 1048576
  7.6 9.9 %copy-start.2 = (s32[4,12]{1,0:T(4,128)S(1)}, s32[4,12]{1,0:T(4,128)}, u32[]{:S(2)}) copy-start(s32[4,12]{1,0:T(4,128)} %pattern_ref.3) | copy-start | bytes 580
  7.6 26.4 %slice-start.3 = ((s8[4718592]{0:T(1024)(128)(4,1)}), s8[524288]{0:T(1024)(128)(4,1)S(1)}, s32[]{:S(2)}) async-start(s8[4718592]{0:T(1024)(128)(4,1)} %bitcast.4), calls=%async_computation.3 | async-start | bytes 1048576
  12.1 21.9 %copy-start.3 = (s32[2]{0:T(128)S(1)}, s32[2]{0:T(128)}, u32[]{:S(2)}) copy-start(s32[2]{0:T(128)} %entry_ref.7) | copy-start | bytes 28
  12.1 21.1 %collective-permute-start.2 = (bf16[2,256,768]{2,1,0:T(8,128)(2,1)S(1)}, bf16[2,256,768]{2,1,0:T(8,128)(2,1)S(1)}, u32[]{:S(2)}, u32[]{:S(2)}) collective-permute-start(bf16[2,256,768]{2,1,0:T(8,128)(2,1)S(1)} %get-tuple-element.27.own_ref), channel_id=1, source_target_pairs={{2,0},{4,2},{6,4},{8,6},{10,8},{12,10},{14,12},{16,14},{18,16},{20... | collective-permute-start | bytes 2359304 | tf_op jit(solution)/shard_map/ppermute | solution.py:310
  13.4 20.6 %collective-permute-start.1 = (bf16[2,256,768]{2,1,0:T(8,128)(2,1)S(1)}, bf16[2,256,768]{2,1,0:T(8,128)(2,1)S(1)}, u32[]{:S(2)}, u32[]{:S(2)}) collective-permute-start(bf16[2,256,768]{2,1,0:T(8,128)(2,1)S(1)} %get-tuple-element.27.own_ref), channel_id=1, source_target_pairs={{0,2},{2,4},{4,6},{6,8},{8,10},{10,12},{12,14},{14,16},{16,18},{18... | collective-permute-start | bytes 2359304 | tf_op jit(solution)/shard_map/ppermute | solution.py:309
  20.9 22.0 %copy-start.4 = (s32[128]{0:T(128)S(1)}, s32[128]{0:T(128)}, u32[]{:S(2)}) copy-start(s32[128]{0:T(128)} %levels_ref.5) | copy-start | bytes 1540
  21.0 22.0 %copy-start.5 = (f32[50]{0:T(128)S(1)}, f32[50]{0:T(128)}, u32[]{:S(2)}) copy-start(f32[50]{0:T(128)} %size_ref.3) | copy-start | bytes 604
  38.7 3.1 %collective-permute-start.3 = (bf16[128,3072]{1,0:T(8,128)(2,1)S(1)}, bf16[128,3072]{1,0:T(8,128)(2,1)S(1)}, u32[]{:S(2)}, u32[]{:S(2)}) collective-permute-start(bf16[128,3072]{1,0:T(8,128)(2,1)S(1)} %get-tuple-element.28.term_mine), channel_id=1, source_target_pairs={{0,1},{1,0},{2,3},{3,2},{4,5},{5,4},{6,7},{7,6},{8,9},{9,8},{10,11... | collective-permute-start | bytes 2359304 | tf_op jit(solution)/shard_map/ppermute | solution.py:28
  39.9 3.0 %collective-permute-start.4 = (bf16[128,3072]{1,0:T(8,128)(2,1)S(1)}, bf16[128,3072]{1,0:T(8,128)(2,1)S(1)}, u32[]{:S(2)}, u32[]{:S(2)}) collective-permute-start(bf16[128,3072]{1,0:T(8,128)(2,1)S(1)} %get-tuple-element.29.term_other), channel_id=1, source_target_pairs={{0,1},{1,0},{2,3},{3,2},{4,5},{5,4},{6,7},{7,6},{8,9},{9,8},{10,11... | collective-permute-start | bytes 2359304 | tf_op jit(solution)/shard_map/ppermute | solution.py:28
  48.7 28.3 %collective-permute-start.6 = (bf16[2,256,768]{2,1,0:T(8,128)(2,1)S(1)}, bf16[2,256,768]{2,1,0:T(8,128)(2,1)S(1)}, u32[]{:S(2)}, u32[]{:S(2)}) collective-permute-start(bf16[2,256,768]{2,1,0:T(8,128)(2,1)S(1)} %get-tuple-element.34.own_ref), channel_id=1, source_target_pairs={{2,0},{4,2},{6,4},{8,6},{10,8},{12,10},{14,12},{16,14},{18,16},{20... | collective-permute-start | bytes 2359304 | tf_op jit(solution)/shard_map/ppermute | solution.py:310
  60.4 25.7 %collective-permute-start.5 = (bf16[2,256,768]{2,1,0:T(8,128)(2,1)S(1)}, bf16[2,256,768]{2,1,0:T(8,128)(2,1)S(1)}, u32[]{:S(2)}, u32[]{:S(2)}) collective-permute-start(bf16[2,256,768]{2,1,0:T(8,128)(2,1)S(1)} %get-tuple-element.34.own_ref), channel_id=1, source_target_pairs={{0,2},{2,4},{4,6},{6,8},{8,10},{10,12},{12,14},{14,16},{16,18},{18... | collective-permute-start | bytes 2359304 | tf_op jit(solution)/shard_map/ppermute | solution.py:309
  90.9 3.5 %collective-permute-start.7 = (bf16[128,3072]{1,0:T(8,128)(2,1)S(1)}, bf16[128,3072]{1,0:T(8,128)(2,1)S(1)}, u32[]{:S(2)}, u32[]{:S(2)}) collective-permute-start(bf16[128,3072]{1,0:T(8,128)(2,1)S(1)} %get-tuple-element.36), channel_id=1, source_target_pairs={{0,1},{1,0},{2,3},{3,2},{4,5},{5,4},{6,7},{7,6},{8,9},{9,8},{10,11... | collective-permute-start | bytes 2359304 | tf_op jit(solution)/shard_map/ppermute | solution.py:28
  95.3 24.6 %collective-permute-start.8 = (bf16[128,3072]{1,0:T(8,128)(2,1)S(1)}, bf16[128,3072]{1,0:T(8,128)(2,1)S(1)}, u32[]{:S(2)}, u32[]{:S(2)}) collective-permute-start(bf16[128,3072]{1,0:T(8,128)(2,1)S(1)} %shard_map.134), channel_id=1, source_target_pairs={{0,4},{2,6},{4,8},{6,10},{8,12},{10,14},{12,16},{14,18},{16,20},{1... | collective-permute-start | bytes 2359304 | tf_op jit(solution)/shard_map/ppermute | solution.py:317

commit v4 on v3

v4 whole, which is shorter than its diff:
```python
import math

import jax
import jax.numpy as jnp
from jax import lax
from jax.experimental import pallas as pl
from jax.experimental.pallas import tpu as pltpu
from jax.sharding import PartitionSpec as P

HD = 64
FRAMES = 4
ITERS = 2
LANES = 128
EPS = 1e-06
CLOSED = -30000.0
BLOCK = 256
OUT_BLOCK = 768
UNITS = 3
CHUNKS = ((0, 1), (2,))
LAST_COLUMNS = 2
MIB = 1 << 20
F32 = jnp.float32
BF16 = jnp.bfloat16

SMEM = pl.BlockSpec(memory_space=pltpu.SMEM)
VMEM = pl.BlockSpec(memory_space=pltpu.VMEM)
HBM = pl.BlockSpec(memory_space=pltpu.HBM)


def swap_cores(block):
    return lax.ppermute(block, "seq", [(0, 1), (1, 0)])


def in_hbm(*arrays):
    return tuple(pltpu.with_memory_space_constraint(array, pltpu.HBM) for array in arrays)


def params(mib):
    return pltpu.CompilerParams(vmem_limit_bytes=mib * MIB)


def slot_of(step):
    return lax.rem(lax.axis_index("queue") + step, lax.axis_size("queue"))


def modulated_rows(values, scale_row, shift_row):
    normed = values * lax.rsqrt(jnp.mean(values * values, axis=-1, keepdims=True) + EPS)
    return (normed * scale_row + shift_row).astype(BF16)


def head_normed(values, gain_row):
    width = values.shape[1]
    squares = values * values
    high = squares.astype(BF16)
    low = (squares - high.astype(F32)).astype(BF16)
    row = lax.broadcasted_iota(jnp.int32, (width, width), 0)
    column = lax.broadcasted_iota(jnp.int32, (width, width), 1)
    same = (row // HD == column // HD).astype(BF16)
    sums = jnp.dot(high, same, preferred_element_type=F32) + jnp.dot(low, same, preferred_element_type=F32)
    return values * lax.rsqrt(sums * (1.0 / HD) + EPS) * gain_row


def window_bias(pattern_ref, bias_ref, slot, frame_rows):
    count, core = lax.axis_size("queue"), lax.axis_index("seq")
    odd = lax.rem(lax.axis_index("queue"), 2)
    lane = lax.broadcasted_iota(jnp.int32, (1, LANES), 1)
    half = FRAMES // 2
    for i, block in enumerate((1, 2 - 2 * odd, 2 * odd)):
        absent = slot == jnp.where(block == 0, 0, count - 1)
        for at in range(FRAMES):
            key_frame = lax.rem(at + half * core, FRAMES)
            row = jnp.zeros((1, LANES), F32)
            for f in range(FRAMES):
                if i == 0 and f == at:
                    continue
                closed = pattern_ref[lax.rem(f + half * core, FRAMES), block * FRAMES + key_frame] != 1
                if i > 0:
                    closed = jnp.logical_or(closed, absent)
                row = row + jnp.where(lane == f, jnp.where(closed, CLOSED, 0.0), 0.0)
            first = at * frame_rows
            bias_ref[i, first : first + frame_rows, :] = jnp.broadcast_to(row, (frame_rows, LANES)).astype(BF16)


def weight_copies(wk_ref, wv_ref, chunk, out_ref, sems):
    width = out_ref.shape[2]
    columns = pl.ds(chunk * width, width)
    return [
        pltpu.make_async_copy(ref.at[:, columns], out_ref.at[i], sems.at[i]) for i, ref in enumerate((wk_ref, wv_ref))
    ]


def weight_shape(wk):
    return jax.ShapeDtypeStruct((2, wk.shape[0], wk.shape[1] // UNITS), BF16)


def prepare(levels, level_scale, level_shift, wk, wv):
    depth = level_scale.shape[1]

    def kernel(levels_ref, scale_ref, shift_ref, wk_ref, wv_ref, rows_ref, weights_ref, held, levels_sm, sems, weight_sems):
        first = pltpu.make_async_copy(levels_ref, levels_sm, sems.at[0])
        first.start()
        tables = [
            pltpu.make_async_copy(scale_ref, held.at[0], sems.at[1]),
            pltpu.make_async_copy(shift_ref, held.at[1], sems.at[2]),
        ]
        weights = weight_copies(wk_ref, wv_ref, 0, weights_ref, weight_sems)
        for copy in tables + weights:
            copy.start()
        for copy in [first] + tables:
            copy.wait()
        for step in range(ITERS):
            row = pl.ds(levels_sm[slot_of(step)], 1)
            rows_ref[step, 0:1, :] = 1.0 + held[0, row, :]
            rows_ref[step, 1:2, :] = held[1, row, :]
        for copy in weights:
            copy.wait()

    return pl.pallas_call(
        kernel,
        out_shape=(jax.ShapeDtypeStruct((ITERS, 2, depth), F32), weight_shape(wk)),
        in_specs=[HBM] * 5,
        out_specs=(VMEM, VMEM),
        scratch_shapes=[
            pltpu.VMEM((2, *level_scale.shape), F32),
            pltpu.SMEM(levels.shape, jnp.int32),
            pltpu.SemaphoreType.DMA((3,)),
            pltpu.SemaphoreType.DMA((2,)),
        ],
        compiler_params=params(8),
    )(*in_hbm(levels, level_scale, level_shift, wk, wv))


def project(whole, gain_ref, weights_refs, out_ref):
    for i, weights_ref in enumerate(weights_refs):
        width = weights_ref.shape[2]
        columns = slice(i * width, (i + 1) * width)
        keys = jnp.dot(whole[...], weights_ref[0], preferred_element_type=F32)
        gain = jnp.concatenate([gain_ref[1:2, :]] * (width // HD), axis=1)
        out_ref[0, :, columns] = head_normed(keys, gain).astype(BF16)
        out_ref[1, :, columns] = jnp.dot(whole[...], weights_ref[1], preferred_element_type=F32).astype(BF16)


def first_modulated(mine, other, rows, qk_gain, weights, wk, wv):
    half, depth = mine.shape
    unit = weights.shape[2]
    chunk = CHUNKS[0]

    def kernel(mine_ref, other_ref, rows_ref, gain_ref, weights_ref, wk_ref, wv_ref, whole, out_ref, *rest):
        more, sems = rest[: UNITS - 1], rest[-1]
        copies = [weight_copies(wk_ref, wv_ref, i + 1, ref, sems.at[i]) for i, ref in enumerate(more)]
        for pair in copies:
            for copy in pair:
                copy.start()
        scale_row, shift_row = rows_ref[0, 0:1, :], rows_ref[0, 1:2, :]
        whole[:half, :] = modulated_rows(mine_ref[...].astype(F32), scale_row, shift_row)
        whole[half:, :] = modulated_rows(other_ref[...].astype(F32), scale_row, shift_row)
        project(whole, gain_ref, [weights_ref], out_ref.at[:, :, pl.ds(0, unit)])
        for i, pair in enumerate(copies):
            for copy in pair:
                copy.wait()
            if i + 1 in chunk:
                project(whole, gain_ref, [more[i]], out_ref.at[:, :, pl.ds((i + 1) * unit, unit)])

    return pl.pallas_call(
        kernel,
        out_shape=(
            jax.ShapeDtypeStruct((2 * half, depth), BF16),
            jax.ShapeDtypeStruct((2, 2 * half, unit * len(chunk)), BF16),
            *[weight_shape(wk)] * (UNITS - 1),
        ),
        in_specs=[VMEM] * 5 + [HBM] * 2,
        out_specs=(VMEM,) * (UNITS + 1),
        scratch_shapes=[pltpu.SemaphoreType.DMA((UNITS - 1, 2))],
        compiler_params=params(8),
    )(mine, other, rows, qk_gain, weights, *in_hbm(wk, wv))


def next_modulated(step, mine, other, terms, received, rows, qk_gain, weights, levels, entry, step_size):
    half, depth = mine.shape
    unit = weights[0].shape[2]
    chunk = CHUNKS[0]

    def kernel(levels_ref, entry_ref, size_ref, mine_ref, other_ref, term_mine, term_other, their_own, their_mine, rows_ref, gain_ref, *rest):
        weights_refs, (state_ref, whole, out_ref) = rest[:-3], rest[-3:]
        slot = slot_of(step - 1)
        fresh = slot_of(step) == entry_ref[step - 1]
        size = size_ref[levels_ref[slot]]
        scale_row, shift_row = rows_ref[step, 0:1, :], rows_ref[step, 1:2, :]

        def moved(state, term_a, term_b, noise):
            velocity = term_a[...].astype(F32) + term_b[...].astype(F32)
            updated = (state[...].astype(F32) + size * velocity).astype(BF16)
            return jnp.where(fresh, noise[...], updated)

        new = moved(mine_ref, term_mine, their_mine, term_mine)
        state_ref[...] = new
        whole[:half, :] = modulated_rows(new.astype(F32), scale_row, shift_row)
        new = moved(other_ref, term_other, their_own, their_own)
        whole[half:, :] = modulated_rows(new.astype(F32), scale_row, shift_row)
        project(whole, gain_ref, weights_refs, out_ref)

    return pl.pallas_call(
        kernel,
        out_shape=(
            jax.ShapeDtypeStruct((half, depth), BF16),
            jax.ShapeDtypeStruct((2 * half, depth), BF16),
            jax.ShapeDtypeStruct((2, 2 * half, unit * len(chunk)), BF16),
        ),
        in_specs=[SMEM] * 3 + [VMEM] * (8 + len(chunk)),
        out_specs=(VMEM,) * 3,
        compiler_params=params(8),
    )(levels, entry, step_size, mine, other, *terms, *received, rows, qk_gain, *[weights[i] for i in chunk])


def keys_values(whole, qk_gain, weights):
    def kernel(whole_ref, gain_ref, *rest):
        project(whole_ref, gain_ref, rest[:-1], rest[-1])

    width = sum(block.shape[2] for block in weights)
    return pl.pallas_call(
        kernel,
        out_shape=jax.ShapeDtypeStruct((2, whole.shape[0], width), BF16),
        in_specs=[VMEM] * (2 + len(weights)),
        out_specs=VMEM,
        compiler_params=params(8),
    )(whole, qk_gain, *weights)


def attention_parts(query_pair, blocks):
    tokens = query_pair.shape[0]
    lane = lax.broadcasted_iota(jnp.int32, (tokens, LANES), 1)
    frame = lax.broadcasted_iota(jnp.int32, (tokens, LANES), 0) // (tokens // FRAMES)
    frame_of = (lane == frame).astype(BF16)
    first = lane < HD
    ones = jnp.ones((tokens, LANES), BF16)
    parts = []
    for which in (first, jnp.logical_not(first)):
        one = jnp.concatenate([jnp.where(which, query_pair, jnp.zeros_like(query_pair)), frame_of], axis=1)
        both = None
        for keys, values, bias in blocks:
            scores = lax.dot_general(
                one, jnp.concatenate([keys, bias], axis=1), (((1,), (1,)), ((), ())), preferred_element_type=F32
            )
            weights = jnp.exp2(scores).astype(BF16)
            part = jnp.dot(weights, jnp.concatenate([values, ones], axis=1), preferred_element_type=F32)
            both = part if both is None else both + part
        parts.append(both)
    return (
        jnp.where(first, parts[0][:, :LANES], parts[1][:, :LANES]),
        jnp.where(first, parts[0][:, LANES:], parts[1][:, LANES:]),
    )


def queries(step, whole, qk_gain, wq, pattern, own):
    tokens = whole.shape[0]
    width = wq.shape[1]
    scale = math.log2(math.e) / math.sqrt(HD)

    def kernel(pattern_ref, gain_ref, whole_ref, wq_ref, *rest):
        own_refs, (out_ref, bias_ref, sums_ref) = rest[:-3], rest[-3:]
        window_bias(pattern_ref, bias_ref, slot_of(step), tokens // FRAMES)
        gain = jnp.concatenate([gain_ref[0:1, :] * scale] * (BLOCK // HD), axis=1)
        for block in range(width // BLOCK):
            columns = slice(block * BLOCK, (block + 1) * BLOCK)
            query = jnp.dot(whole_ref[...], wq_ref[:, columns], preferred_element_type=F32)
            out_ref[:, columns] = head_normed(query, gain).astype(BF16)
        start = 0
        for ref in own_refs:
            for first in range(0, ref.shape[2], LANES):
                at = slice(first, first + LANES)
                columns = slice(start, start + LANES)
                start += LANES
                top, bottom = attention_parts(out_ref[:, columns], [(ref[0, :, at], ref[1, :, at], bias_ref[0])])
                sums_ref[0, :, columns] = top
                sums_ref[1, :, columns] = bottom

    return pl.pallas_call(
        kernel,
        out_shape=(
            jax.ShapeDtypeStruct((tokens, width), BF16),
            jax.ShapeDtypeStruct((3, tokens, LANES), BF16),
            jax.ShapeDtypeStruct((2, tokens, width), F32),
        ),
        in_specs=[SMEM] + [VMEM] * (3 + len(own)),
        out_specs=(VMEM,) * 3,
        compiler_params=params(8),
    )(pattern, qk_gain, whole, wq, *own)


def attend_columns(start, query_ref, bias_ref, sums_ref, partner_ref, neighbour_ref, attended):
    for first in range(0, partner_ref.shape[2], LANES):
        at = slice(first, first + LANES)
        columns = slice(start + first, start + first + LANES)
        blocks = [(ref[0, :, at], ref[1, :, at], bias_ref[i + 1]) for i, ref in enumerate((partner_ref, neighbour_ref))]
        top, bottom = attention_parts(query_ref[:, columns], blocks)
        top = top + sums_ref[0, :, columns]
        bottom = bottom + sums_ref[1, :, columns]
        attended[:, columns] = (top / bottom).astype(BF16)


def attend(query, bias, sums, partner, neighbour):
    def kernel(*refs):
        attend_columns(0, *refs)

    return pl.pallas_call(
        kernel,
        out_shape=jax.ShapeDtypeStruct(query.shape, BF16),
        in_specs=[VMEM] * 5,
        out_specs=VMEM,
        compiler_params=params(8),
    )(query, bias, sums, partner, neighbour)


def project_term(attended, wo_ref, first, keep_ref, send_ref):
    half = keep_ref.shape[0]
    for start in range(0, keep_ref.shape[1], OUT_BLOCK):
        columns = slice(start, start + OUT_BLOCK)
        term = jnp.dot(
            attended[...], wo_ref[:, first + start : first + start + OUT_BLOCK], preferred_element_type=F32
        ).astype(BF16)
        keep_ref[:, columns] = term[:half]
        send_ref[:, columns] = term[half:]


def attend_project(step, query, bias, sums, partner, neighbour, so_far, wo, fresh_noise, entry, width):
    tokens = query.shape[0]
    half = tokens // 2
    start = query.shape[1] - partner.shape[2]

    def kernel(entry_ref, query_ref, bias_ref, sums_ref, partner_ref, neighbour_ref, so_far_ref, wo_ref, noise_ref, keep_ref, send_ref, attended, sem):
        attended[:, :start] = so_far_ref[:, :start]
        attend_columns(start, query_ref, bias_ref, sums_ref, partner_ref, neighbour_ref, attended)
        project_term(attended, wo_ref, 0, keep_ref, send_ref)
        if step < ITERS - 1:

            @pl.when(slot_of(step + 1) == entry_ref[step])
            def _():
                copy = pltpu.make_async_copy(noise_ref.at[step], keep_ref, sem)
                copy.start()
                copy.wait()

    out = jax.ShapeDtypeStruct((half, width), BF16)
    return pl.pallas_call(
        kernel,
        out_shape=(out, out, jax.ShapeDtypeStruct(query.shape, BF16)),
        in_specs=[SMEM] + [VMEM] * 7 + [HBM],
        out_specs=(VMEM,) * 3,
        scratch_shapes=[pltpu.SemaphoreType.DMA(())],
        compiler_params=params(8),
    )(entry, query, bias, sums, partner, neighbour, so_far, wo, *in_hbm(fresh_noise))


def more_term(attended, wo, first, width):
    def kernel(attended_ref, wo_ref, keep_ref, send_ref):
        project_term(attended_ref, wo_ref, first, keep_ref, send_ref)

    out = jax.ShapeDtypeStruct((attended.shape[0] // 2, width), BF16)
    return pl.pallas_call(
        kernel,
        out_shape=(out, out),
        in_specs=[VMEM, VMEM],
        out_specs=(VMEM, VMEM),
        compiler_params=params(8),
    )(attended, wo)


def last_update(state, first, kept, received, fresh_noise, levels, entry, step_size):
    step = ITERS - 1
    width = kept.shape[1]

    def kernel(levels_ref, entry_ref, size_ref, state_ref, kept_ref, received_ref, noise_ref, out_ref, sem):
        velocity = kept_ref[...].astype(F32) + received_ref[...].astype(F32)
        size = size_ref[levels_ref[slot_of(step)]]
        out_ref[...] = (state_ref[:, first : first + width].astype(F32) + size * velocity).astype(BF16)

        @pl.when(slot_of(step + 1) == entry_ref[step])
        def _():
            copy = pltpu.make_async_copy(noise_ref.at[step, :, pl.ds(first, width)], out_ref, sem)
            copy.start()
            copy.wait()

    return pl.pallas_call(
        kernel,
        out_shape=jax.ShapeDtypeStruct(kept.shape, BF16),
        in_specs=[SMEM, SMEM, SMEM, VMEM, VMEM, VMEM, HBM],
        out_specs=VMEM,
        scratch_shapes=[pltpu.SemaphoreType.DMA(())],
        compiler_params=params(8),
    )(levels, entry, step_size, state, kept, received, *in_hbm(fresh_noise))


def exchanged(step, block):
    count = lax.axis_size("queue")
    got = []
    for first in (1, 0):
        pairs = []
        for i in range(first, count, 2):
            if (i + step) % count != count - 1:
                pairs += [(i, (i + 1) % count), ((i + 1) % count, i)]
        got.append(lax.ppermute(block, "queue", pairs))
    return got[::-1]


def on_device(
    latents, fresh_noise, levels, pattern, entry, level_scale, level_shift, step_size, qk_gain, wq, wk, wv, wo
):
    count = lax.axis_size("queue")
    mine = latents[0]
    depth = mine.shape[1]
    other = swap_cores(mine)
    rows, *weights = prepare(levels, level_scale, level_shift, wk, wv)
    for step in range(ITERS):
        if step == 0:
            whole, own, *more = first_modulated(mine, other, rows, qk_gain, weights[0], wk, wv)
            weights += more
        else:
            state, whole, own = next_modulated(
                step, mine, other, terms, received, rows, qk_gain, weights, levels, entry, step_size
            )
        theirs = exchanged(step, own)
        late = keys_values(whole, qk_gain, [weights[i] for i in CHUNKS[1]])
        late_theirs = exchanged(step, late)
        query, bias, sums = queries(step, whole, qk_gain, wq, pattern, [own, late])
        attended = attend(query, bias, sums, *theirs)
        width = depth if step < ITERS - 1 else depth // LAST_COLUMNS
        *terms, attended = attend_project(
            step, query, bias, sums, *late_theirs, attended, wo, fresh_noise, entry, width
        )
        if step < ITERS - 1:
            received = [swap_cores(term) for term in terms]
    route = [(i, (i + ITERS) % count) for i in range(count)]
    result = []
    for first in range(0, depth, width):
        if first > 0:
            terms = more_term(attended, wo, first, width)
        part = last_update(state, first, terms[0], swap_cores(terms[1]), fresh_noise, levels, entry, step_size)
        result.append(lax.ppermute(part, "queue", route))
    return jnp.concatenate(result, axis=1)[None]


def solution(mesh):
    return jax.shard_map(
        on_device,
        mesh=mesh,
        in_specs=(
            P("queue", "seq", None),
            P(None, "seq", None),
            P(),
            P(),
            P(),
            P(),
            P(),
            P(),
            P(),
            P(None, "seq"),
            P(None, "seq"),
            P(None, "seq"),
            P("seq", None),
        ),
        out_specs=P("queue", "seq", None),
        check_vma=False,
    )
```

time: 121 us -> 105 us (0.87); the launches traced: 121 us -> 103 us
  waiting for transfers between devices: 62.6 us -> 38.7 us
  Pallas kernels: 31.6 us -> 37.5 us
    ppermute x5 -> x10, waiting for transfers between devices: 57.9 us -> 34.9 us  [the longest x2 23 us: on_device(): result.append(lax.ppermute(part, 'queue', route))]
    pallas_call x5 -> x11, Pallas kernels: 20.4 us -> 24.4 us  [the longest x2 5.62 us: attend_project(): pl.pallas_call(kernel, out_shape=(out, out, jax.ShapeDtypeStruct(query.sh...]
    pallas_call x2, Pallas kernels: 6.84 us -> 10.5 us  [queries(): pl.pallas_call(kernel, out_shape=(jax.ShapeDtypeStruct((tokens, width), B...]
    pallas_call x1, Pallas kernels: 4.31 us -> 2.5 us  [prepare(): pl.pallas_call(kernel, out_shape=(jax.ShapeDtypeStruct((ITERS, 2, depth),...]
    ppermute x4 -> x5, waiting for transfers between devices: 4.67 us -> 3.81 us  [swap_cores(): return lax.ppermute(block, 'seq', [(0, 1), (1, 0)])]
    ppermute x4 -> x5, starting transfers between devices: 6.34 us -> 5.92 us  [swap_cores(): return lax.ppermute(block, 'seq', [(0, 1), (1, 0)])]
    ppermute x5 -> x10, starting transfers between devices: 19.1 us -> 19.1 us  [the longest x8 18.7 us: exchanged(): got.append(lax.ppermute(block, 'queue', pairs))]
  transfers between devices with their start and end apart: 9 -> 15, of which waited for: 8 -> 10; matrix products, arithmetic and copies ran while one was open for 0% -> 0% of each run, Pallas kernels for 9% -> 22%
where the time goes in v4:
time: 105 us; the launch traced here: 103 us
  waiting for transfers between devices  38.7 us (37%)
  Pallas kernels  37.5 us (36%)
  starting transfers between devices  25 us (24%)
    ppermute x2, waiting for transfers between devices, on_device(): result.append(lax.ppermute(part, 'queue', route))  23 us
    ppermute x8, starting transfers between devices, exchanged(): got.append(lax.ppermute(block, 'queue', pairs))  18.7 us
    ppermute x8, waiting for transfers between devices, exchanged(): got.append(lax.ppermute(block, 'queue', pairs))  11.9 us
    pallas_call x2, Pallas kernels, queries(): pl.pallas_call(kernel, out_shape=(jax.ShapeDtypeStruct((tokens, width), B...  10.5 us
    ppermute x5, starting transfers between devices, swap_cores(): return lax.ppermute(block, 'seq', [(0, 1), (1, 0)])  5.92 us
    pallas_call x2, Pallas kernels, attend_project(): pl.pallas_call(kernel, out_shape=(out, out, jax.ShapeDtypeStruct(query.sh...  5.62 us
    pallas_call x1, Pallas kernels, first_modulated(): pl.pallas_call(kernel, out_shape=(jax.ShapeDtypeStruct((2 * half, depth),...  5.05 us
    pallas_call x1, Pallas kernels, next_modulated(): pl.pallas_call(kernel, out_shape=(jax.ShapeDtypeStruct((half, depth), BF1...  4.7 us
  transfers between devices with their start and end apart: 15, of which 10 were waited for; matrix products, arithmetic and copies ran while one was open for 0% of the time, Pallas kernels for 22%

profile of v4, /device:TPU:1, one launch (start us, length us, event | category | flops | bytes accessed | tf_op | source)
XLA Modules:
  0.0 102.5 jit_solution(1099437269887304161)
XLA Ops:
  0.0 3.2 %collective-permute-start = (bf16[128,3072]{1,0:T(8,128)(2,1)}, bf16[128,3072]{1,0:T(8,128)(2,1)S(1)}, u32[]{:S(2)}, u32[]{:S(2)}) collective-permute-start(bf16[128,3072]{1,0:T(8,128)(2,1)} %bitcast.7), channel_id=1, source_target_pairs={{0,1},{1,0},{2,3},{3,2},{4,5},{5,4},{6,7},{7,6},{8,9},{9,8},{10,11... | collective-permute-start | bytes 2359304 | tf_op jit(solution)/shard_map/ppermute | solution.py:31
  3.2 2.5 %shard_map.127 = (f32[2,2,3072]{2,1,0:T(2,128)S(1)}, bf16[2,3072,256]{2,1,0:T(8,128)(2,1)S(1)}) custom-call(s32[128]{0:T(128)} %levels_ref.7, f32[50,3072]{1,0:T(8,128)} %scale_ref.1, f32[50,3072]{1,0:T(8,128)} %shift_ref.1, bf16[3072,768]{1,0:T(8,128)(2,1)} %wk_ref.3, bf16[3072,768]{1,0:T(8,128)(2,1)} %wv_ref.3), custom_call_target="tpu_custom_call" | custom-call | tf_op jit(solution)/shard_map/pallas_call | solution.py:118
  5.8 5.0 %shard_map.128 = (bf16[256,3072]{1,0:T(8,128)(2,1)S(1)}, bf16[2,256,512]{2,1,0:T(8,128)(2,1)S(1)}, bf16[2,3072,256]{2,1,0:T(8,128)(2,1)S(1)}, bf16[2,3072,256]{2,1,0:T(8,128)(2,1)S(1)}) custom-call(bf16[128,3072]{1,0:T(8,128)(2,1)S(1)} %bitcast.8, bf16[128,3072]{1,0:T(8,128)(2,1)S(1)} %collective-permute-done.other_ref, ...), custom_call_target="tpu_custom_call" | custom-call | tf_op jit(solution)/shard_map/pallas_call | solution.py:164
  11.0 0.7 collective-permute-start.4
  11.7 1.9 %shard_map.129.rest_1_ = bf16[2,256,256]{2,1,0:T(8,128)(2,1)S(1)} custom-call(bf16[256,3072]{1,0:T(8,128)(2,1)S(1)} %get-tuple-element.29.whole_ref, f32[2,64]{1,0:T(2,128)S(1)} %copy-done.1, bf16[2,3072,256]{2,1,0:T(8,128)(2,1)S(1)} %get-tuple-element.31.rest_0_), custom_call_target="tpu_custom_call" | custom-call | tf_op jit(solution)/shard_map/pallas_call | solution.py:220
  13.6 2.9 %collective-permute-start.1 = (bf16[2,256,256]{2,1,0:T(8,128)(2,1)S(1)}, bf16[2,256,256]{2,1,0:T(8,128)(2,1)S(1)}, u32[]{:S(2)}, u32[]{:S(2)}) collective-permute-start(bf16[2,256,256]{2,1,0:T(8,128)(2,1)S(1)} %shard_map.129.rest_1_), channel_id=1, source_target_pairs={{0,2},{2,0},{4,6},{6,4},{8,10},{10,8},{12,14},{14,12},{16,18},{18,... | collective-permute-start | bytes 786440 | tf_op jit(solution)/shard_map/ppermute | solution.py:400
  16.5 0.8 collective-permute-start.2
  17.4 5.3 %shard_map.130 = (bf16[256,768]{1,0:T(8,128)(2,1)S(1)}, bf16[3,256,128]{2,1,0:T(8,128)(2,1)S(1)}, f32[2,256,768]{2,1,0:T(8,128)S(1)}) custom-call(s32[4,12]{1,0:T(4,128)S(1)} %copy-done.3, f32[2,64]{1,0:T(2,128)S(1)} %copy-done.1, bf16[256,3072]{1,0:T(8,128)(2,1)S(1)} %get-tuple-element.29.whole_ref, bf16[3072,768]{1,0:T(8,128)(2,1)S(1)} %bitcast.6, ...), custom_call_target="tpu_custom_call" | custom-call | tf_op jit(solution)/shard_map/pallas_call | solution.py:277
  22.7 1.8 %collective-permute-done.3.refs_3_ = bf16[2,256,512]{2,1,0:T(8,128)(2,1)S(1)} collective-permute-done((bf16[2,256,512]{2,1,0:T(8,128)(2,1)S(1)}, bf16[2,256,512]{2,1,0:T(8,128)(2,1)S(1)}, u32[]{:S(2)}, u32[]{:S(2)}) %collective-permute-start.3) | collective-permute-done | bytes 524320 | tf_op jit(solution)/shard_map/ppermute | solution.py:400
  24.5 1.5 %shard_map.131.so_far_ref = bf16[256,768]{1,0:T(8,128)(2,1)S(1)} custom-call(bf16[256,768]{1,0:T(8,128)(2,1)S(1)} %get-tuple-element.32.refs_0_.query_ref, bf16[3,256,128]{2,1,0:T(8,128)(2,1)S(1)} %get-tuple-element.33.refs_1_.bias_ref, f32[2,256,768]{2,1,0:T(8,128)S(1)} %get-tuple-element.34.refs_2_.sums_ref, ...), custom_call_target="tpu_custom_call" | custom-call | tf_op jit(solution)/shard_map/pallas_call | solution.py:305
  26.1 4.1 %collective-permute-done.1.partner_ref = bf16[2,256,256]{2,1,0:T(8,128)(2,1)S(1)} collective-permute-done((bf16[2,256,256]{2,1,0:T(8,128)(2,1)S(1)}, bf16[2,256,256]{2,1,0:T(8,128)(2,1)S(1)}, u32[]{:S(2)}, u32[]{:S(2)}) %collective-permute-start.1) | collective-permute-done | bytes 262176 | tf_op jit(solution)/shard_map/ppermute | solution.py:400
  30.2 3.5 %shard_map.132 = (bf16[128,3072]{1,0:T(8,128)(2,1)S(1)}, bf16[128,3072]{1,0:T(8,128)(2,1)S(1)}, bf16[256,768]{1,0:T(8,128)(2,1)}) custom-call(s32[2]{0:T(128)S(1)} %copy-done.2, bf16[256,768]{1,0:T(8,128)(2,1)S(1)} %get-tuple-element.32.refs_0_.query_ref, bf16[3,256,128]{2,1,0:T(8,128)(2,1)S(1)} %get-tuple-element.33.refs_1_.bias_ref, ...), custom_call_target="tpu_custom_call" | custom-call | tf_op jit(solution)/shard_map/pallas_call | solution.py:343
  33.7 0.9 collective-permute-start.5
  34.6 1.8 %collective-permute-done.5.their_own = bf16[128,3072]{1,0:T(8,128)(2,1)S(1)} collective-permute-done((bf16[128,3072]{1,0:T(8,128)(2,1)S(1)}, bf16[128,3072]{1,0:T(8,128)(2,1)S(1)}, u32[]{:S(2)}, u32[]{:S(2)}) %collective-permute-start.5) | collective-permute-done | bytes 786464 | tf_op jit(solution)/shard_map/ppermute | solution.py:31
  36.4 1.1 %collective-permute-done.6.their_mine = bf16[128,3072]{1,0:T(8,128)(2,1)S(1)} collective-permute-done((bf16[128,3072]{1,0:T(8,128)(2,1)S(1)}, bf16[128,3072]{1,0:T(8,128)(2,1)S(1)}, u32[]{:S(2)}, u32[]{:S(2)}) %collective-permute-start.6) | collective-permute-done | bytes 786464 | tf_op jit(solution)/shard_map/ppermute | solution.py:31
  37.6 4.7 %shard_map.133 = (bf16[128,3072]{1,0:T(8,128)(2,1)S(1)}, bf16[256,3072]{1,0:T(8,128)(2,1)S(1)}, bf16[2,256,512]{2,1,0:T(8,128)(2,1)S(1)}) custom-call(s32[128]{0:T(128)S(1)} %copy-done.4, s32[2]{0:T(128)S(1)} %copy-done.2, f32[50]{0:T(128)S(1)} %copy-done.5, bf16[128,3072]{1,0:T(8,128)(2,1)S(1)} %bitcast.9, ...), custom_call_target="tpu_custom_call" | custom-call | tf_op jit(solution)/shard_map/pallas_call | solution.py:202
  42.3 8.6 %collective-permute-start.10 = (bf16[2,256,512]{2,1,0:T(8,128)(2,1)S(1)}, bf16[2,256,512]{2,1,0:T(8,128)(2,1)S(1)}, u32[]{:S(2)}, u32[]{:S(2)}) collective-permute-start(bf16[2,256,512]{2,1,0:T(8,128)(2,1)S(1)} %get-tuple-element.40.rest_0_), channel_id=1, source_target_pairs={{2,4},{4,2},{6,8},{8,6},{10,12},{12,10},{14,16},{16,14},{18,20},{2... | collective-permute-start | bytes 1572872 | tf_op jit(solution)/shard_map/ppermute | solution.py:400
  50.8 2.1 %collective-permute-start.9 = (bf16[2,256,512]{2,1,0:T(8,128)(2,1)S(1)}, bf16[2,256,512]{2,1,0:T(8,128)(2,1)S(1)}, u32[]{:S(2)}, u32[]{:S(2)}) collective-permute-start(bf16[2,256,512]{2,1,0:T(8,128)(2,1)S(1)} %get-tuple-element.40.rest_0_), channel_id=1, source_target_pairs={{0,2},{2,0},{4,6},{6,4},{8,10},{10,8},{12,14},{14,12},{16,18},{18,... | collective-permute-start | bytes 1572872 | tf_op jit(solution)/shard_map/ppermute | solution.py:400
  53.0 1.9 %shard_map.134.rest_1_ = bf16[2,256,256]{2,1,0:T(8,128)(2,1)S(1)} custom-call(bf16[256,3072]{1,0:T(8,128)(2,1)S(1)} %get-tuple-element.39.whole_ref, f32[2,64]{1,0:T(2,128)S(1)} %copy-done.1, bf16[2,3072,256]{2,1,0:T(8,128)(2,1)S(1)} %get-tuple-element.31.rest_0_), custom_call_target="tpu_custom_call" | custom-call | tf_op jit(solution)/shard_map/pallas_call | solution.py:220
  54.9 3.4 %collective-permute-start.7 = (bf16[2,256,256]{2,1,0:T(8,128)(2,1)S(1)}, bf16[2,256,256]{2,1,0:T(8,128)(2,1)S(1)}, u32[]{:S(2)}, u32[]{:S(2)}) collective-permute-start(bf16[2,256,256]{2,1,0:T(8,128)(2,1)S(1)} %shard_map.134.rest_1_), channel_id=1, source_target_pairs={{0,2},{2,0},{4,6},{6,4},{8,10},{10,8},{12,14},{14,12},{16,18},{18,... | collective-permute-start | bytes 786440 | tf_op jit(solution)/shard_map/ppermute | solution.py:400
  58.4 5.3 %shard_map.135 = (bf16[256,768]{1,0:T(8,128)(2,1)S(1)}, bf16[3,256,128]{2,1,0:T(8,128)(2,1)S(1)}, f32[2,256,768]{2,1,0:T(8,128)S(1)}) custom-call(s32[4,12]{1,0:T(4,128)S(1)} %copy-done.3, f32[2,64]{1,0:T(2,128)S(1)} %copy-done.1, bf16[256,3072]{1,0:T(8,128)(2,1)S(1)} %get-tuple-element.39.whole_ref, bf16[3072,768]{1,0:T(8,128)(2,1)S(1)} %bitcast.6, ...), custom_call_target="tpu_custom_call" | custom-call | tf_op jit(solution)/shard_map/pallas_call | solution.py:277
  63.6 1.9 %collective-permute-done.9.refs_3_ = bf16[2,256,512]{2,1,0:T(8,128)(2,1)S(1)} collective-permute-done((bf16[2,256,512]{2,1,0:T(8,128)(2,1)S(1)}, bf16[2,256,512]{2,1,0:T(8,128)(2,1)S(1)}, u32[]{:S(2)}, u32[]{:S(2)}) %collective-permute-start.9) | collective-permute-done | bytes 524320 | tf_op jit(solution)/shard_map/ppermute | solution.py:400
  65.5 1.5 %shard_map.136.so_far_ref = bf16[256,768]{1,0:T(8,128)(2,1)S(1)} custom-call(bf16[256,768]{1,0:T(8,128)(2,1)S(1)} %get-tuple-element.41.refs_0_.query_ref, bf16[3,256,128]{2,1,0:T(8,128)(2,1)S(1)} %get-tuple-element.42.refs_1_.bias_ref, f32[2,256,768]{2,1,0:T(8,128)S(1)} %get-tuple-element.43.refs_2_.sums_ref, ...), custom_call_target="tpu_custom_call" | custom-call | tf_op jit(solution)/shard_map/pallas_call | solution.py:305
  67.0 4.1 %collective-permute-done.7.partner_ref = bf16[2,256,256]{2,1,0:T(8,128)(2,1)S(1)} collective-permute-done((bf16[2,256,256]{2,1,0:T(8,128)(2,1)S(1)}, bf16[2,256,256]{2,1,0:T(8,128)(2,1)S(1)}, u32[]{:S(2)}, u32[]{:S(2)}) %collective-permute-start.7) | collective-permute-done | bytes 262176 | tf_op jit(solution)/shard_map/ppermute | solution.py:400
  71.2 2.1 %shard_map.137 = (bf16[128,1536]{1,0:T(8,128)(2,1)S(1)}, bf16[128,1536]{1,0:T(8,128)(2,1)S(1)}, bf16[256,768]{1,0:T(8,128)(2,1)S(1)}) custom-call(s32[2]{0:T(128)S(1)} %copy-done.2, bf16[256,768]{1,0:T(8,128)(2,1)S(1)} %get-tuple-element.41.refs_0_.query_ref, bf16[3,256,128]{2,1,0:T(8,128)(2,1)S(1)} %get-tuple-element.42.refs_1_.bias_ref, ...), custom_call_target="tpu_custom_call" | custom-call | tf_op jit(solution)/shard_map/pallas_call | solution.py:343
  73.3 1.6 %collective-permute-start.11 = (bf16[128,1536]{1,0:T(8,128)(2,1)S(1)}, bf16[128,1536]{1,0:T(8,128)(2,1)S(1)}, u32[]{:S(2)}, u32[]{:S(2)}) collective-permute-start(bf16[128,1536]{1,0:T(8,128)(2,1)S(1)} %get-tuple-element.45), channel_id=1, source_target_pairs={{0,1},{1,0},{2,3},{3,2},{4,5},{5,4},{6,7},{7,6},{8,9},{9,8},{10,11... | collective-permute-start | bytes 1179656 | tf_op jit(solution)/shard_map/ppermute | solution.py:31
  74.9 0.8 shard_map.139
  76.3 0.7 shard_map.138
  77.5 0.7 shard_map.140
  78.6 14.6 %collective-permute-done.12 = bf16[128,1536]{1,0:T(8,128)(2,1)S(1)} collective-permute-done((bf16[128,1536]{1,0:T(8,128)(2,1)S(1)}, bf16[128,1536]{1,0:T(8,128)(2,1)S(1)}, u32[]{:S(2)}, u32[]{:S(2)}) %collective-permute-start.12) | collective-permute-done | bytes 393248 | tf_op jit(solution)/shard_map/ppermute | solution.py:437
  93.1 8.4 %collective-permute-done.14 = bf16[128,1536]{1,0:T(8,128)(2,1)S(1)} collective-permute-done((bf16[128,1536]{1,0:T(8,128)(2,1)S(1)}, bf16[128,1536]{1,0:T(8,128)(2,1)S(1)}, u32[]{:S(2)}, u32[]{:S(2)}) %collective-permute-start.14) | collective-permute-done | bytes 393248 | tf_op jit(solution)/shard_map/ppermute | solution.py:437
  101.6 1.0 maximum_bitcast_fusion
  (35 shorter events, 1.7 us)
Async XLA Ops:
  0.0 5.8 %copy-start = (bf16[1,128,3072]{2,1,0:T(8,128)(2,1)S(1)}, bf16[1,128,3072]{2,1,0:T(8,128)(2,1)}, u32[]{:S(2)}) copy-start(bf16[1,128,3072]{2,1,0:T(8,128)(2,1)} %param.13) | copy-start | bytes 2359300
  0.0 5.8 %copy-start.1 = (f32[2,64]{1,0:T(2,128)S(1)}, f32[2,64]{1,0:T(2,128)}, u32[]{:S(2)}) copy-start(f32[2,64]{1,0:T(2,128)} %gain_ref.11) | copy-start | bytes 1540
  0.0 5.8 %collective-permute-start = (bf16[128,3072]{1,0:T(8,128)(2,1)}, bf16[128,3072]{1,0:T(8,128)(2,1)S(1)}, u32[]{:S(2)}, u32[]{:S(2)}) collective-permute-start(bf16[128,3072]{1,0:T(8,128)(2,1)} %bitcast.7), channel_id=1, source_target_pairs={{0,1},{1,0},{2,3},{3,2},{4,5},{5,4},{6,7},{7,6},{8,9},{9,8},{10,11... | collective-permute-start | bytes 2359304 | tf_op jit(solution)/shard_map/ppermute | solution.py:31
  3.2 14.1 %slice-start.2 = ((s8[4718592]{0:T(1024)(128)(4,1)}), s8[4194304]{0:T(1024)(128)(4,1)S(1)}, s32[]{:S(2)}) async-start(s8[4718592]{0:T(1024)(128)(4,1)} %bitcast.5), calls=%async_computation.2 | async-start | bytes 8388608
  5.8 11.6 %slice-start.3 = ((s8[4718592]{0:T(1024)(128)(4,1)}), s8[524288]{0:T(1024)(128)(4,1)S(1)}, s32[]{:S(2)}) async-start(s8[4718592]{0:T(1024)(128)(4,1)} %bitcast.5), calls=%async_computation.3 | async-start | bytes 1048576
  10.9 13.6 %collective-permute-start.3 = (bf16[2,256,512]{2,1,0:T(8,128)(2,1)S(1)}, bf16[2,256,512]{2,1,0:T(8,128)(2,1)S(1)}, u32[]{:S(2)}, u32[]{:S(2)}) collective-permute-start(bf16[2,256,512]{2,1,0:T(8,128)(2,1)S(1)} %get-tuple-element.30.rest_0_), channel_id=1, source_target_pairs={{0,2},{2,0},{4,6},{6,4},{8,10},{10,8},{12,14},{14,12},{16,18},{18,... | collective-permute-start | bytes 1572872 | tf_op jit(solution)/shard_map/ppermute | solution.py:400
  11.0 13.5 %collective-permute-start.4 = (bf16[2,256,512]{2,1,0:T(8,128)(2,1)S(1)}, bf16[2,256,512]{2,1,0:T(8,128)(2,1)S(1)}, u32[]{:S(2)}, u32[]{:S(2)}) collective-permute-start(bf16[2,256,512]{2,1,0:T(8,128)(2,1)S(1)} %get-tuple-element.30.rest_0_), channel_id=1, source_target_pairs={{2,4},{4,2},{6,8},{8,6},{10,12},{12,10},{14,16},{16,14},{18,20},{2... | collective-permute-start | bytes 1572872 | tf_op jit(solution)/shard_map/ppermute | solution.py:400
  11.7 5.7 %copy-start.3 = (s32[4,12]{1,0:T(4,128)S(1)}, s32[4,12]{1,0:T(4,128)}, u32[]{:S(2)}) copy-start(s32[4,12]{1,0:T(4,128)} %pattern_ref.3) | copy-start | bytes 580
  11.7 18.4 %slice-start = ((s8[4718592]{0:T(1024)(128)(4,1)}), s8[4194304]{0:T(1024)(128)(4,1)S(1)}, s32[]{:S(2)}) async-start(s8[4718592]{0:T(1024)(128)(4,1)} %bitcast.3), calls=%async_computation | async-start | bytes 8388608
  13.6 16.5 %slice-start.1 = ((s8[4718592]{0:T(1024)(128)(4,1)}), s8[524288]{0:T(1024)(128)(4,1)S(1)}, s32[]{:S(2)}) async-start(s8[4718592]{0:T(1024)(128)(4,1)} %bitcast.3), calls=%async_computation.1 | async-start | bytes 1048576
  13.6 16.5 %collective-permute-start.1 = (bf16[2,256,256]{2,1,0:T(8,128)(2,1)S(1)}, bf16[2,256,256]{2,1,0:T(8,128)(2,1)S(1)}, u32[]{:S(2)}, u32[]{:S(2)}) collective-permute-start(bf16[2,256,256]{2,1,0:T(8,128)(2,1)S(1)} %shard_map.129.rest_1_), channel_id=1, source_target_pairs={{0,2},{2,0},{4,6},{6,4},{8,10},{10,8},{12,14},{14,12},{16,18},{18,... | collective-permute-start | bytes 786440 | tf_op jit(solution)/shard_map/ppermute | solution.py:400
  16.5 13.6 %collective-permute-start.2 = (bf16[2,256,256]{2,1,0:T(8,128)(2,1)S(1)}, bf16[2,256,256]{2,1,0:T(8,128)(2,1)S(1)}, u32[]{:S(2)}, u32[]{:S(2)}) collective-permute-start(bf16[2,256,256]{2,1,0:T(8,128)(2,1)S(1)} %shard_map.129.rest_1_), channel_id=1, source_target_pairs={{2,4},{4,2},{6,8},{8,6},{10,12},{12,10},{14,16},{16,14},{18,20},{2... | collective-permute-start | bytes 786440 | tf_op jit(solution)/shard_map/ppermute | solution.py:400
  24.5 5.6 %copy-start.2 = (s32[2]{0:T(128)S(1)}, s32[2]{0:T(128)}, u32[]{:S(2)}) copy-start(s32[2]{0:T(128)} %entry_ref.9) | copy-start | bytes 28
  26.0 11.5 %copy-start.4 = (s32[128]{0:T(128)S(1)}, s32[128]{0:T(128)}, u32[]{:S(2)}) copy-start(s32[128]{0:T(128)} %levels_ref.7) | copy-start | bytes 1540
  26.1 11.5 %copy-start.5 = (f32[50]{0:T(128)S(1)}, f32[50]{0:T(128)}, u32[]{:S(2)}) copy-start(f32[50]{0:T(128)} %size_ref.5) | copy-start | bytes 604
  33.7 2.8 %collective-permute-start.5 = (bf16[128,3072]{1,0:T(8,128)(2,1)S(1)}, bf16[128,3072]{1,0:T(8,128)(2,1)S(1)}, u32[]{:S(2)}, u32[]{:S(2)}) collective-permute-start(bf16[128,3072]{1,0:T(8,128)(2,1)S(1)} %get-tuple-element.35.term_mine), channel_id=1, source_target_pairs={{0,1},{1,0},{2,3},{3,2},{4,5},{5,4},{6,7},{7,6},{8,9},{9,8},{10,11... | collective-permute-start | bytes 2359304 | tf_op jit(solution)/shard_map/ppermute | solution.py:31
  34.5 3.0 %collective-permute-start.6 = (bf16[128,3072]{1,0:T(8,128)(2,1)S(1)}, bf16[128,3072]{1,0:T(8,128)(2,1)S(1)}, u32[]{:S(2)}, u32[]{:S(2)}) collective-permute-start(bf16[128,3072]{1,0:T(8,128)(2,1)S(1)} %get-tuple-element.36.term_other), channel_id=1, source_target_pairs={{0,1},{1,0},{2,3},{3,2},{4,5},{5,4},{6,7},{7,6},{8,9},{9,8},{10,11... | collective-permute-start | bytes 2359304 | tf_op jit(solution)/shard_map/ppermute | solution.py:31
  42.3 21.4 %collective-permute-start.10 = (bf16[2,256,512]{2,1,0:T(8,128)(2,1)S(1)}, bf16[2,256,512]{2,1,0:T(8,128)(2,1)S(1)}, u32[]{:S(2)}, u32[]{:S(2)}) collective-permute-start(bf16[2,256,512]{2,1,0:T(8,128)(2,1)S(1)} %get-tuple-element.40.rest_0_), channel_id=1, source_target_pairs={{2,4},{4,2},{6,8},{8,6},{10,12},{12,10},{14,16},{16,14},{18,20},{2... | collective-permute-start | bytes 1572872 | tf_op jit(solution)/shard_map/ppermute | solution.py:400
  50.8 14.7 %collective-permute-start.9 = (bf16[2,256,512]{2,1,0:T(8,128)(2,1)S(1)}, bf16[2,256,512]{2,1,0:T(8,128)(2,1)S(1)}, u32[]{:S(2)}, u32[]{:S(2)}) collective-permute-start(bf16[2,256,512]{2,1,0:T(8,128)(2,1)S(1)} %get-tuple-element.40.rest_0_), channel_id=1, source_target_pairs={{0,2},{2,0},{4,6},{6,4},{8,10},{10,8},{12,14},{14,12},{16,18},{18,... | collective-permute-start | bytes 1572872 | tf_op jit(solution)/shard_map/ppermute | solution.py:400
  54.9 16.3 %collective-permute-start.7 = (bf16[2,256,256]{2,1,0:T(8,128)(2,1)S(1)}, bf16[2,256,256]{2,1,0:T(8,128)(2,1)S(1)}, u32[]{:S(2)}, u32[]{:S(2)}) collective-permute-start(bf16[2,256,256]{2,1,0:T(8,128)(2,1)S(1)} %shard_map.134.rest_1_), channel_id=1, source_target_pairs={{0,2},{2,0},{4,6},{6,4},{8,10},{10,8},{12,14},{14,12},{16,18},{18,... | collective-permute-start | bytes 786440 | tf_op jit(solution)/shard_map/ppermute | solution.py:400
  58.3 12.9 %collective-permute-start.8 = (bf16[2,256,256]{2,1,0:T(8,128)(2,1)S(1)}, bf16[2,256,256]{2,1,0:T(8,128)(2,1)S(1)}, u32[]{:S(2)}, u32[]{:S(2)}) collective-permute-start(bf16[2,256,256]{2,1,0:T(8,128)(2,1)S(1)} %shard_map.134.rest_1_), channel_id=1, source_target_pairs={{2,4},{4,2},{6,8},{8,6},{10,12},{12,10},{14,16},{16,14},{18,20},{2... | collective-permute-start | bytes 786440 | tf_op jit(solution)/shard_map/ppermute | solution.py:400
  73.3 3.0 %collective-permute-start.11 = (bf16[128,1536]{1,0:T(8,128)(2,1)S(1)}, bf16[128,1536]{1,0:T(8,128)(2,1)S(1)}, u32[]{:S(2)}, u32[]{:S(2)}) collective-permute-start(bf16[128,1536]{1,0:T(8,128)(2,1)S(1)} %get-tuple-element.45), channel_id=1, source_target_pairs={{0,1},{1,0},{2,3},{3,2},{4,5},{5,4},{6,7},{7,6},{8,9},{9,8},{10,11... | collective-permute-start | bytes 1179656 | tf_op jit(solution)/shard_map/ppermute | solution.py:31
  75.7 1.8 %collective-permute-start.13 = (bf16[128,1536]{1,0:T(8,128)(2,1)S(1)}, bf16[128,1536]{1,0:T(8,128)(2,1)S(1)}, u32[]{:S(2)}, u32[]{:S(2)}) collective-permute-start(bf16[128,1536]{1,0:T(8,128)(2,1)S(1)} %get-tuple-element.48), channel_id=1, source_target_pairs={{0,1},{1,0},{2,3},{3,2},{4,5},{5,4},{6,7},{7,6},{8,9},{9,8},{10,11... | collective-permute-start | bytes 1179656 | tf_op jit(solution)/shard_map/ppermute | solution.py:31
  77.0 16.1 %collective-permute-start.12 = (bf16[128,1536]{1,0:T(8,128)(2,1)S(1)}, bf16[128,1536]{1,0:T(8,128)(2,1)S(1)}, u32[]{:S(2)}, u32[]{:S(2)}) collective-permute-start(bf16[128,1536]{1,0:T(8,128)(2,1)S(1)} %shard_map.138), channel_id=1, source_target_pairs={{0,4},{2,6},{4,8},{6,10},{8,12},{10,14},{12,16},{14,18},{16,20},{1... | collective-permute-start | bytes 1179656 | tf_op jit(solution)/shard_map/ppermute | solution.py:437
  78.2 23.3 %collective-permute-start.14 = (bf16[128,1536]{1,0:T(8,128)(2,1)S(1)}, bf16[128,1536]{1,0:T(8,128)(2,1)S(1)}, u32[]{:S(2)}, u32[]{:S(2)}) collective-permute-start(bf16[128,1536]{1,0:T(8,128)(2,1)S(1)} %shard_map.140), channel_id=1, source_target_pairs={{0,4},{2,6},{4,8},{6,10},{8,12},{10,14},{12,16},{14,18},{16,20},{1... | collective-permute-start | bytes 1179656 | tf_op jit(solution)/shard_map/ppermute | solution.py:437

commit v5 on v1

v5 whole, which is shorter than its diff:
```python
import math

import jax
import jax.numpy as jnp
from jax import lax
from jax.experimental import pallas as pl
from jax.experimental.pallas import tpu as pltpu
from jax.sharding import PartitionSpec as P

HD = 64
FRAMES = 4
ITERS = 2
LANES = 128
EPS = 1e-06
CLOSED = -30000.0
BLOCK = 256
OUT_BLOCK = 768
LAST_COLUMNS = 2
MIB = 1 << 20
F32 = jnp.float32
BF16 = jnp.bfloat16

SMEM = pl.BlockSpec(memory_space=pltpu.SMEM)
VMEM = pl.BlockSpec(memory_space=pltpu.VMEM)
HBM = pl.BlockSpec(memory_space=pltpu.HBM)


def swap_cores(block):
    return lax.ppermute(block, "seq", [(0, 1), (1, 0)])


def in_hbm(*arrays):
    return tuple(pltpu.with_memory_space_constraint(array, pltpu.HBM) for array in arrays)


def params(mib):
    return pltpu.CompilerParams(vmem_limit_bytes=mib * MIB)


def slot_of(step):
    return lax.rem(lax.axis_index("queue") + step, lax.axis_size("queue"))


def modulated_rows(values, scale_row, shift_row):
    normed = values * lax.rsqrt(jnp.mean(values * values, axis=-1, keepdims=True) + EPS)
    return (normed * scale_row + shift_row).astype(BF16)


def head_normed(values, gain_row):
    rows, width = values.shape
    blocks = [values[:, first : first + BLOCK] for first in range(0, width, BLOCK)]
    stacked = jnp.concatenate(blocks, axis=0)
    row = lax.broadcasted_iota(jnp.int32, (BLOCK, BLOCK), 0)
    column = lax.broadcasted_iota(jnp.int32, (BLOCK, BLOCK), 1)
    same = (row // HD == column // HD).astype(BF16)
    sums = jnp.dot((stacked * stacked).astype(BF16), same, preferred_element_type=F32)
    normed = (stacked * lax.rsqrt(sums * (1.0 / HD) + EPS) * gain_row).astype(BF16)
    return jnp.concatenate([normed[i * rows : (i + 1) * rows] for i in range(len(blocks))], axis=1)


def gain_columns(gain_ref, which):
    return jnp.concatenate([gain_ref[which : which + 1, :]] * (BLOCK // HD), axis=1)


def window_bias(pattern_ref, bias_ref, slot, frame_rows):
    count, core = lax.axis_size("queue"), lax.axis_index("seq")
    odd = lax.rem(lax.axis_index("queue"), 2)
    lane = lax.broadcasted_iota(jnp.int32, (1, LANES), 1)
    half = FRAMES // 2
    for i, block in enumerate((1, 2 - 2 * odd, 2 * odd)):
        absent = slot == jnp.where(block == 0, 0, count - 1)
        for at in range(FRAMES):
            key_frame = lax.rem(at + half * core, FRAMES)
            row = jnp.zeros((1, LANES), F32)
            for f in range(FRAMES):
                if i == 0 and f == at:
                    continue
                closed = pattern_ref[lax.rem(f + half * core, FRAMES), block * FRAMES + key_frame] != 1
                if i > 0:
                    closed = jnp.logical_or(closed, absent)
                row = row + jnp.where(lane == f, jnp.where(closed, CLOSED, 0.0), 0.0)
            to, first = (0, at) if i == 0 else (1 + at // half, (i - 1) * half + at % half)
            rows = slice(first * frame_rows, (first + 1) * frame_rows)
            bias_ref[to, rows, :] = jnp.broadcast_to(row, (frame_rows, LANES)).astype(BF16)


def project(modulated, gain_ref, wk_ref, wv_ref, out_ref):
    keys = jnp.dot(modulated, wk_ref[...], preferred_element_type=F32)
    out_ref[0] = head_normed(keys, gain_columns(gain_ref, 1))
    out_ref[1] = jnp.dot(modulated, wv_ref[...], preferred_element_type=F32).astype(BF16)


def first_half(state, levels, level_scale, level_shift, qk_gain, wk, wv):
    half, depth = state.shape
    width = wk.shape[1]

    def kernel(levels_ref, scale_ref, shift_ref, state_hbm, gain_hbm, wk_ref, wv_ref, modulated_ref, out_ref, rows_ref, wk_out, wv_out, held, state_ref, gain_ref, levels_sm, sems, weight_sems):
        first = pltpu.make_async_copy(levels_ref, levels_sm, sems.at[0])
        first.start()
        tables = [
            pltpu.make_async_copy(scale_ref, held.at[0], sems.at[1]),
            pltpu.make_async_copy(shift_ref, held.at[1], sems.at[2]),
            pltpu.make_async_copy(state_hbm, state_ref, sems.at[3]),
            pltpu.make_async_copy(gain_hbm, gain_ref, sems.at[4]),
        ]
        parts = [pl.ds(0, depth // 2), pl.ds(depth // 2, depth // 2)]
        weights = [
            pltpu.make_async_copy(ref.at[part], out.at[part], weight_sems.at[2 * i + j])
            for i, (ref, out) in enumerate(((wk_ref, wk_out), (wv_ref, wv_out)))
            for j, part in enumerate(parts)
        ]
        for copy in tables + weights[:2]:
            copy.start()
        for copy in [first] + tables:
            copy.wait()
        for step in range(ITERS):
            row = pl.ds(levels_sm[slot_of(step)], 1)
            rows_ref[step, 0:1, :] = 1.0 + held[0, row, :]
            rows_ref[step, 1:2, :] = held[1, row, :]
        modulated_ref[...] = modulated_rows(state_ref[...].astype(F32), rows_ref[0, 0:1, :], rows_ref[0, 1:2, :])
        for i, weight in enumerate((wk_out, wv_out)):
            total = None
            for j, part in enumerate(parts):
                weights[2 * i + j].wait()
                if i == 0:
                    weights[2 + j].start()
                product = jnp.dot(modulated_ref[:, part], weight[part, :], preferred_element_type=F32)
                total = product if total is None else total + product
            out_ref[i] = head_normed(total, gain_columns(gain_ref, 1)) if i == 0 else total.astype(BF16)

    return pl.pallas_call(
        kernel,
        out_shape=(
            jax.ShapeDtypeStruct((half, depth), BF16),
            jax.ShapeDtypeStruct((2, half, width), BF16),
            jax.ShapeDtypeStruct((ITERS, 2, depth), F32),
            jax.ShapeDtypeStruct(wk.shape, BF16),
            jax.ShapeDtypeStruct(wv.shape, BF16),
        ),
        in_specs=[HBM] * 7,
        out_specs=(VMEM,) * 5,
        scratch_shapes=[
            pltpu.VMEM((2, *level_scale.shape), F32),
            pltpu.VMEM(state.shape, BF16),
            pltpu.VMEM(qk_gain.shape, F32),
            pltpu.SMEM(levels.shape, jnp.int32),
            pltpu.SemaphoreType.DMA((5,)),
            pltpu.SemaphoreType.DMA((4,)),
        ],
        compiler_params=params(8),
    )(*in_hbm(levels, level_scale, level_shift, state, qk_gain, wk, wv))


def next_half(step, state, kept, received, fresh_noise, rows, qk_gain, wk, wv, levels, entry, step_size):
    half, depth = state.shape
    width = wk.shape[1]

    def kernel(levels_ref, entry_ref, size_ref, state_ref, kept_ref, received_ref, rows_ref, gain_ref, wk_ref, wv_ref, noise_ref, new_ref, modulated_ref, out_ref, sem):
        size = size_ref[levels_ref[slot_of(step - 1)]]
        velocity = kept_ref[...].astype(F32) + received_ref[...].astype(F32)
        new_ref[...] = (state_ref[...].astype(F32) + size * velocity).astype(BF16)

        @pl.when(slot_of(step) == entry_ref[step - 1])
        def _():
            copy = pltpu.make_async_copy(noise_ref.at[step - 1], new_ref, sem)
            copy.start()
            copy.wait()

        modulated_ref[...] = modulated_rows(new_ref[...].astype(F32), rows_ref[step, 0:1, :], rows_ref[step, 1:2, :])
        project(modulated_ref[...], gain_ref, wk_ref, wv_ref, out_ref)

    return pl.pallas_call(
        kernel,
        out_shape=(
            jax.ShapeDtypeStruct((half, depth), BF16),
            jax.ShapeDtypeStruct((half, depth), BF16),
            jax.ShapeDtypeStruct((2, half, width), BF16),
        ),
        in_specs=[SMEM] * 3 + [VMEM] * 7 + [HBM],
        out_specs=(VMEM,) * 3,
        scratch_shapes=[pltpu.SemaphoreType.DMA(())],
        compiler_params=params(8),
    )(levels, entry, step_size, state, kept, received, rows, qk_gain, wk, wv, *in_hbm(fresh_noise))


def other_half(modulated, qk_gain, wk, wv, wq):
    half = modulated.shape[0]
    width = wk.shape[1]
    load = wq is not None

    def kernel(modulated_ref, gain_ref, wk_ref, wv_ref, *rest):
        out_ref = rest[load]
        if load:
            copy = pltpu.make_async_copy(rest[0], rest[2], rest[3])
            copy.start()
        project(modulated_ref[...], gain_ref, wk_ref, wv_ref, out_ref)
        if load:
            copy.wait()

    out = jax.ShapeDtypeStruct((2, half, width), BF16)
    return pl.pallas_call(
        kernel,
        out_shape=(out, jax.ShapeDtypeStruct(wq.shape, BF16)) if load else (out,),
        in_specs=[VMEM] * 4 + [HBM] * load,
        out_specs=(VMEM,) * (1 + load),
        scratch_shapes=[pltpu.SemaphoreType.DMA(())] * load,
        compiler_params=params(8),
    )(modulated, qk_gain, wk, wv, *(in_hbm(wq) if load else ()))


def attention_parts(query_pair, keys, values, bias):
    tokens = query_pair.shape[0]
    lane = lax.broadcasted_iota(jnp.int32, (tokens, LANES), 1)
    frame = lax.broadcasted_iota(jnp.int32, (tokens, LANES), 0) // (tokens // FRAMES)
    frame_of = (lane == frame).astype(BF16)
    first = lane < HD
    ones = jnp.ones((tokens, LANES), BF16)
    parts = []
    for which in (first, jnp.logical_not(first)):
        one = jnp.concatenate([jnp.where(which, query_pair, jnp.zeros_like(query_pair)), frame_of], axis=1)
        scores = lax.dot_general(
            one, jnp.concatenate([keys, bias], axis=1), (((1,), (1,)), ((), ())), preferred_element_type=F32
        )
        weights = jnp.exp2(scores).astype(BF16)
        parts.append(jnp.dot(weights, jnp.concatenate([values, ones], axis=1), preferred_element_type=F32))
    return (
        jnp.where(first, parts[0][:, :LANES], parts[1][:, :LANES]),
        jnp.where(first, parts[0][:, LANES:], parts[1][:, LANES:]),
    )


def pair_parts(query_ref, first_ref, second_ref, bias, columns):
    keys, values = (
        jnp.concatenate([first_ref[i, :, columns], second_ref[i, :, columns]], axis=0) for i in range(2)
    )
    return attention_parts(query_ref[:, columns], keys, values, bias)


def queries(step, mine, other, qk_gain, wq, pattern, own, own_other, wo):
    half, _ = mine.shape
    tokens, width = 2 * half, wq.shape[1]
    scale = math.log2(math.e) / math.sqrt(HD)
    load = wo is not None

    def kernel(pattern_ref, gain_ref, mine_ref, other_ref, wq_ref, own_ref, own_other_ref, *rest):
        out_ref, bias_ref, sums_ref = rest[load : load + 3]
        whole = rest[-1 - load]
        if load:
            copy = pltpu.make_async_copy(rest[0], rest[load + 3], rest[-1])
            copy.start()
        whole[:half, :] = mine_ref[...]
        whole[half:, :] = other_ref[...]
        window_bias(pattern_ref, bias_ref, slot_of(step), tokens // FRAMES)
        query = jnp.dot(whole[...], wq_ref[...], preferred_element_type=F32)
        out_ref[...] = head_normed(query, gain_columns(gain_ref, 0) * scale)
        for first in range(0, width, LANES):
            columns = slice(first, first + LANES)
            sums_ref[0, :, columns], sums_ref[1, :, columns] = pair_parts(out_ref, own_ref, own_other_ref, bias_ref[0], columns)
        if load:
            copy.wait()

    out_shape = [
        jax.ShapeDtypeStruct((tokens, width), BF16),
        jax.ShapeDtypeStruct((3, tokens, LANES), BF16),
        jax.ShapeDtypeStruct((2, tokens, width), F32),
    ]
    if load:
        out_shape.append(jax.ShapeDtypeStruct(wo.shape, BF16))
    return pl.pallas_call(
        kernel,
        out_shape=out_shape,
        in_specs=[SMEM] + [VMEM] * 6 + [HBM] * load,
        out_specs=[VMEM] * (3 + load),
        scratch_shapes=[pltpu.VMEM((tokens, mine.shape[1]), BF16)] + [pltpu.SemaphoreType.DMA(())] * load,
        compiler_params=params(8),
    )(pattern, qk_gain, mine, other, wq, own, own_other, *(in_hbm(wo) if load else ()))


def attend(query, bias, sums, partner, neighbour):
    def kernel(query_ref, bias_ref, sums_ref, partner_ref, neighbour_ref, out_ref):
        for first in range(0, query_ref.shape[1], LANES):
            columns = slice(first, first + LANES)
            parts = pair_parts(query_ref, partner_ref, neighbour_ref, bias_ref[1], columns)
            for i in range(2):
                out_ref[i, :, columns] = sums_ref[i, :, columns] + parts[i]

    return pl.pallas_call(
        kernel,
        out_shape=jax.ShapeDtypeStruct(sums.shape, F32),
        in_specs=[VMEM] * 5,
        out_specs=VMEM,
        compiler_params=params(8),
    )(query, bias, sums, partner, neighbour)


def project_term(attended, wo_ref, rows, first, outs):
    for start in range(0, outs[0].shape[1], OUT_BLOCK):
        term = jnp.dot(
            attended[rows, :], wo_ref[:, first + start : first + start + OUT_BLOCK], preferred_element_type=F32
        ).astype(BF16)
        height = outs[0].shape[0]
        for i, out_ref in enumerate(outs):
            out_ref[:, start : start + OUT_BLOCK] = term[i * height : (i + 1) * height]


def attend_project(query, bias, sums, partner, neighbour, wo, both, width):
    tokens = query.shape[0]
    half = tokens // 2

    def kernel(query_ref, bias_ref, sums_ref, partner_ref, neighbour_ref, wo_ref, attended, *outs):
        for first in range(0, query_ref.shape[1], LANES):
            columns = slice(first, first + LANES)
            top, bottom = pair_parts(query_ref, partner_ref, neighbour_ref, bias_ref[2], columns)
            top = top + sums_ref[0, :, columns]
            bottom = bottom + sums_ref[1, :, columns]
            attended[:, columns] = (top / bottom).astype(BF16)
        project_term(attended, wo_ref, slice(0 if both else half, tokens), 0, outs)

    out = jax.ShapeDtypeStruct((half, width), BF16)
    return pl.pallas_call(
        kernel,
        out_shape=(jax.ShapeDtypeStruct(query.shape, BF16), *[out] * (1 + both)),
        in_specs=[VMEM] * 6,
        out_specs=(VMEM,) * (2 + both),
        compiler_params=params(8),
    )(query, bias, sums, partner, neighbour, wo)


def more_term(attended, wo, both, first, width):
    tokens = attended.shape[0]
    half = tokens // 2

    def kernel(attended_ref, wo_ref, *outs):
        project_term(attended_ref, wo_ref, slice(0, tokens if both else half), first, outs)

    out = jax.ShapeDtypeStruct((half, width), BF16)
    return pl.pallas_call(
        kernel,
        out_shape=(out,) * (1 + both),
        in_specs=[VMEM, VMEM],
        out_specs=(VMEM,) * (1 + both),
        compiler_params=params(8),
    )(attended, wo)


def last_update(state, first, kept, received, fresh_noise, levels, entry, step_size):
    step = ITERS - 1
    width = kept.shape[1]

    def kernel(levels_ref, entry_ref, size_ref, state_ref, kept_ref, received_ref, noise_ref, out_ref, sem):
        velocity = kept_ref[...].astype(F32) + received_ref[...].astype(F32)
        size = size_ref[levels_ref[slot_of(step)]]
        out_ref[...] = (state_ref[:, first : first + width].astype(F32) + size * velocity).astype(BF16)

        @pl.when(slot_of(step + 1) == entry_ref[step])
        def _():
            copy = pltpu.make_async_copy(noise_ref.at[step, :, pl.ds(first, width)], out_ref, sem)
            copy.start()
            copy.wait()

    return pl.pallas_call(
        kernel,
        out_shape=jax.ShapeDtypeStruct(kept.shape, BF16),
        in_specs=[SMEM, SMEM, SMEM, VMEM, VMEM, VMEM, HBM],
        out_specs=VMEM,
        scratch_shapes=[pltpu.SemaphoreType.DMA(())],
        compiler_params=params(8),
    )(levels, entry, step_size, state, kept, received, *in_hbm(fresh_noise))


def exchanged(step, partner, block):
    count = lax.axis_size("queue")
    pairs = []
    for i in range(0 if partner else 1, count, 2):
        if (i + step) % count != count - 1:
            pairs += [(i, (i + 1) % count), ((i + 1) % count, i)]
    return lax.ppermute(block, "queue", pairs)


def on_device(
    latents, fresh_noise, levels, pattern, entry, level_scale, level_shift, step_size, qk_gain, wq, wk, wv, wo
):
    count = lax.axis_size("queue")
    state = latents[0]
    depth = state.shape[1]
    for step in range(ITERS):
        if step == 0:
            mine, own, rows, wk, wv = first_half(state, levels, level_scale, level_shift, qk_gain, wk, wv)
        else:
            state, mine, own = next_half(
                step, state, kept, received, fresh_noise, rows, qk_gain, wk, wv, levels, entry, step_size
            )
        other = swap_cores(mine)
        neighbour = exchanged(step, False, own)
        other, own = lax.optimization_barrier((other, own))
        theirs = exchanged(step, True, own), neighbour
        own_other, *loaded = other_half(other, qk_gain, wk, wv, wq if step == 0 else None)
        if loaded:
            wq = loaded[0]
        theirs_other = exchanged(step, True, own_other), exchanged(step, False, own_other)
        query, bias, sums, *loaded = queries(
            step, mine, other, qk_gain, wq, pattern, own, own_other, wo if step == 0 else None
        )
        if loaded:
            wo = loaded[0]
        sums = attend(query, bias, sums, *theirs)
        if step < ITERS - 1:
            attended, sent = attend_project(query, bias, sums, *theirs_other, wo, False, depth)
            received = swap_cores(sent)
            (kept,) = more_term(attended, wo, False, 0, depth)
    width = depth // LAST_COLUMNS
    attended, *terms = attend_project(query, bias, sums, *theirs_other, wo, True, width)
    route = [(i, (i + ITERS) % count) for i in range(count)]
    result = []
    for first in range(0, depth, width):
        if first > 0:
            terms = more_term(attended, wo, True, first, width)
        part = last_update(state, first, terms[0], swap_cores(terms[1]), fresh_noise, levels, entry, step_size)
        result.append(lax.ppermute(part, "queue", route))
    return jnp.concatenate(result, axis=1)[None]


def solution(mesh):
    return jax.shard_map(
        on_device,
        mesh=mesh,
        in_specs=(
            P("queue", "seq", None),
            P(None, "seq", None),
            P(),
            P(),
            P(),
            P(),
            P(),
            P(),
            P(),
            P(None, "seq"),
            P(None, "seq"),
            P(None, "seq"),
            P("seq", None),
        ),
        out_specs=P("queue", "seq", None),
        check_vma=False,
    )
```

time: 203 us -> 100 us (0.49)
  matrix products: 69.4 us -> 0 us
  Pallas kernels: 0 us -> 33.4 us
  waiting for transfers between devices: 68.3 us -> 41 us
  local copies, waits for them, and re-layouts: 21.1 us -> 0.03 us
  other arithmetic: 19.9 us -> 0.96 us
  starting transfers between devices: 17.3 us -> 23.9 us
  between operations: 5.66 us -> 0.23 us
    dot_general x56 -> x0, matrix products: 69.4 us -> none  [the longest x24 30.8 us: one_head(): jnp.dot(query_head, key_head.T, preferred_element_type=jnp.float32) * scale]
    pallas_call x0 -> x14, Pallas kernels: none -> 33.4 us  [the longest x2 10 us: queries(): pl.pallas_call(kernel, out_shape=out_shape, in_specs=[SMEM] + [VMEM] * 6...]
    ppermute x5 -> x10, waiting for transfers between devices: 65.1 us -> 37.8 us  [the longest x2 23.2 us: on_device(): result.append(lax.ppermute(part, 'queue', route))]
    reduce_sum x30 -> x0, other arithmetic: 11 us -> none  [the longest x24 6.73 us: one_head(): jnp.sum(expo, axis=-1, keepdims=True)]
    reshape x30 -> x0, local copies, waits for them, and re-layouts: 7.23 us -> none  [the longest x24 6.7 us: on_device(): jnp.repeat(jnp.repeat(table, per_frame, axis=0), per_frame, axis=1)]
    ppermute x5 -> x10, starting transfers between devices: 10.2 us -> 17.1 us  [the longest x8 17 us: exchanged(): return lax.ppermute(block, 'queue', pairs)]
    slice x9 -> x0, local copies, waits for them, and re-layouts: 5.22 us -> none  [the longest x2 2.93 us: on_device(): window[0]]
    convert_element_type x4 -> x0, other arithmetic: 3.2 us -> none  [the longest x2 1.73 us: modulate(): return (normed * (1.0 + scale_row) + shift_row).astype(jnp.bfloat16)]
  transfers between devices with their start and end apart: 9 -> 15, of which waited for: 9 -> 10; matrix products, arithmetic and copies ran while one was open for 5% -> 0% of each run, Pallas kernels for 0% -> 20%
where the time goes in v5:
time: 100 us; the launch traced here: 99.5 us
  waiting for transfers between devices  41 us (41%)
  Pallas kernels  33.4 us (33%)
  starting transfers between devices  23.9 us (24%)
    ppermute x2, waiting for transfers between devices, on_device(): result.append(lax.ppermute(part, 'queue', route))  23.2 us
    ppermute x8, starting transfers between devices, exchanged(): return lax.ppermute(block, 'queue', pairs)  17 us
    ppermute x8, waiting for transfers between devices, exchanged(): return lax.ppermute(block, 'queue', pairs)  14.5 us
    pallas_call x2, Pallas kernels, queries(): pl.pallas_call(kernel, out_shape=out_shape, in_specs=[SMEM] + [VMEM] * 6...  10 us
    ppermute x5, starting transfers between devices, swap_cores(): return lax.ppermute(block, 'seq', [(0, 1), (1, 0)])  6.71 us
    pallas_call x1, Pallas kernels, first_half(): pl.pallas_call(kernel, out_shape=(jax.ShapeDtypeStruct((half, depth), BF1...  6.64 us
    pallas_call x2, Pallas kernels, other_half(): pl.pallas_call(kernel, out_shape=(out, jax.ShapeDtypeStruct(wq.shape, BF1...  4.3 us
    pallas_call x2, Pallas kernels, attend_project(): pl.pallas_call(kernel, out_shape=(jax.ShapeDtypeStruct(query.shape, BF16)...  3.84 us
  transfers between devices with their start and end apart: 15, of which 10 were waited for; matrix products, arithmetic and copies ran while one was open for 0% of the time, Pallas kernels for 20%

profile of v5, /device:TPU:1, one launch (start us, length us, event | category | flops | bytes accessed | tf_op | source)
XLA Modules:
  0.0 99.5 jit_solution(12006985112773346790)
XLA Ops:
  0.0 6.6 %shard_map.127 = (bf16[128,3072]{1,0:T(8,128)(2,1)S(1)}, bf16[2,128,768]{2,1,0:T(8,128)(2,1)S(1)}, f32[2,2,3072]{2,1,0:T(2,128)S(1)}, bf16[3072,768]{1,0:T(8,128)(2,1)S(1)}, bf16[3072,768]{1,0:T(8,128)(2,1)S(1)}) custom-call(s32[128]{0:T(128)} %levels_ref.7, f32[50,3072]{1,0:T(8,128)} %scale_ref.1, f32[50,3072]{1,0:T(8,128)} %shift_ref.1, ...), custom_call_target="tpu_custom_call" | custom-call | tf_op jit(solution)/shard_map/pallas_call | solution.py:131
  6.7 3.3 %collective-permute-start = (bf16[128,3072]{1,0:T(8,128)(2,1)S(1)}, bf16[128,3072]{1,0:T(8,128)(2,1)S(1)}, u32[]{:S(2)}, u32[]{:S(2)}) collective-permute-start(bf16[128,3072]{1,0:T(8,128)(2,1)S(1)} %get-tuple-element.33.mine_ref), channel_id=1, source_target_pairs={{0,1},{1,0},{2,3},{3,2},{4,5},{5,4},{6,7},{7,6},{8,9},{9,8},{10,11... | collective-permute-start | bytes 2359304 | tf_op jit(solution)/shard_map/ppermute | solution.py:29
  10.0 0.7 collective-permute-start.2
  10.7 1.2 %collective-permute-done.modulated_ref.other_ref = bf16[128,3072]{1,0:T(8,128)(2,1)S(1)} collective-permute-done((bf16[128,3072]{1,0:T(8,128)(2,1)S(1)}, bf16[128,3072]{1,0:T(8,128)(2,1)S(1)}, u32[]{:S(2)}, u32[]{:S(2)}) %collective-permute-start) | collective-permute-done | bytes 786464 | tf_op jit(solution)/shard_map/ppermute | solution.py:29
  11.9 0.8 collective-permute-start.1
  12.7 2.4 %shard_map.128 = (bf16[2,128,768]{2,1,0:T(8,128)(2,1)S(1)}, bf16[3072,768]{1,0:T(8,128)(2,1)S(1)}) custom-call(bf16[128,3072]{1,0:T(8,128)(2,1)S(1)} %collective-permute-done.modulated_ref.other_ref, f32[2,64]{1,0:T(2,128)S(1)} %copy-done.1, bf16[3072,768]{1,0:T(8,128)(2,1)S(1)} %get-tuple-element.36.wk_ref, bf16[3072,768]{1,0:T(8,128)(2,1)S(1)} %get-tuple-element.37.wv_ref, ...), custom_call_target="tpu_custom_call" | custom-call | tf_op jit(solution)/shard_map/pallas_call | solution.py:201
  15.0 0.8 collective-permute-start.3
  16.5 6.0 %shard_map.129 = (bf16[256,768]{1,0:T(8,128)(2,1)S(1)}, bf16[3,256,128]{2,1,0:T(8,128)(2,1)S(1)}, f32[2,256,768]{2,1,0:T(8,128)S(1)}, bf16[768,3072]{1,0:T(8,128)(2,1)S(1)}) custom-call(s32[4,12]{1,0:T(4,128)S(1)} %copy-done.2, f32[2,64]{1,0:T(2,128)S(1)} %copy-done.1, bf16[128,3072]{1,0:T(8,128)(2,1)S(1)} %get-tuple-element.33.mine_ref, ...), custom_call_target="tpu_custom_call" | custom-call | tf_op jit(solution)/shard_map/pallas_call | solution.py:269
  22.6 1.3 %shard_map.130.sums_ref = f32[2,256,768]{2,1,0:T(8,128)S(1)} custom-call(bf16[256,768]{1,0:T(8,128)(2,1)S(1)} %get-tuple-element.41.query_ref, bf16[3,256,128]{2,1,0:T(8,128)(2,1)S(1)} %get-tuple-element.42.bias_ref, f32[2,256,768]{2,1,0:T(8,128)S(1)} %get-tuple-element.43.sums_ref, bf16[2,128,768]{2,1,0:T(8,128)(2,1)S(1)} %collective-permute-done.1.partner_ref, ...), custom_call_target="tpu_custom_call" | custom-call | tf_op jit(solution)/shard_map/pallas_call | solution.py:287
  23.9 6.8 %collective-permute-done.3.partner_ref = bf16[2,128,768]{2,1,0:T(8,128)(2,1)S(1)} collective-permute-done((bf16[2,128,768]{2,1,0:T(8,128)(2,1)S(1)}, bf16[2,128,768]{2,1,0:T(8,128)(2,1)S(1)}, u32[]{:S(2)}, u32[]{:S(2)}) %collective-permute-start.3) | collective-permute-done | bytes 393248 | tf_op jit(solution)/shard_map/ppermute | solution.py:377
  30.6 2.0 %shard_map.131 = (bf16[256,768]{1,0:T(8,128)(2,1)S(1)}, bf16[128,3072]{1,0:T(8,128)(2,1)S(1)}) custom-call(bf16[256,768]{1,0:T(8,128)(2,1)S(1)} %get-tuple-element.41.query_ref, bf16[3,256,128]{2,1,0:T(8,128)(2,1)S(1)} %get-tuple-element.42.bias_ref, f32[2,256,768]{2,1,0:T(8,128)S(1)} %shard_map.130.sums_ref, ...), custom_call_target="tpu_custom_call" | custom-call | tf_op jit(solution)/shard_map/pallas_call | solution.py:320
  32.7 1.5 %collective-permute-start.5 = (bf16[128,3072]{1,0:T(8,128)(2,1)S(1)}, bf16[128,3072]{1,0:T(8,128)(2,1)S(1)}, u32[]{:S(2)}, u32[]{:S(2)}) collective-permute-start(bf16[128,3072]{1,0:T(8,128)(2,1)S(1)} %get-tuple-element.46), channel_id=1, source_target_pairs={{0,1},{1,0},{2,3},{3,2},{4,5},{5,4},{6,7},{7,6},{8,9},{9,8},{10,11... | collective-permute-start | bytes 2359304 | tf_op jit(solution)/shard_map/ppermute | solution.py:29
  34.1 0.8 shard_map.132.kept_ref
  34.9 1.1 %collective-permute-done.5.received_ref = bf16[128,3072]{1,0:T(8,128)(2,1)S(1)} collective-permute-done((bf16[128,3072]{1,0:T(8,128)(2,1)S(1)}, bf16[128,3072]{1,0:T(8,128)(2,1)S(1)}, u32[]{:S(2)}, u32[]{:S(2)}) %collective-permute-start.5) | collective-permute-done | bytes 786464 | tf_op jit(solution)/shard_map/ppermute | solution.py:29
  36.1 3.1 %shard_map.133 = (bf16[128,3072]{1,0:T(8,128)(2,1)S(1)}, bf16[128,3072]{1,0:T(8,128)(2,1)S(1)}, bf16[2,128,768]{2,1,0:T(8,128)(2,1)S(1)}) custom-call(s32[128]{0:T(128)S(1)} %copy-done.3, s32[2]{0:T(128)S(1)} %copy-done.4, f32[50]{0:T(128)S(1)} %copy-done.5, bf16[128,3072]{1,0:T(8,128)(2,1)S(1)} %bitcast.4, bf16[128,3072]{1,0:T(8,128)(2,1)S(1)} %shard_map.132.kept_ref, ...), custom_call_target="tpu_custom_call" | custom-call | tf_op jit(solution)/shard_map/pallas_call | solution.py:172
  39.6 8.5 %collective-permute-start.8 = (bf16[2,128,768]{2,1,0:T(8,128)(2,1)S(1)}, bf16[2,128,768]{2,1,0:T(8,128)(2,1)S(1)}, u32[]{:S(2)}, u32[]{:S(2)}) collective-permute-start(bf16[2,128,768]{2,1,0:T(8,128)(2,1)S(1)} %get-tuple-element.52.own_ref), channel_id=1, source_target_pairs={{2,4},{4,2},{6,8},{8,6},{10,12},{12,10},{14,16},{16,14},{18,20},{2... | collective-permute-start | bytes 1179656 | tf_op jit(solution)/shard_map/ppermute | solution.py:377
  48.1 1.9 %collective-permute-start.7 = (bf16[2,128,768]{2,1,0:T(8,128)(2,1)S(1)}, bf16[2,128,768]{2,1,0:T(8,128)(2,1)S(1)}, u32[]{:S(2)}, u32[]{:S(2)}) collective-permute-start(bf16[2,128,768]{2,1,0:T(8,128)(2,1)S(1)} %get-tuple-element.52.own_ref), channel_id=1, source_target_pairs={{0,2},{2,0},{4,6},{6,4},{8,10},{10,8},{12,14},{14,12},{16,18},{18,... | collective-permute-start | bytes 1179656 | tf_op jit(solution)/shard_map/ppermute | solution.py:377
  50.0 1.9 %shard_map.134.own_other_ref = bf16[2,128,768]{2,1,0:T(8,128)(2,1)S(1)} custom-call(bf16[128,3072]{1,0:T(8,128)(2,1)S(1)} %collective-permute-done.6.modulated_ref.other_ref, f32[2,64]{1,0:T(2,128)S(1)} %copy-done.1, bf16[3072,768]{1,0:T(8,128)(2,1)S(1)} %get-tuple-element.36.wk_ref, bf16[3072,768]{1,0:T(8,128)(2,1)S(1)} %get-tuple-element.37.wv_ref), custom_call_target="tpu_custom_call" | custom-call | tf_op jit(solution)/shard_map/pallas_call | solution.py:201
  51.9 0.8 collective-permute-start.10
  52.7 2.9 %collective-permute-start.9 = (bf16[2,128,768]{2,1,0:T(8,128)(2,1)S(1)}, bf16[2,128,768]{2,1,0:T(8,128)(2,1)S(1)}, u32[]{:S(2)}, u32[]{:S(2)}) collective-permute-start(bf16[2,128,768]{2,1,0:T(8,128)(2,1)S(1)} %shard_map.134.own_other_ref), channel_id=1, source_target_pairs={{0,2},{2,0},{4,6},{6,4},{8,10},{10,8},{12,14},{14,12},{16,18},{18,... | collective-permute-start | bytes 1179656 | tf_op jit(solution)/shard_map/ppermute | solution.py:377
  55.6 4.0 %shard_map.135 = (bf16[256,768]{1,0:T(8,128)(2,1)S(1)}, bf16[3,256,128]{2,1,0:T(8,128)(2,1)S(1)}, f32[2,256,768]{2,1,0:T(8,128)S(1)}) custom-call(s32[4,12]{1,0:T(4,128)S(1)} %copy-done.2, f32[2,64]{1,0:T(2,128)S(1)} %copy-done.1, bf16[128,3072]{1,0:T(8,128)(2,1)S(1)} %get-tuple-element.49.mine_ref, ...), custom_call_target="tpu_custom_call" | custom-call | tf_op jit(solution)/shard_map/pallas_call | solution.py:269
  60.2 1.3 %shard_map.136.sums_ref = f32[2,256,768]{2,1,0:T(8,128)S(1)} custom-call(bf16[256,768]{1,0:T(8,128)(2,1)S(1)} %get-tuple-element.53.query_ref, bf16[3,256,128]{2,1,0:T(8,128)(2,1)S(1)} %get-tuple-element.54.bias_ref, f32[2,256,768]{2,1,0:T(8,128)S(1)} %get-tuple-element.55.sums_ref, bf16[2,128,768]{2,1,0:T(8,128)(2,1)S(1)} %collective-permute-done.7.partner_ref, ...), custom_call_target="tpu_custom_call" | custom-call | tf_op jit(solution)/shard_map/pallas_call | solution.py:287
  61.5 6.2 %collective-permute-done.10.neighbour_ref = bf16[2,128,768]{2,1,0:T(8,128)(2,1)S(1)} collective-permute-done((bf16[2,128,768]{2,1,0:T(8,128)(2,1)S(1)}, bf16[2,128,768]{2,1,0:T(8,128)(2,1)S(1)}, u32[]{:S(2)}, u32[]{:S(2)}) %collective-permute-start.10) | collective-permute-done | bytes 393248 | tf_op jit(solution)/shard_map/ppermute | solution.py:377
  67.7 0.9 collective-permute-done.9.partner_ref
  68.7 1.9 %shard_map.137 = (bf16[256,768]{1,0:T(8,128)(2,1)S(1)}, bf16[128,1536]{1,0:T(8,128)(2,1)S(1)}, bf16[128,1536]{1,0:T(8,128)(2,1)S(1)}) custom-call(bf16[256,768]{1,0:T(8,128)(2,1)S(1)} %get-tuple-element.53.query_ref, bf16[3,256,128]{2,1,0:T(8,128)(2,1)S(1)} %get-tuple-element.54.bias_ref, f32[2,256,768]{2,1,0:T(8,128)S(1)} %shard_map.136.sums_ref, ...), custom_call_target="tpu_custom_call" | custom-call | tf_op jit(solution)/shard_map/pallas_call | solution.py:320
  70.5 1.4 %collective-permute-start.11 = (bf16[128,1536]{1,0:T(8,128)(2,1)S(1)}, bf16[128,1536]{1,0:T(8,128)(2,1)S(1)}, u32[]{:S(2)}, u32[]{:S(2)}) collective-permute-start(bf16[128,1536]{1,0:T(8,128)(2,1)S(1)} %get-tuple-element.57), channel_id=1, source_target_pairs={{0,1},{1,0},{2,3},{3,2},{4,5},{5,4},{6,7},{7,6},{8,9},{9,8},{10,11... | collective-permute-start | bytes 1179656 | tf_op jit(solution)/shard_map/ppermute | solution.py:29
  71.9 0.8 shard_map.139
  73.2 0.7 shard_map.138
  74.5 0.7 shard_map.140
  75.3 14.8 %collective-permute-done.12 = bf16[128,1536]{1,0:T(8,128)(2,1)S(1)} collective-permute-done((bf16[128,1536]{1,0:T(8,128)(2,1)S(1)}, bf16[128,1536]{1,0:T(8,128)(2,1)S(1)}, u32[]{:S(2)}, u32[]{:S(2)}) %collective-permute-start.12) | collective-permute-done | bytes 393248 | tf_op jit(solution)/shard_map/ppermute | solution.py:419
  90.1 8.4 %collective-permute-done.14 = bf16[128,1536]{1,0:T(8,128)(2,1)S(1)} collective-permute-done((bf16[128,1536]{1,0:T(8,128)(2,1)S(1)}, bf16[128,1536]{1,0:T(8,128)(2,1)S(1)}, u32[]{:S(2)}, u32[]{:S(2)}) %collective-permute-start.14) | collective-permute-done | bytes 393248 | tf_op jit(solution)/shard_map/ppermute | solution.py:419
  98.5 1.0 maximum_bitcast_fusion
  (25 shorter events, 2.9 us)
Async XLA Ops:
  0.0 12.7 %copy-start.1 = (f32[2,64]{1,0:T(2,128)S(1)}, f32[2,64]{1,0:T(2,128)}, u32[]{:S(2)}) copy-start(f32[2,64]{1,0:T(2,128)} %gain_ref.9) | copy-start | bytes 1540
  6.7 5.2 %collective-permute-start = (bf16[128,3072]{1,0:T(8,128)(2,1)S(1)}, bf16[128,3072]{1,0:T(8,128)(2,1)S(1)}, u32[]{:S(2)}, u32[]{:S(2)}) collective-permute-start(bf16[128,3072]{1,0:T(8,128)(2,1)S(1)} %get-tuple-element.33.mine_ref), channel_id=1, source_target_pairs={{0,1},{1,0},{2,3},{3,2},{4,5},{5,4},{6,7},{7,6},{8,9},{9,8},{10,11... | collective-permute-start | bytes 2359304 | tf_op jit(solution)/shard_map/ppermute | solution.py:29
  10.0 12.6 %collective-permute-start.2 = (bf16[2,128,768]{2,1,0:T(8,128)(2,1)S(1)}, bf16[2,128,768]{2,1,0:T(8,128)(2,1)S(1)}, u32[]{:S(2)}, u32[]{:S(2)}) collective-permute-start(bf16[2,128,768]{2,1,0:T(8,128)(2,1)S(1)} %get-tuple-element.39.own_ref), channel_id=1, source_target_pairs={{2,4},{4,2},{6,8},{8,6},{10,12},{12,10},{14,16},{16,14},{18,20},{2... | collective-permute-start | bytes 1179656 | tf_op jit(solution)/shard_map/ppermute | solution.py:377
  11.9 10.7 %collective-permute-start.1 = (bf16[2,128,768]{2,1,0:T(8,128)(2,1)S(1)}, bf16[2,128,768]{2,1,0:T(8,128)(2,1)S(1)}, u32[]{:S(2)}, u32[]{:S(2)}) collective-permute-start(bf16[2,128,768]{2,1,0:T(8,128)(2,1)S(1)} %get-tuple-element.39.own_ref), channel_id=1, source_target_pairs={{0,2},{2,0},{4,6},{6,4},{8,10},{10,8},{12,14},{14,12},{16,18},{18,... | collective-permute-start | bytes 1179656 | tf_op jit(solution)/shard_map/ppermute | solution.py:377
  12.7 3.8 %copy-start.2 = (s32[4,12]{1,0:T(4,128)S(1)}, s32[4,12]{1,0:T(4,128)}, u32[]{:S(2)}) copy-start(s32[4,12]{1,0:T(4,128)} %pattern_ref.3) | copy-start | bytes 580
  15.0 15.6 %collective-permute-start.3 = (bf16[2,128,768]{2,1,0:T(8,128)(2,1)S(1)}, bf16[2,128,768]{2,1,0:T(8,128)(2,1)S(1)}, u32[]{:S(2)}, u32[]{:S(2)}) collective-permute-start(bf16[2,128,768]{2,1,0:T(8,128)(2,1)S(1)} %get-tuple-element.40.own_other_ref), channel_id=1, source_target_pairs={{0,2},{2,0},{4,6},{6,4},{8,10},{10,8},{12,14},{14,12},{16,18},{18,... | collective-permute-start | bytes 1179656 | tf_op jit(solution)/shard_map/ppermute | solution.py:377
  15.8 14.8 %collective-permute-start.4 = (bf16[2,128,768]{2,1,0:T(8,128)(2,1)S(1)}, bf16[2,128,768]{2,1,0:T(8,128)(2,1)S(1)}, u32[]{:S(2)}, u32[]{:S(2)}) collective-permute-start(bf16[2,128,768]{2,1,0:T(8,128)(2,1)S(1)} %get-tuple-element.40.own_other_ref), channel_id=1, source_target_pairs={{2,4},{4,2},{6,8},{8,6},{10,12},{12,10},{14,16},{16,14},{18,20},{2... | collective-permute-start | bytes 1179656 | tf_op jit(solution)/shard_map/ppermute | solution.py:377
  32.6 3.4 %copy-start = (bf16[1,128,3072]{2,1,0:T(8,128)(2,1)S(1)}, bf16[1,128,3072]{2,1,0:T(8,128)(2,1)}, u32[]{:S(2)}) copy-start(bf16[1,128,3072]{2,1,0:T(8,128)(2,1)} %param.13) | copy-start | bytes 2359300
  32.6 3.4 %copy-start.3 = (s32[128]{0:T(128)S(1)}, s32[128]{0:T(128)}, u32[]{:S(2)}) copy-start(s32[128]{0:T(128)} %levels_ref.7) | copy-start | bytes 1540
  32.6 3.4 %copy-start.4 = (s32[2]{0:T(128)S(1)}, s32[2]{0:T(128)}, u32[]{:S(2)}) copy-start(s32[2]{0:T(128)} %entry_ref.5) | copy-start | bytes 28
  32.7 3.4 %copy-start.5 = (f32[50]{0:T(128)S(1)}, f32[50]{0:T(128)}, u32[]{:S(2)}) copy-start(f32[50]{0:T(128)} %size_ref.5) | copy-start | bytes 604
  32.7 3.4 %collective-permute-start.5 = (bf16[128,3072]{1,0:T(8,128)(2,1)S(1)}, bf16[128,3072]{1,0:T(8,128)(2,1)S(1)}, u32[]{:S(2)}, u32[]{:S(2)}) collective-permute-start(bf16[128,3072]{1,0:T(8,128)(2,1)S(1)} %get-tuple-element.46), channel_id=1, source_target_pairs={{0,1},{1,0},{2,3},{3,2},{4,5},{5,4},{6,7},{7,6},{8,9},{9,8},{10,11... | collective-permute-start | bytes 2359304 | tf_op jit(solution)/shard_map/ppermute | solution.py:29
  39.1 9.0 %collective-permute-start.6 = (bf16[128,3072]{1,0:T(8,128)(2,1)S(1)}, bf16[128,3072]{1,0:T(8,128)(2,1)S(1)}, u32[]{:S(2)}, u32[]{:S(2)}) collective-permute-start(bf16[128,3072]{1,0:T(8,128)(2,1)S(1)} %get-tuple-element.49.mine_ref), channel_id=1, source_target_pairs={{0,1},{1,0},{2,3},{3,2},{4,5},{5,4},{6,7},{7,6},{8,9},{9,8},{10,11... | collective-permute-start | bytes 2359304 | tf_op jit(solution)/shard_map/ppermute | solution.py:29
  39.6 20.0 %collective-permute-start.8 = (bf16[2,128,768]{2,1,0:T(8,128)(2,1)S(1)}, bf16[2,128,768]{2,1,0:T(8,128)(2,1)S(1)}, u32[]{:S(2)}, u32[]{:S(2)}) collective-permute-start(bf16[2,128,768]{2,1,0:T(8,128)(2,1)S(1)} %get-tuple-element.52.own_ref), channel_id=1, source_target_pairs={{2,4},{4,2},{6,8},{8,6},{10,12},{12,10},{14,16},{16,14},{18,20},{2... | collective-permute-start | bytes 1179656 | tf_op jit(solution)/shard_map/ppermute | solution.py:377
  48.1 12.1 %collective-permute-start.7 = (bf16[2,128,768]{2,1,0:T(8,128)(2,1)S(1)}, bf16[2,128,768]{2,1,0:T(8,128)(2,1)S(1)}, u32[]{:S(2)}, u32[]{:S(2)}) collective-permute-start(bf16[2,128,768]{2,1,0:T(8,128)(2,1)S(1)} %get-tuple-element.52.own_ref), channel_id=1, source_target_pairs={{0,2},{2,0},{4,6},{6,4},{8,10},{10,8},{12,14},{14,12},{16,18},{18,... | collective-permute-start | bytes 1179656 | tf_op jit(solution)/shard_map/ppermute | solution.py:377
  51.9 15.8 %collective-permute-start.10 = (bf16[2,128,768]{2,1,0:T(8,128)(2,1)S(1)}, bf16[2,128,768]{2,1,0:T(8,128)(2,1)S(1)}, u32[]{:S(2)}, u32[]{:S(2)}) collective-permute-start(bf16[2,128,768]{2,1,0:T(8,128)(2,1)S(1)} %shard_map.134.own_other_ref), channel_id=1, source_target_pairs={{2,4},{4,2},{6,8},{8,6},{10,12},{12,10},{14,16},{16,14},{18,20},{2... | collective-permute-start | bytes 1179656 | tf_op jit(solution)/shard_map/ppermute | solution.py:377
  52.7 16.0 %collective-permute-start.9 = (bf16[2,128,768]{2,1,0:T(8,128)(2,1)S(1)}, bf16[2,128,768]{2,1,0:T(8,128)(2,1)S(1)}, u32[]{:S(2)}, u32[]{:S(2)}) collective-permute-start(bf16[2,128,768]{2,1,0:T(8,128)(2,1)S(1)} %shard_map.134.own_other_ref), channel_id=1, source_target_pairs={{0,2},{2,0},{4,6},{6,4},{8,10},{10,8},{12,14},{14,12},{16,18},{18,... | collective-permute-start | bytes 1179656 | tf_op jit(solution)/shard_map/ppermute | solution.py:377
  70.5 2.7 %collective-permute-start.11 = (bf16[128,1536]{1,0:T(8,128)(2,1)S(1)}, bf16[128,1536]{1,0:T(8,128)(2,1)S(1)}, u32[]{:S(2)}, u32[]{:S(2)}) collective-permute-start(bf16[128,1536]{1,0:T(8,128)(2,1)S(1)} %get-tuple-element.57), channel_id=1, source_target_pairs={{0,1},{1,0},{2,3},{3,2},{4,5},{5,4},{6,7},{7,6},{8,9},{9,8},{10,11... | collective-permute-start | bytes 1179656 | tf_op jit(solution)/shard_map/ppermute | solution.py:29
  72.7 1.8 %collective-permute-start.13 = (bf16[128,1536]{1,0:T(8,128)(2,1)S(1)}, bf16[128,1536]{1,0:T(8,128)(2,1)S(1)}, u32[]{:S(2)}, u32[]{:S(2)}) collective-permute-start(bf16[128,1536]{1,0:T(8,128)(2,1)S(1)} %get-tuple-element.60), channel_id=1, source_target_pairs={{0,1},{1,0},{2,3},{3,2},{4,5},{5,4},{6,7},{7,6},{8,9},{9,8},{10,11... | collective-permute-start | bytes 1179656 | tf_op jit(solution)/shard_map/ppermute | solution.py:29
  74.0 16.1 %collective-permute-start.12 = (bf16[128,1536]{1,0:T(8,128)(2,1)S(1)}, bf16[128,1536]{1,0:T(8,128)(2,1)S(1)}, u32[]{:S(2)}, u32[]{:S(2)}) collective-permute-start(bf16[128,1536]{1,0:T(8,128)(2,1)S(1)} %shard_map.138), channel_id=1, source_target_pairs={{0,4},{2,6},{4,8},{6,10},{8,12},{10,14},{12,16},{14,18},{16,20},{1... | collective-permute-start | bytes 1179656 | tf_op jit(solution)/shard_map/ppermute | solution.py:419
  75.2 23.3 %collective-permute-start.14 = (bf16[128,1536]{1,0:T(8,128)(2,1)S(1)}, bf16[128,1536]{1,0:T(8,128)(2,1)S(1)}, u32[]{:S(2)}, u32[]{:S(2)}) collective-permute-start(bf16[128,1536]{1,0:T(8,128)(2,1)S(1)} %shard_map.140), channel_id=1, source_target_pairs={{0,4},{2,6},{4,8},{6,10},{8,12},{10,14},{12,16},{14,18},{16,20},{1... | collective-permute-start | bytes 1179656 | tf_op jit(solution)/shard_map/ppermute | solution.py:419

commit v6 on v5

--- a/solution.py
+++ b/solution.py
@@ -109,7 +109,7 @@
             for i, (ref, out) in enumerate(((wk_ref, wk_out), (wv_ref, wv_out)))
             for j, part in enumerate(parts)
         ]
-        for copy in tables + weights[:2]:
+        for copy in tables + weights[:3]:
             copy.start()
         for copy in [first] + tables:
             copy.wait()
@@ -122,8 +122,8 @@
             total = None
             for j, part in enumerate(parts):
                 weights[2 * i + j].wait()
-                if i == 0:
-                    weights[2 + j].start()
+                if i == 0 and j == 0:
+                    weights[3].start()
                 product = jnp.dot(modulated_ref[:, part], weight[part, :], preferred_element_type=F32)
                 total = product if total is None else total + product
             out_ref[i] = head_normed(total, gain_columns(gain_ref, 1)) if i == 0 else total.astype(BF16)
@@ -151,21 +151,20 @@
     )(*in_hbm(levels, level_scale, level_shift, state, qk_gain, wk, wv))
 
 
-def next_half(step, state, kept, received, fresh_noise, rows, qk_gain, wk, wv, levels, entry, step_size):
+def updated(state, kept, received, size_row, fresh_row, noise):
+    velocity = kept.astype(F32) + received.astype(F32)
+    moved = state.astype(F32) + size_row * velocity
+    return jnp.where(jnp.broadcast_to(fresh_row, moved.shape) > 0.5, noise.astype(F32), moved).astype(BF16)
+
+
+def next_half(step, state, kept, received, control, noise, rows, qk_gain, wk, wv):
     half, depth = state.shape
     width = wk.shape[1]
 
-    def kernel(levels_ref, entry_ref, size_ref, state_ref, kept_ref, received_ref, rows_ref, gain_ref, wk_ref, wv_ref, noise_ref, new_ref, modulated_ref, out_ref, sem):
-        size = size_ref[levels_ref[slot_of(step - 1)]]
-        velocity = kept_ref[...].astype(F32) + received_ref[...].astype(F32)
-        new_ref[...] = (state_ref[...].astype(F32) + size * velocity).astype(BF16)
-
-        @pl.when(slot_of(step) == entry_ref[step - 1])
-        def _():
-            copy = pltpu.make_async_copy(noise_ref.at[step - 1], new_ref, sem)
-            copy.start()
-            copy.wait()
-
+    def kernel(state_ref, kept_ref, received_ref, control_ref, noise_ref, rows_ref, gain_ref, wk_ref, wv_ref, new_ref, modulated_ref, out_ref):
+        new_ref[...] = updated(
+            state_ref[...], kept_ref[...], received_ref[...], control_ref[0:1, :], control_ref[1:2, :], noise_ref[...]
+        )
         modulated_ref[...] = modulated_rows(new_ref[...].astype(F32), rows_ref[step, 0:1, :], rows_ref[step, 1:2, :])
         project(modulated_ref[...], gain_ref, wk_ref, wv_ref, out_ref)
 
@@ -176,11 +175,10 @@
             jax.ShapeDtypeStruct((half, depth), BF16),
             jax.ShapeDtypeStruct((2, half, width), BF16),
         ),
-        in_specs=[SMEM] * 3 + [VMEM] * 7 + [HBM],
+        in_specs=[VMEM] * 9,
         out_specs=(VMEM,) * 3,
-        scratch_shapes=[pltpu.SemaphoreType.DMA(())],
-        compiler_params=params(8),
-    )(levels, entry, step_size, state, kept, received, rows, qk_gain, wk, wv, *in_hbm(fresh_noise))
+        compiler_params=params(8),
+    )(state, kept, received, control, noise, rows, qk_gain, wk, wv)
 
 
 def other_half(modulated, qk_gain, wk, wv, wq):
@@ -236,18 +234,23 @@
     return attention_parts(query_ref[:, columns], keys, values, bias)
 
 
-def queries(step, mine, other, qk_gain, wq, pattern, own, own_other, wo):
-    half, _ = mine.shape
+def queries(step, mine, other, qk_gain, wq, pattern, own, own_other, levels, entry, step_size, fresh_noise, wo):
+    half, depth = mine.shape
     tokens, width = 2 * half, wq.shape[1]
     scale = math.log2(math.e) / math.sqrt(HD)
     load = wo is not None
 
-    def kernel(pattern_ref, gain_ref, mine_ref, other_ref, wq_ref, own_ref, own_other_ref, *rest):
-        out_ref, bias_ref, sums_ref = rest[load : load + 3]
-        whole = rest[-1 - load]
+    def kernel(pattern_ref, levels_ref, entry_ref, size_ref, gain_ref, mine_ref, other_ref, wq_ref, own_ref, own_other_ref, noise_hbm, *rest):
+        out_ref, bias_ref, sums_ref, control_ref, noise_ref = rest[load : load + 5]
+        whole, sems = rest[-2:]
+        copies = [pltpu.make_async_copy(noise_hbm.at[step], noise_ref, sems.at[0])]
         if load:
-            copy = pltpu.make_async_copy(rest[0], rest[load + 3], rest[-1])
+            copies.append(pltpu.make_async_copy(rest[0], rest[load + 5], sems.at[1]))
+        for copy in copies:
             copy.start()
+        fresh = slot_of(step + 1) == entry_ref[step]
+        control_ref[0:1, :] = jnp.full((1, depth), size_ref[levels_ref[slot_of(step)]], F32)
+        control_ref[1:2, :] = jnp.full((1, depth), jnp.where(fresh, 1.0, 0.0), F32)
         whole[:half, :] = mine_ref[...]
         whole[half:, :] = other_ref[...]
         window_bias(pattern_ref, bias_ref, slot_of(step), tokens // FRAMES)
@@ -256,24 +259,26 @@
         for first in range(0, width, LANES):
             columns = slice(first, first + LANES)
             sums_ref[0, :, columns], sums_ref[1, :, columns] = pair_parts(out_ref, own_ref, own_other_ref, bias_ref[0], columns)
-        if load:
+        for copy in copies:
             copy.wait()
 
     out_shape = [
         jax.ShapeDtypeStruct((tokens, width), BF16),
         jax.ShapeDtypeStruct((3, tokens, LANES), BF16),
         jax.ShapeDtypeStruct((2, tokens, width), F32),
+        jax.ShapeDtypeStruct((2, depth), F32),
+        jax.ShapeDtypeStruct((half, depth), BF16),
     ]
     if load:
         out_shape.append(jax.ShapeDtypeStruct(wo.shape, BF16))
     return pl.pallas_call(
         kernel,
         out_shape=out_shape,
-        in_specs=[SMEM] + [VMEM] * 6 + [HBM] * load,
-        out_specs=[VMEM] * (3 + load),
-        scratch_shapes=[pltpu.VMEM((tokens, mine.shape[1]), BF16)] + [pltpu.SemaphoreType.DMA(())] * load,
-        compiler_params=params(8),
-    )(pattern, qk_gain, mine, other, wq, own, own_other, *(in_hbm(wo) if load else ()))
+        in_specs=[SMEM] * 4 + [VMEM] * 6 + [HBM] * (1 + load),
+        out_specs=[VMEM] * (5 + load),
+        scratch_shapes=[pltpu.VMEM((tokens, depth), BF16), pltpu.SemaphoreType.DMA((2,))],
+        compiler_params=params(8),
+    )(pattern, levels, entry, step_size, qk_gain, mine, other, wq, own, own_other, *in_hbm(fresh_noise), *(in_hbm(wo) if load else ()))
 
 
 def attend(query, bias, sums, partner, neighbour):
@@ -343,29 +348,26 @@
     )(attended, wo)
 
 
-def last_update(state, first, kept, received, fresh_noise, levels, entry, step_size):
-    step = ITERS - 1
-    width = kept.shape[1]
-
-    def kernel(levels_ref, entry_ref, size_ref, state_ref, kept_ref, received_ref, noise_ref, out_ref, sem):
-        velocity = kept_ref[...].astype(F32) + received_ref[...].astype(F32)
-        size = size_ref[levels_ref[slot_of(step)]]
-        out_ref[...] = (state_ref[:, first : first + width].astype(F32) + size * velocity).astype(BF16)
-
-        @pl.when(slot_of(step + 1) == entry_ref[step])
-        def _():
-            copy = pltpu.make_async_copy(noise_ref.at[step, :, pl.ds(first, width)], out_ref, sem)
-            copy.start()
-            copy.wait()
+def last_update(state, first, kept, received, control, noise):
+    columns = slice(first, first + kept.shape[1])
+
+    def kernel(state_ref, kept_ref, received_ref, control_ref, noise_ref, out_ref):
+        out_ref[...] = updated(
+            state_ref[:, columns],
+            kept_ref[...],
+            received_ref[...],
+            control_ref[0:1, columns],
+            control_ref[1:2, columns],
+            noise_ref[:, columns],
+        )
 
     return pl.pallas_call(
         kernel,
         out_shape=jax.ShapeDtypeStruct(kept.shape, BF16),
-        in_specs=[SMEM, SMEM, SMEM, VMEM, VMEM, VMEM, HBM],
+        in_specs=[VMEM] * 5,
         out_specs=VMEM,
-        scratch_shapes=[pltpu.SemaphoreType.DMA(())],
-        compiler_params=params(8),
-    )(levels, entry, step_size, state, kept, received, *in_hbm(fresh_noise))
+        compiler_params=params(8),
+    )(state, kept, received, control, noise)
 
 
 def exchanged(step, partner, block):
@@ -388,7 +390,7 @@
             mine, own, rows, wk, wv = first_half(state, levels, level_scale, level_shift, qk_gain, wk, wv)
         else:
             state, mine, own = next_half(
-                step, state, kept, received, fresh_noise, rows, qk_gain, wk, wv, levels, entry, step_size
+                step, state, kept, received, control, noise, rows, qk_gain, wk, wv
             )
         other = swap_cores(mine)
         neighbour = exchanged(step, False, own)
@@ -398,8 +400,20 @@
         if loaded:
             wq = loaded[0]
         theirs_other = exchanged(step, True, own_other), exchanged(step, False, own_other)
-        query, bias, sums, *loaded = queries(
-            step, mine, other, qk_gain, wq, pattern, own, own_other, wo if step == 0 else None
+        query, bias, sums, control, noise, *loaded = queries(
+            step,
+            mine,
+            other,
+            qk_gain,
+            wq,
+            pattern,
+            own,
+            own_other,
+            levels,
+            entry,
+            step_size,
+            fresh_noise,
+            wo if step == 0 else None,
         )
         if loaded:
             wo = loaded[0]
@@ -415,7 +429,7 @@
     for first in range(0, depth, width):
         if first > 0:
             terms = more_term(attended, wo, True, first, width)
-        part = last_update(state, first, terms[0], swap_cores(terms[1]), fresh_noise, levels, entry, step_size)
+        part = last_update(state, first, terms[0], swap_cores(terms[1]), control, noise)
         result.append(lax.ppermute(part, "queue", route))
     return jnp.concatenate(result, axis=1)[None]
 

time: 100 us -> 99.2 us (level)
    ppermute x8, waiting for transfers between devices: 14.5 us -> 13.2 us  [exchanged(): return lax.ppermute(block, 'queue', pairs)]
    pallas_call x2, Pallas kernels: 1.47 us -> 0.46 us  [last_update(): pl.pallas_call(kernel, out_shape=jax.ShapeDtypeStruct(kept.shape, BF16),...]
  transfers between devices with their start and end apart: 15 -> 15, of which waited for: 10 -> 9; matrix products, arithmetic and copies ran while one was open for 0% -> 0% of each run, Pallas kernels for 20% -> 20%
where the time goes in v6:
time: 99.2 us; the launch traced here: 98.4 us
  waiting for transfers between devices  40.1 us (40%)
  Pallas kernels  33.2 us (33%)
  starting transfers between devices  23.9 us (24%)
    ppermute x2, waiting for transfers between devices, on_device(): result.append(lax.ppermute(part, 'queue', route))  23.2 us
    ppermute x8, starting transfers between devices, exchanged(): return lax.ppermute(block, 'queue', pairs)  17.2 us
    ppermute x8, waiting for transfers between devices, exchanged(): return lax.ppermute(block, 'queue', pairs)  13.2 us
    pallas_call x2, Pallas kernels, queries(): pl.pallas_call(kernel, out_shape=out_shape, in_specs=[SMEM] * 4 + [VMEM]...  11 us
    ppermute x5, starting transfers between devices, swap_cores(): return lax.ppermute(block, 'seq', [(0, 1), (1, 0)])  6.54 us
    pallas_call x1, Pallas kernels, first_half(): pl.pallas_call(kernel, out_shape=(jax.ShapeDtypeStruct((half, depth), BF1...  6.48 us
    pallas_call x2, Pallas kernels, other_half(): pl.pallas_call(kernel, out_shape=(out, jax.ShapeDtypeStruct(wq.shape, BF1...  4.39 us
    pallas_call x2, Pallas kernels, attend_project(): pl.pallas_call(kernel, out_shape=(jax.ShapeDtypeStruct(query.shape, BF16)...  3.94 us
  transfers between devices with their start and end apart: 15, of which 9 were waited for; matrix products, arithmetic and copies ran while one was open for 0% of the time, Pallas kernels for 20%

profile of v6, /device:TPU:1, one launch (start us, length us, event | category | flops | bytes accessed | tf_op | source)
XLA Modules:
  0.0 98.4 jit_solution(8238853562017553618)
XLA Ops:
  0.0 6.5 %shard_map.127 = (bf16[128,3072]{1,0:T(8,128)(2,1)S(1)}, bf16[2,128,768]{2,1,0:T(8,128)(2,1)S(1)}, f32[2,2,3072]{2,1,0:T(2,128)S(1)}, bf16[3072,768]{1,0:T(8,128)(2,1)S(1)}, bf16[3072,768]{1,0:T(8,128)(2,1)S(1)}) custom-call(s32[128]{0:T(128)} %levels_ref.5, f32[50,3072]{1,0:T(8,128)} %scale_ref.1, f32[50,3072]{1,0:T(8,128)} %shift_ref.1, ...), custom_call_target="tpu_custom_call" | custom-call | tf_op jit(solution)/shard_map/pallas_call | solution.py:131
  6.5 3.3 %collective-permute-start = (bf16[128,3072]{1,0:T(8,128)(2,1)S(1)}, bf16[128,3072]{1,0:T(8,128)(2,1)S(1)}, u32[]{:S(2)}, u32[]{:S(2)}) collective-permute-start(bf16[128,3072]{1,0:T(8,128)(2,1)S(1)} %get-tuple-element.37.mine_ref), channel_id=1, source_target_pairs={{0,1},{1,0},{2,3},{3,2},{4,5},{5,4},{6,7},{7,6},{8,9},{9,8},{10,11... | collective-permute-start | bytes 2359304 | tf_op jit(solution)/shard_map/ppermute | solution.py:29
  9.8 0.7 collective-permute-start.2
  10.5 1.2 %collective-permute-done.modulated_ref.other_ref = bf16[128,3072]{1,0:T(8,128)(2,1)S(1)} collective-permute-done((bf16[128,3072]{1,0:T(8,128)(2,1)S(1)}, bf16[128,3072]{1,0:T(8,128)(2,1)S(1)}, u32[]{:S(2)}, u32[]{:S(2)}) %collective-permute-start) | collective-permute-done | bytes 786464 | tf_op jit(solution)/shard_map/ppermute | solution.py:29
  11.7 0.8 collective-permute-start.1
  12.5 2.4 %shard_map.128 = (bf16[2,128,768]{2,1,0:T(8,128)(2,1)S(1)}, bf16[3072,768]{1,0:T(8,128)(2,1)S(1)}) custom-call(bf16[128,3072]{1,0:T(8,128)(2,1)S(1)} %collective-permute-done.modulated_ref.other_ref, f32[2,64]{1,0:T(2,128)S(1)} %copy-done.1, bf16[3072,768]{1,0:T(8,128)(2,1)S(1)} %get-tuple-element.40.wk_ref, bf16[3072,768]{1,0:T(8,128)(2,1)S(1)} %get-tuple-element.41.wv_ref, ...), custom_call_target="tpu_custom_call" | custom-call | tf_op jit(solution)/shard_map/pallas_call | solution.py:199
  14.9 0.8 collective-permute-start.3
  15.7 0.9 collective-permute-start.4
  16.6 6.1 %shard_map.129 = (bf16[256,768]{1,0:T(8,128)(2,1)S(1)}, bf16[3,256,128]{2,1,0:T(8,128)(2,1)S(1)}, f32[2,256,768]{2,1,0:T(8,128)S(1)}, f32[2,3072]{1,0:T(2,128)S(...) custom-call(s32[4,12]{1,0:T(4,128)S(1)} %copy-done.2, s32[128]{0:T(128)S(1)} %copy-done.3, ...), custom_call_target="tpu_custom_call" | custom-call | tf_op jit(solution)/shard_map/pallas_call | solution.py:274
  22.7 1.3 %shard_map.130.sums_ref = f32[2,256,768]{2,1,0:T(8,128)S(1)} custom-call(bf16[256,768]{1,0:T(8,128)(2,1)S(1)} %get-tuple-element.45.query_ref, bf16[3,256,128]{2,1,0:T(8,128)(2,1)S(1)} %get-tuple-element.46.bias_ref, f32[2,256,768]{2,1,0:T(8,128)S(1)} %get-tuple-element.47.sums_ref, bf16[2,128,768]{2,1,0:T(8,128)(2,1)S(1)} %collective-permute-done.1.partner_ref, ...), custom_call_target="tpu_custom_call" | custom-call | tf_op jit(solution)/shard_map/pallas_call | solution.py:292
  24.0 6.5 %collective-permute-done.3.partner_ref = bf16[2,128,768]{2,1,0:T(8,128)(2,1)S(1)} collective-permute-done((bf16[2,128,768]{2,1,0:T(8,128)(2,1)S(1)}, bf16[2,128,768]{2,1,0:T(8,128)(2,1)S(1)}, u32[]{:S(2)}, u32[]{:S(2)}) %collective-permute-start.3) | collective-permute-done | bytes 393248 | tf_op jit(solution)/shard_map/ppermute | solution.py:379
  30.5 2.0 %shard_map.131 = (bf16[256,768]{1,0:T(8,128)(2,1)S(1)}, bf16[128,3072]{1,0:T(8,128)(2,1)S(1)}) custom-call(bf16[256,768]{1,0:T(8,128)(2,1)S(1)} %get-tuple-element.45.query_ref, bf16[3,256,128]{2,1,0:T(8,128)(2,1)S(1)} %get-tuple-element.46.bias_ref, f32[2,256,768]{2,1,0:T(8,128)S(1)} %shard_map.130.sums_ref, ...), custom_call_target="tpu_custom_call" | custom-call | tf_op jit(solution)/shard_map/pallas_call | solution.py:325
  32.5 1.3 %collective-permute-start.5 = (bf16[128,3072]{1,0:T(8,128)(2,1)S(1)}, bf16[128,3072]{1,0:T(8,128)(2,1)S(1)}, u32[]{:S(2)}, u32[]{:S(2)}) collective-permute-start(bf16[128,3072]{1,0:T(8,128)(2,1)S(1)} %get-tuple-element.50), channel_id=1, source_target_pairs={{0,1},{1,0},{2,3},{3,2},{4,5},{5,4},{6,7},{7,6},{8,9},{9,8},{10,11... | collective-permute-start | bytes 2359304 | tf_op jit(solution)/shard_map/ppermute | solution.py:29
  33.8 0.8 shard_map.132.kept_ref
  34.6 1.1 %collective-permute-done.5.received_ref = bf16[128,3072]{1,0:T(8,128)(2,1)S(1)} collective-permute-done((bf16[128,3072]{1,0:T(8,128)(2,1)S(1)}, bf16[128,3072]{1,0:T(8,128)(2,1)S(1)}, u32[]{:S(2)}, u32[]{:S(2)}) %collective-permute-start.5) | collective-permute-done | bytes 786464 | tf_op jit(solution)/shard_map/ppermute | solution.py:29
  35.7 2.8 %shard_map.133 = (bf16[128,3072]{1,0:T(8,128)(2,1)S(1)}, bf16[128,3072]{1,0:T(8,128)(2,1)S(1)}, bf16[2,128,768]{2,1,0:T(8,128)(2,1)S(1)}) custom-call(bf16[128,3072]{1,0:T(8,128)(2,1)S(1)} %bitcast.4, bf16[128,3072]{1,0:T(8,128)(2,1)S(1)} %shard_map.132.kept_ref, bf16[128,3072]{1,0:T(8,128)(2,1)S(1)} %collective-permute-done.5.received_ref, ...), custom_call_target="tpu_custom_call" | custom-call | tf_op jit(solution)/shard_map/pallas_call | solution.py:171
  39.0 8.5 %collective-permute-start.8 = (bf16[2,128,768]{2,1,0:T(8,128)(2,1)S(1)}, bf16[2,128,768]{2,1,0:T(8,128)(2,1)S(1)}, u32[]{:S(2)}, u32[]{:S(2)}) collective-permute-start(bf16[2,128,768]{2,1,0:T(8,128)(2,1)S(1)} %get-tuple-element.58.own_ref), channel_id=1, source_target_pairs={{2,4},{4,2},{6,8},{8,6},{10,12},{12,10},{14,16},{16,14},{18,20},{2... | collective-permute-start | bytes 1179656 | tf_op jit(solution)/shard_map/ppermute | solution.py:379
  47.5 2.1 %collective-permute-start.7 = (bf16[2,128,768]{2,1,0:T(8,128)(2,1)S(1)}, bf16[2,128,768]{2,1,0:T(8,128)(2,1)S(1)}, u32[]{:S(2)}, u32[]{:S(2)}) collective-permute-start(bf16[2,128,768]{2,1,0:T(8,128)(2,1)S(1)} %get-tuple-element.58.own_ref), channel_id=1, source_target_pairs={{0,2},{2,0},{4,6},{6,4},{8,10},{10,8},{12,14},{14,12},{16,18},{18,... | collective-permute-start | bytes 1179656 | tf_op jit(solution)/shard_map/ppermute | solution.py:379
  49.6 2.0 %shard_map.134.own_other_ref = bf16[2,128,768]{2,1,0:T(8,128)(2,1)S(1)} custom-call(bf16[128,3072]{1,0:T(8,128)(2,1)S(1)} %collective-permute-done.6.modulated_ref.other_ref, f32[2,64]{1,0:T(2,128)S(1)} %copy-done.1, bf16[3072,768]{1,0:T(8,128)(2,1)S(1)} %get-tuple-element.40.wk_ref, bf16[3072,768]{1,0:T(8,128)(2,1)S(1)} %get-tuple-element.41.wv_ref), custom_call_target="tpu_custom_call" | custom-call | tf_op jit(solution)/shard_map/pallas_call | solution.py:199
  51.6 0.8 collective-permute-start.10
  52.4 2.7 %collective-permute-start.9 = (bf16[2,128,768]{2,1,0:T(8,128)(2,1)S(1)}, bf16[2,128,768]{2,1,0:T(8,128)(2,1)S(1)}, u32[]{:S(2)}, u32[]{:S(2)}) collective-permute-start(bf16[2,128,768]{2,1,0:T(8,128)(2,1)S(1)} %shard_map.134.own_other_ref), channel_id=1, source_target_pairs={{0,2},{2,0},{4,6},{6,4},{8,10},{10,8},{12,14},{14,12},{16,18},{18,... | collective-permute-start | bytes 1179656 | tf_op jit(solution)/shard_map/ppermute | solution.py:379
  55.1 4.9 %shard_map.135 = (bf16[256,768]{1,0:T(8,128)(2,1)S(1)}, bf16[3,256,128]{2,1,0:T(8,128)(2,1)S(1)}, f32[2,256,768]{2,1,0:T(8,128)S(1)}, f32[2,3072]{1,0:T(2,128)S(1)}, bf16[128,3072]{1,0:T(8,128)(2,1)S(1)}) custom-call(s32[4,12]{1,0:T(4,128)S(1)} %copy-done.2, s32[128]{0:T(128)S(1)} %copy-done.3, s32[2]{0:T(128)S(1)} %copy-done.4, f32[50]{0:T(128)S(1)} %copy-done.5, ...), custom_call_target="tpu_custom_call" | custom-call | tf_op jit(solution)/shard_map/pallas_call | solution.py:274
  60.0 1.3 %shard_map.136.sums_ref = f32[2,256,768]{2,1,0:T(8,128)S(1)} custom-call(bf16[256,768]{1,0:T(8,128)(2,1)S(1)} %get-tuple-element.59.query_ref, bf16[3,256,128]{2,1,0:T(8,128)(2,1)S(1)} %get-tuple-element.60.bias_ref, f32[2,256,768]{2,1,0:T(8,128)S(1)} %get-tuple-element.61.sums_ref, bf16[2,128,768]{2,1,0:T(8,128)(2,1)S(1)} %collective-permute-done.7.partner_ref, ...), custom_call_target="tpu_custom_call" | custom-call | tf_op jit(solution)/shard_map/pallas_call | solution.py:292
  61.3 6.1 %collective-permute-done.10.neighbour_ref = bf16[2,128,768]{2,1,0:T(8,128)(2,1)S(1)} collective-permute-done((bf16[2,128,768]{2,1,0:T(8,128)(2,1)S(1)}, bf16[2,128,768]{2,1,0:T(8,128)(2,1)S(1)}, u32[]{:S(2)}, u32[]{:S(2)}) %collective-permute-start.10) | collective-permute-done | bytes 393248 | tf_op jit(solution)/shard_map/ppermute | solution.py:379
  67.4 0.6 collective-permute-done.9.partner_ref
  68.0 1.9 %shard_map.137 = (bf16[256,768]{1,0:T(8,128)(2,1)S(1)}, bf16[128,1536]{1,0:T(8,128)(2,1)S(1)}, bf16[128,1536]{1,0:T(8,128)(2,1)S(1)}) custom-call(bf16[256,768]{1,0:T(8,128)(2,1)S(1)} %get-tuple-element.59.query_ref, bf16[3,256,128]{2,1,0:T(8,128)(2,1)S(1)} %get-tuple-element.60.bias_ref, f32[2,256,768]{2,1,0:T(8,128)S(1)} %shard_map.136.sums_ref, ...), custom_call_target="tpu_custom_call" | custom-call | tf_op jit(solution)/shard_map/pallas_call | solution.py:325
  69.9 1.4 %collective-permute-start.11 = (bf16[128,1536]{1,0:T(8,128)(2,1)S(1)}, bf16[128,1536]{1,0:T(8,128)(2,1)S(1)}, u32[]{:S(2)}, u32[]{:S(2)}) collective-permute-start(bf16[128,1536]{1,0:T(8,128)(2,1)S(1)} %get-tuple-element.63), channel_id=1, source_target_pairs={{0,1},{1,0},{2,3},{3,2},{4,5},{5,4},{6,7},{7,6},{8,9},{9,8},{10,11... | collective-permute-start | bytes 1179656 | tf_op jit(solution)/shard_map/ppermute | solution.py:29
  71.3 0.8 shard_map.139
  73.0 0.9 collective-permute-done.13.received_ref
  74.2 14.8 %collective-permute-done.12 = bf16[128,1536]{1,0:T(8,128)(2,1)S(1)} collective-permute-done((bf16[128,1536]{1,0:T(8,128)(2,1)S(1)}, bf16[128,1536]{1,0:T(8,128)(2,1)S(1)}, u32[]{:S(2)}, u32[]{:S(2)}) %collective-permute-start.12) | collective-permute-done | bytes 393248 | tf_op jit(solution)/shard_map/ppermute | solution.py:433
  89.0 8.4 %collective-permute-done.14 = bf16[128,1536]{1,0:T(8,128)(2,1)S(1)} collective-permute-done((bf16[128,1536]{1,0:T(8,128)(2,1)S(1)}, bf16[128,1536]{1,0:T(8,128)(2,1)S(1)}, u32[]{:S(2)}, u32[]{:S(2)}) %collective-permute-start.14) | collective-permute-done | bytes 393248 | tf_op jit(solution)/shard_map/ppermute | solution.py:433
  97.5 1.0 maximum_bitcast_fusion
  (25 shorter events, 1.7 us)
Async XLA Ops:
  0.0 12.5 %copy-start.1 = (f32[2,64]{1,0:T(2,128)S(1)}, f32[2,64]{1,0:T(2,128)}, u32[]{:S(2)}) copy-start(f32[2,64]{1,0:T(2,128)} %gain_ref.9) | copy-start | bytes 1540
  6.5 5.2 %collective-permute-start = (bf16[128,3072]{1,0:T(8,128)(2,1)S(1)}, bf16[128,3072]{1,0:T(8,128)(2,1)S(1)}, u32[]{:S(2)}, u32[]{:S(2)}) collective-permute-start(bf16[128,3072]{1,0:T(8,128)(2,1)S(1)} %get-tuple-element.37.mine_ref), channel_id=1, source_target_pairs={{0,1},{1,0},{2,3},{3,2},{4,5},{5,4},{6,7},{7,6},{8,9},{9,8},{10,11... | collective-permute-start | bytes 2359304 | tf_op jit(solution)/shard_map/ppermute | solution.py:29
  9.8 12.9 %collective-permute-start.2 = (bf16[2,128,768]{2,1,0:T(8,128)(2,1)S(1)}, bf16[2,128,768]{2,1,0:T(8,128)(2,1)S(1)}, u32[]{:S(2)}, u32[]{:S(2)}) collective-permute-start(bf16[2,128,768]{2,1,0:T(8,128)(2,1)S(1)} %get-tuple-element.43.own_ref), channel_id=1, source_target_pairs={{2,4},{4,2},{6,8},{8,6},{10,12},{12,10},{14,16},{16,14},{18,20},{2... | collective-permute-start | bytes 1179656 | tf_op jit(solution)/shard_map/ppermute | solution.py:379
  11.7 11.0 %collective-permute-start.1 = (bf16[2,128,768]{2,1,0:T(8,128)(2,1)S(1)}, bf16[2,128,768]{2,1,0:T(8,128)(2,1)S(1)}, u32[]{:S(2)}, u32[]{:S(2)}) collective-permute-start(bf16[2,128,768]{2,1,0:T(8,128)(2,1)S(1)} %get-tuple-element.43.own_ref), channel_id=1, source_target_pairs={{0,2},{2,0},{4,6},{6,4},{8,10},{10,8},{12,14},{14,12},{16,18},{18,... | collective-permute-start | bytes 1179656 | tf_op jit(solution)/shard_map/ppermute | solution.py:379
  12.5 4.1 %copy-start.2 = (s32[4,12]{1,0:T(4,128)S(1)}, s32[4,12]{1,0:T(4,128)}, u32[]{:S(2)}) copy-start(s32[4,12]{1,0:T(4,128)} %pattern_ref.3) | copy-start | bytes 580
  12.5 4.1 %copy-start.3 = (s32[128]{0:T(128)S(1)}, s32[128]{0:T(128)}, u32[]{:S(2)}) copy-start(s32[128]{0:T(128)} %levels_ref.5) | copy-start | bytes 1540
  12.5 4.1 %copy-start.4 = (s32[2]{0:T(128)S(1)}, s32[2]{0:T(128)}, u32[]{:S(2)}) copy-start(s32[2]{0:T(128)} %entry_ref.3) | copy-start | bytes 28
  12.5 4.1 %copy-start.5 = (f32[50]{0:T(128)S(1)}, f32[50]{0:T(128)}, u32[]{:S(2)}) copy-start(f32[50]{0:T(128)} %size_ref.3) | copy-start | bytes 604
  14.9 15.6 %collective-permute-start.3 = (bf16[2,128,768]{2,1,0:T(8,128)(2,1)S(1)}, bf16[2,128,768]{2,1,0:T(8,128)(2,1)S(1)}, u32[]{:S(2)}, u32[]{:S(2)}) collective-permute-start(bf16[2,128,768]{2,1,0:T(8,128)(2,1)S(1)} %get-tuple-element.44.own_other_ref), channel_id=1, source_target_pairs={{0,2},{2,0},{4,6},{6,4},{8,10},{10,8},{12,14},{14,12},{16,18},{18,... | collective-permute-start | bytes 1179656 | tf_op jit(solution)/shard_map/ppermute | solution.py:379
  15.7 14.8 %collective-permute-start.4 = (bf16[2,128,768]{2,1,0:T(8,128)(2,1)S(1)}, bf16[2,128,768]{2,1,0:T(8,128)(2,1)S(1)}, u32[]{:S(2)}, u32[]{:S(2)}) collective-permute-start(bf16[2,128,768]{2,1,0:T(8,128)(2,1)S(1)} %get-tuple-element.44.own_other_ref), channel_id=1, source_target_pairs={{2,4},{4,2},{6,8},{8,6},{10,12},{12,10},{14,16},{16,14},{18,20},{2... | collective-permute-start | bytes 1179656 | tf_op jit(solution)/shard_map/ppermute | solution.py:379
  32.5 3.2 %copy-start = (bf16[1,128,3072]{2,1,0:T(8,128)(2,1)S(1)}, bf16[1,128,3072]{2,1,0:T(8,128)(2,1)}, u32[]{:S(2)}) copy-start(bf16[1,128,3072]{2,1,0:T(8,128)(2,1)} %param.13) | copy-start | bytes 2359300
  32.5 3.2 %collective-permute-start.5 = (bf16[128,3072]{1,0:T(8,128)(2,1)S(1)}, bf16[128,3072]{1,0:T(8,128)(2,1)S(1)}, u32[]{:S(2)}, u32[]{:S(2)}) collective-permute-start(bf16[128,3072]{1,0:T(8,128)(2,1)S(1)} %get-tuple-element.50), channel_id=1, source_target_pairs={{0,1},{1,0},{2,3},{3,2},{4,5},{5,4},{6,7},{7,6},{8,9},{9,8},{10,11... | collective-permute-start | bytes 2359304 | tf_op jit(solution)/shard_map/ppermute | solution.py:29
  38.5 9.0 %collective-permute-start.6 = (bf16[128,3072]{1,0:T(8,128)(2,1)S(1)}, bf16[128,3072]{1,0:T(8,128)(2,1)S(1)}, u32[]{:S(2)}, u32[]{:S(2)}) collective-permute-start(bf16[128,3072]{1,0:T(8,128)(2,1)S(1)} %get-tuple-element.55.mine_ref), channel_id=1, source_target_pairs={{0,1},{1,0},{2,3},{3,2},{4,5},{5,4},{6,7},{7,6},{8,9},{9,8},{10,11... | collective-permute-start | bytes 2359304 | tf_op jit(solution)/shard_map/ppermute | solution.py:29
  39.0 21.0 %collective-permute-start.8 = (bf16[2,128,768]{2,1,0:T(8,128)(2,1)S(1)}, bf16[2,128,768]{2,1,0:T(8,128)(2,1)S(1)}, u32[]{:S(2)}, u32[]{:S(2)}) collective-permute-start(bf16[2,128,768]{2,1,0:T(8,128)(2,1)S(1)} %get-tuple-element.58.own_ref), channel_id=1, source_target_pairs={{2,4},{4,2},{6,8},{8,6},{10,12},{12,10},{14,16},{16,14},{18,20},{2... | collective-permute-start | bytes 1179656 | tf_op jit(solution)/shard_map/ppermute | solution.py:379
  47.5 12.5 %collective-permute-start.7 = (bf16[2,128,768]{2,1,0:T(8,128)(2,1)S(1)}, bf16[2,128,768]{2,1,0:T(8,128)(2,1)S(1)}, u32[]{:S(2)}, u32[]{:S(2)}) collective-permute-start(bf16[2,128,768]{2,1,0:T(8,128)(2,1)S(1)} %get-tuple-element.58.own_ref), channel_id=1, source_target_pairs={{0,2},{2,0},{4,6},{6,4},{8,10},{10,8},{12,14},{14,12},{16,18},{18,... | collective-permute-start | bytes 1179656 | tf_op jit(solution)/shard_map/ppermute | solution.py:379
  51.6 15.8 %collective-permute-start.10 = (bf16[2,128,768]{2,1,0:T(8,128)(2,1)S(1)}, bf16[2,128,768]{2,1,0:T(8,128)(2,1)S(1)}, u32[]{:S(2)}, u32[]{:S(2)}) collective-permute-start(bf16[2,128,768]{2,1,0:T(8,128)(2,1)S(1)} %shard_map.134.own_other_ref), channel_id=1, source_target_pairs={{2,4},{4,2},{6,8},{8,6},{10,12},{12,10},{14,16},{16,14},{18,20},{2... | collective-permute-start | bytes 1179656 | tf_op jit(solution)/shard_map/ppermute | solution.py:379
  52.4 15.7 %collective-permute-start.9 = (bf16[2,128,768]{2,1,0:T(8,128)(2,1)S(1)}, bf16[2,128,768]{2,1,0:T(8,128)(2,1)S(1)}, u32[]{:S(2)}, u32[]{:S(2)}) collective-permute-start(bf16[2,128,768]{2,1,0:T(8,128)(2,1)S(1)} %shard_map.134.own_other_ref), channel_id=1, source_target_pairs={{0,2},{2,0},{4,6},{6,4},{8,10},{10,8},{12,14},{14,12},{16,18},{18,... | collective-permute-start | bytes 1179656 | tf_op jit(solution)/shard_map/ppermute | solution.py:379
  69.9 2.7 %collective-permute-start.11 = (bf16[128,1536]{1,0:T(8,128)(2,1)S(1)}, bf16[128,1536]{1,0:T(8,128)(2,1)S(1)}, u32[]{:S(2)}, u32[]{:S(2)}) collective-permute-start(bf16[128,1536]{1,0:T(8,128)(2,1)S(1)} %get-tuple-element.63), channel_id=1, source_target_pairs={{0,1},{1,0},{2,3},{3,2},{4,5},{5,4},{6,7},{7,6},{8,9},{9,8},{10,11... | collective-permute-start | bytes 1179656 | tf_op jit(solution)/shard_map/ppermute | solution.py:29
  72.1 1.8 %collective-permute-start.13 = (bf16[128,1536]{1,0:T(8,128)(2,1)S(1)}, bf16[128,1536]{1,0:T(8,128)(2,1)S(1)}, u32[]{:S(2)}, u32[]{:S(2)}) collective-permute-start(bf16[128,1536]{1,0:T(8,128)(2,1)S(1)} %get-tuple-element.68), channel_id=1, source_target_pairs={{0,1},{1,0},{2,3},{3,2},{4,5},{5,4},{6,7},{7,6},{8,9},{9,8},{10,11... | collective-permute-start | bytes 1179656 | tf_op jit(solution)/shard_map/ppermute | solution.py:29
  72.9 16.1 %collective-permute-start.12 = (bf16[128,1536]{1,0:T(8,128)(2,1)S(1)}, bf16[128,1536]{1,0:T(8,128)(2,1)S(1)}, u32[]{:S(2)}, u32[]{:S(2)}) collective-permute-start(bf16[128,1536]{1,0:T(8,128)(2,1)S(1)} %shard_map.138), channel_id=1, source_target_pairs={{0,4},{2,6},{4,8},{6,10},{8,12},{10,14},{12,16},{14,18},{16,20},{1... | collective-permute-start | bytes 1179656 | tf_op jit(solution)/shard_map/ppermute | solution.py:433
  74.2 23.3 %collective-permute-start.14 = (bf16[128,1536]{1,0:T(8,128)(2,1)S(1)}, bf16[128,1536]{1,0:T(8,128)(2,1)S(1)}, u32[]{:S(2)}, u32[]{:S(2)}) collective-permute-start(bf16[128,1536]{1,0:T(8,128)(2,1)S(1)} %shard_map.140), channel_id=1, source_target_pairs={{0,4},{2,6},{4,8},{6,10},{8,12},{10,14},{12,16},{14,18},{16,20},{1... | collective-permute-start | bytes 1179656 | tf_op jit(solution)/shard_map/ppermute | solution.py:433

commit v7 on v6

--- a/solution.py
+++ b/solution.py
@@ -109,10 +109,12 @@
             for i, (ref, out) in enumerate(((wk_ref, wk_out), (wv_ref, wv_out)))
             for j, part in enumerate(parts)
         ]
-        for copy in tables + weights[:3]:
+        for copy in tables + weights[:1]:
             copy.start()
         for copy in [first] + tables:
             copy.wait()
+        for copy in weights[1:3]:
+            copy.start()
         for step in range(ITERS):
             row = pl.ds(levels_sm[slot_of(step)], 1)
             rows_ref[step, 0:1, :] = 1.0 + held[0, row, :]

time: 99.2 us -> 98.8 us (level)
  no operation moved by 1% of the time
where the time goes in v7:
time: 98.8 us; the launch traced here: 98.1 us
  waiting for transfers between devices  40.1 us (41%)
  Pallas kernels  32.9 us (33%)
  starting transfers between devices  23.9 us (24%)
    ppermute x2, waiting for transfers between devices, on_device(): result.append(lax.ppermute(part, 'queue', route))  23.2 us
    ppermute x8, starting transfers between devices, exchanged(): return lax.ppermute(block, 'queue', pairs)  17.2 us
    ppermute x8, waiting for transfers between devices, exchanged(): return lax.ppermute(block, 'queue', pairs)  13.2 us
    pallas_call x2, Pallas kernels, queries(): pl.pallas_call(kernel, out_shape=out_shape, in_specs=[SMEM] * 4 + [VMEM]...  11 us
    ppermute x5, starting transfers between devices, swap_cores(): return lax.ppermute(block, 'seq', [(0, 1), (1, 0)])  6.54 us
    pallas_call x1, Pallas kernels, first_half(): pl.pallas_call(kernel, out_shape=(jax.ShapeDtypeStruct((half, depth), BF1...  6.2 us
    pallas_call x2, Pallas kernels, other_half(): pl.pallas_call(kernel, out_shape=(out, jax.ShapeDtypeStruct(wq.shape, BF1...  4.39 us
    pallas_call x2, Pallas kernels, attend_project(): pl.pallas_call(kernel, out_shape=(jax.ShapeDtypeStruct(query.shape, BF16)...  3.94 us
  transfers between devices with their start and end apart: 15, of which 9 were waited for; matrix products, arithmetic and copies ran while one was open for 0% of the time, Pallas kernels for 20%

profile of v7, /device:TPU:1, one launch (start us, length us, event | category | flops | bytes accessed | tf_op | source)
XLA Modules:
  0.0 98.1 jit_solution(7496637838113738392)
XLA Ops:
  0.0 6.2 %shard_map.127 = (bf16[128,3072]{1,0:T(8,128)(2,1)S(1)}, bf16[2,128,768]{2,1,0:T(8,128)(2,1)S(1)}, f32[2,2,3072]{2,1,0:T(2,128)S(1)}, bf16[3072,768]{1,0:T(8,128)(2,1)S(1)}, bf16[3072,768]{1,0:T(8,128)(2,1)S(1)}) custom-call(s32[128]{0:T(128)} %levels_ref.5, f32[50,3072]{1,0:T(8,128)} %scale_ref.1, f32[50,3072]{1,0:T(8,128)} %shift_ref.1, ...), custom_call_target="tpu_custom_call" | custom-call | tf_op jit(solution)/shard_map/pallas_call | solution.py:133
  6.2 3.3 %collective-permute-start = (bf16[128,3072]{1,0:T(8,128)(2,1)S(1)}, bf16[128,3072]{1,0:T(8,128)(2,1)S(1)}, u32[]{:S(2)}, u32[]{:S(2)}) collective-permute-start(bf16[128,3072]{1,0:T(8,128)(2,1)S(1)} %get-tuple-element.37.mine_ref), channel_id=1, source_target_pairs={{0,1},{1,0},{2,3},{3,2},{4,5},{5,4},{6,7},{7,6},{8,9},{9,8},{10,11... | collective-permute-start | bytes 2359304 | tf_op jit(solution)/shard_map/ppermute | solution.py:29
  9.5 0.7 collective-permute-start.2
  10.2 1.2 %collective-permute-done.modulated_ref.other_ref = bf16[128,3072]{1,0:T(8,128)(2,1)S(1)} collective-permute-done((bf16[128,3072]{1,0:T(8,128)(2,1)S(1)}, bf16[128,3072]{1,0:T(8,128)(2,1)S(1)}, u32[]{:S(2)}, u32[]{:S(2)}) %collective-permute-start) | collective-permute-done | bytes 786464 | tf_op jit(solution)/shard_map/ppermute | solution.py:29
  11.4 0.8 collective-permute-start.1
  12.2 2.4 %shard_map.128 = (bf16[2,128,768]{2,1,0:T(8,128)(2,1)S(1)}, bf16[3072,768]{1,0:T(8,128)(2,1)S(1)}) custom-call(bf16[128,3072]{1,0:T(8,128)(2,1)S(1)} %collective-permute-done.modulated_ref.other_ref, f32[2,64]{1,0:T(2,128)S(1)} %copy-done.1, bf16[3072,768]{1,0:T(8,128)(2,1)S(1)} %get-tuple-element.40.wk_ref, bf16[3072,768]{1,0:T(8,128)(2,1)S(1)} %get-tuple-element.41.wv_ref, ...), custom_call_target="tpu_custom_call" | custom-call | tf_op jit(solution)/shard_map/pallas_call | solution.py:201
  14.6 0.8 collective-permute-start.3
  15.4 0.9 collective-permute-start.4
  16.3 6.1 %shard_map.129 = (bf16[256,768]{1,0:T(8,128)(2,1)S(1)}, bf16[3,256,128]{2,1,0:T(8,128)(2,1)S(1)}, f32[2,256,768]{2,1,0:T(8,128)S(1)}, f32[2,3072]{1,0:T(2,128)S(...) custom-call(s32[4,12]{1,0:T(4,128)S(1)} %copy-done.2, s32[128]{0:T(128)S(1)} %copy-done.3, ...), custom_call_target="tpu_custom_call" | custom-call | tf_op jit(solution)/shard_map/pallas_call | solution.py:276
  22.4 1.3 %shard_map.130.sums_ref = f32[2,256,768]{2,1,0:T(8,128)S(1)} custom-call(bf16[256,768]{1,0:T(8,128)(2,1)S(1)} %get-tuple-element.45.query_ref, bf16[3,256,128]{2,1,0:T(8,128)(2,1)S(1)} %get-tuple-element.46.bias_ref, f32[2,256,768]{2,1,0:T(8,128)S(1)} %get-tuple-element.47.sums_ref, bf16[2,128,768]{2,1,0:T(8,128)(2,1)S(1)} %collective-permute-done.1.partner_ref, ...), custom_call_target="tpu_custom_call" | custom-call | tf_op jit(solution)/shard_map/pallas_call | solution.py:294
  23.7 6.5 %collective-permute-done.3.partner_ref = bf16[2,128,768]{2,1,0:T(8,128)(2,1)S(1)} collective-permute-done((bf16[2,128,768]{2,1,0:T(8,128)(2,1)S(1)}, bf16[2,128,768]{2,1,0:T(8,128)(2,1)S(1)}, u32[]{:S(2)}, u32[]{:S(2)}) %collective-permute-start.3) | collective-permute-done | bytes 393248 | tf_op jit(solution)/shard_map/ppermute | solution.py:381
  30.2 2.0 %shard_map.131 = (bf16[256,768]{1,0:T(8,128)(2,1)S(1)}, bf16[128,3072]{1,0:T(8,128)(2,1)S(1)}) custom-call(bf16[256,768]{1,0:T(8,128)(2,1)S(1)} %get-tuple-element.45.query_ref, bf16[3,256,128]{2,1,0:T(8,128)(2,1)S(1)} %get-tuple-element.46.bias_ref, f32[2,256,768]{2,1,0:T(8,128)S(1)} %shard_map.130.sums_ref, ...), custom_call_target="tpu_custom_call" | custom-call | tf_op jit(solution)/shard_map/pallas_call | solution.py:327
  32.2 1.3 %collective-permute-start.5 = (bf16[128,3072]{1,0:T(8,128)(2,1)S(1)}, bf16[128,3072]{1,0:T(8,128)(2,1)S(1)}, u32[]{:S(2)}, u32[]{:S(2)}) collective-permute-start(bf16[128,3072]{1,0:T(8,128)(2,1)S(1)} %get-tuple-element.50), channel_id=1, source_target_pairs={{0,1},{1,0},{2,3},{3,2},{4,5},{5,4},{6,7},{7,6},{8,9},{9,8},{10,11... | collective-permute-start | bytes 2359304 | tf_op jit(solution)/shard_map/ppermute | solution.py:29
  33.5 0.8 shard_map.132.kept_ref
  34.4 1.1 %collective-permute-done.5.received_ref = bf16[128,3072]{1,0:T(8,128)(2,1)S(1)} collective-permute-done((bf16[128,3072]{1,0:T(8,128)(2,1)S(1)}, bf16[128,3072]{1,0:T(8,128)(2,1)S(1)}, u32[]{:S(2)}, u32[]{:S(2)}) %collective-permute-start.5) | collective-permute-done | bytes 786464 | tf_op jit(solution)/shard_map/ppermute | solution.py:29
  35.4 2.8 %shard_map.133 = (bf16[128,3072]{1,0:T(8,128)(2,1)S(1)}, bf16[128,3072]{1,0:T(8,128)(2,1)S(1)}, bf16[2,128,768]{2,1,0:T(8,128)(2,1)S(1)}) custom-call(bf16[128,3072]{1,0:T(8,128)(2,1)S(1)} %bitcast.4, bf16[128,3072]{1,0:T(8,128)(2,1)S(1)} %shard_map.132.kept_ref, bf16[128,3072]{1,0:T(8,128)(2,1)S(1)} %collective-permute-done.5.received_ref, ...), custom_call_target="tpu_custom_call" | custom-call | tf_op jit(solution)/shard_map/pallas_call | solution.py:173
  38.7 8.5 %collective-permute-start.8 = (bf16[2,128,768]{2,1,0:T(8,128)(2,1)S(1)}, bf16[2,128,768]{2,1,0:T(8,128)(2,1)S(1)}, u32[]{:S(2)}, u32[]{:S(2)}) collective-permute-start(bf16[2,128,768]{2,1,0:T(8,128)(2,1)S(1)} %get-tuple-element.58.own_ref), channel_id=1, source_target_pairs={{2,4},{4,2},{6,8},{8,6},{10,12},{12,10},{14,16},{16,14},{18,20},{2... | collective-permute-start | bytes 1179656 | tf_op jit(solution)/shard_map/ppermute | solution.py:381
  47.2 2.1 %collective-permute-start.7 = (bf16[2,128,768]{2,1,0:T(8,128)(2,1)S(1)}, bf16[2,128,768]{2,1,0:T(8,128)(2,1)S(1)}, u32[]{:S(2)}, u32[]{:S(2)}) collective-permute-start(bf16[2,128,768]{2,1,0:T(8,128)(2,1)S(1)} %get-tuple-element.58.own_ref), channel_id=1, source_target_pairs={{0,2},{2,0},{4,6},{6,4},{8,10},{10,8},{12,14},{14,12},{16,18},{18,... | collective-permute-start | bytes 1179656 | tf_op jit(solution)/shard_map/ppermute | solution.py:381
  49.3 2.0 %shard_map.134.own_other_ref = bf16[2,128,768]{2,1,0:T(8,128)(2,1)S(1)} custom-call(bf16[128,3072]{1,0:T(8,128)(2,1)S(1)} %collective-permute-done.6.modulated_ref.other_ref, f32[2,64]{1,0:T(2,128)S(1)} %copy-done.1, bf16[3072,768]{1,0:T(8,128)(2,1)S(1)} %get-tuple-element.40.wk_ref, bf16[3072,768]{1,0:T(8,128)(2,1)S(1)} %get-tuple-element.41.wv_ref), custom_call_target="tpu_custom_call" | custom-call | tf_op jit(solution)/shard_map/pallas_call | solution.py:201
  51.3 0.8 collective-permute-start.10
  52.1 2.7 %collective-permute-start.9 = (bf16[2,128,768]{2,1,0:T(8,128)(2,1)S(1)}, bf16[2,128,768]{2,1,0:T(8,128)(2,1)S(1)}, u32[]{:S(2)}, u32[]{:S(2)}) collective-permute-start(bf16[2,128,768]{2,1,0:T(8,128)(2,1)S(1)} %shard_map.134.own_other_ref), channel_id=1, source_target_pairs={{0,2},{2,0},{4,6},{6,4},{8,10},{10,8},{12,14},{14,12},{16,18},{18,... | collective-permute-start | bytes 1179656 | tf_op jit(solution)/shard_map/ppermute | solution.py:381
  54.8 4.9 %shard_map.135 = (bf16[256,768]{1,0:T(8,128)(2,1)S(1)}, bf16[3,256,128]{2,1,0:T(8,128)(2,1)S(1)}, f32[2,256,768]{2,1,0:T(8,128)S(1)}, f32[2,3072]{1,0:T(2,128)S(1)}, bf16[128,3072]{1,0:T(8,128)(2,1)S(1)}) custom-call(s32[4,12]{1,0:T(4,128)S(1)} %copy-done.2, s32[128]{0:T(128)S(1)} %copy-done.3, s32[2]{0:T(128)S(1)} %copy-done.4, f32[50]{0:T(128)S(1)} %copy-done.5, ...), custom_call_target="tpu_custom_call" | custom-call | tf_op jit(solution)/shard_map/pallas_call | solution.py:276
  59.7 1.3 %shard_map.136.sums_ref = f32[2,256,768]{2,1,0:T(8,128)S(1)} custom-call(bf16[256,768]{1,0:T(8,128)(2,1)S(1)} %get-tuple-element.59.query_ref, bf16[3,256,128]{2,1,0:T(8,128)(2,1)S(1)} %get-tuple-element.60.bias_ref, f32[2,256,768]{2,1,0:T(8,128)S(1)} %get-tuple-element.61.sums_ref, bf16[2,128,768]{2,1,0:T(8,128)(2,1)S(1)} %collective-permute-done.7.partner_ref, ...), custom_call_target="tpu_custom_call" | custom-call | tf_op jit(solution)/shard_map/pallas_call | solution.py:294
  61.0 6.1 %collective-permute-done.10.neighbour_ref = bf16[2,128,768]{2,1,0:T(8,128)(2,1)S(1)} collective-permute-done((bf16[2,128,768]{2,1,0:T(8,128)(2,1)S(1)}, bf16[2,128,768]{2,1,0:T(8,128)(2,1)S(1)}, u32[]{:S(2)}, u32[]{:S(2)}) %collective-permute-start.10) | collective-permute-done | bytes 393248 | tf_op jit(solution)/shard_map/ppermute | solution.py:381
  67.1 0.6 collective-permute-done.9.partner_ref
  67.7 1.9 %shard_map.137 = (bf16[256,768]{1,0:T(8,128)(2,1)S(1)}, bf16[128,1536]{1,0:T(8,128)(2,1)S(1)}, bf16[128,1536]{1,0:T(8,128)(2,1)S(1)}) custom-call(bf16[256,768]{1,0:T(8,128)(2,1)S(1)} %get-tuple-element.59.query_ref, bf16[3,256,128]{2,1,0:T(8,128)(2,1)S(1)} %get-tuple-element.60.bias_ref, f32[2,256,768]{2,1,0:T(8,128)S(1)} %shard_map.136.sums_ref, ...), custom_call_target="tpu_custom_call" | custom-call | tf_op jit(solution)/shard_map/pallas_call | solution.py:327
  69.7 1.4 %collective-permute-start.11 = (bf16[128,1536]{1,0:T(8,128)(2,1)S(1)}, bf16[128,1536]{1,0:T(8,128)(2,1)S(1)}, u32[]{:S(2)}, u32[]{:S(2)}) collective-permute-start(bf16[128,1536]{1,0:T(8,128)(2,1)S(1)} %get-tuple-element.63), channel_id=1, source_target_pairs={{0,1},{1,0},{2,3},{3,2},{4,5},{5,4},{6,7},{7,6},{8,9},{9,8},{10,11... | collective-permute-start | bytes 1179656 | tf_op jit(solution)/shard_map/ppermute | solution.py:29
  71.0 0.8 shard_map.139
  72.7 0.9 collective-permute-done.13.received_ref
  74.0 14.8 %collective-permute-done.12 = bf16[128,1536]{1,0:T(8,128)(2,1)S(1)} collective-permute-done((bf16[128,1536]{1,0:T(8,128)(2,1)S(1)}, bf16[128,1536]{1,0:T(8,128)(2,1)S(1)}, u32[]{:S(2)}, u32[]{:S(2)}) %collective-permute-start.12) | collective-permute-done | bytes 393248 | tf_op jit(solution)/shard_map/ppermute | solution.py:435
  88.7 8.4 %collective-permute-done.14 = bf16[128,1536]{1,0:T(8,128)(2,1)S(1)} collective-permute-done((bf16[128,1536]{1,0:T(8,128)(2,1)S(1)}, bf16[128,1536]{1,0:T(8,128)(2,1)S(1)}, u32[]{:S(2)}, u32[]{:S(2)}) %collective-permute-start.14) | collective-permute-done | bytes 393248 | tf_op jit(solution)/shard_map/ppermute | solution.py:435
  97.2 1.0 maximum_bitcast_fusion
  (25 shorter events, 1.7 us)
Async XLA Ops:
  0.0 12.2 %copy-start.1 = (f32[2,64]{1,0:T(2,128)S(1)}, f32[2,64]{1,0:T(2,128)}, u32[]{:S(2)}) copy-start(f32[2,64]{1,0:T(2,128)} %gain_ref.9) | copy-start | bytes 1540
  6.2 5.2 %collective-permute-start = (bf16[128,3072]{1,0:T(8,128)(2,1)S(1)}, bf16[128,3072]{1,0:T(8,128)(2,1)S(1)}, u32[]{:S(2)}, u32[]{:S(2)}) collective-permute-start(bf16[128,3072]{1,0:T(8,128)(2,1)S(1)} %get-tuple-element.37.mine_ref), channel_id=1, source_target_pairs={{0,1},{1,0},{2,3},{3,2},{4,5},{5,4},{6,7},{7,6},{8,9},{9,8},{10,11... | collective-permute-start | bytes 2359304 | tf_op jit(solution)/shard_map/ppermute | solution.py:29
  9.5 12.9 %collective-permute-start.2 = (bf16[2,128,768]{2,1,0:T(8,128)(2,1)S(1)}, bf16[2,128,768]{2,1,0:T(8,128)(2,1)S(1)}, u32[]{:S(2)}, u32[]{:S(2)}) collective-permute-start(bf16[2,128,768]{2,1,0:T(8,128)(2,1)S(1)} %get-tuple-element.43.own_ref), channel_id=1, source_target_pairs={{2,4},{4,2},{6,8},{8,6},{10,12},{12,10},{14,16},{16,14},{18,20},{2... | collective-permute-start | bytes 1179656 | tf_op jit(solution)/shard_map/ppermute | solution.py:381
  11.4 11.0 %collective-permute-start.1 = (bf16[2,128,768]{2,1,0:T(8,128)(2,1)S(1)}, bf16[2,128,768]{2,1,0:T(8,128)(2,1)S(1)}, u32[]{:S(2)}, u32[]{:S(2)}) collective-permute-start(bf16[2,128,768]{2,1,0:T(8,128)(2,1)S(1)} %get-tuple-element.43.own_ref), channel_id=1, source_target_pairs={{0,2},{2,0},{4,6},{6,4},{8,10},{10,8},{12,14},{14,12},{16,18},{18,... | collective-permute-start | bytes 1179656 | tf_op jit(solution)/shard_map/ppermute | solution.py:381
  12.2 4.1 %copy-start.2 = (s32[4,12]{1,0:T(4,128)S(1)}, s32[4,12]{1,0:T(4,128)}, u32[]{:S(2)}) copy-start(s32[4,12]{1,0:T(4,128)} %pattern_ref.3) | copy-start | bytes 580
  12.2 4.1 %copy-start.3 = (s32[128]{0:T(128)S(1)}, s32[128]{0:T(128)}, u32[]{:S(2)}) copy-start(s32[128]{0:T(128)} %levels_ref.5) | copy-start | bytes 1540
  12.2 4.1 %copy-start.4 = (s32[2]{0:T(128)S(1)}, s32[2]{0:T(128)}, u32[]{:S(2)}) copy-start(s32[2]{0:T(128)} %entry_ref.3) | copy-start | bytes 28
  12.2 4.1 %copy-start.5 = (f32[50]{0:T(128)S(1)}, f32[50]{0:T(128)}, u32[]{:S(2)}) copy-start(f32[50]{0:T(128)} %size_ref.3) | copy-start | bytes 604
  14.6 15.6 %collective-permute-start.3 = (bf16[2,128,768]{2,1,0:T(8,128)(2,1)S(1)}, bf16[2,128,768]{2,1,0:T(8,128)(2,1)S(1)}, u32[]{:S(2)}, u32[]{:S(2)}) collective-permute-start(bf16[2,128,768]{2,1,0:T(8,128)(2,1)S(1)} %get-tuple-element.44.own_other_ref), channel_id=1, source_target_pairs={{0,2},{2,0},{4,6},{6,4},{8,10},{10,8},{12,14},{14,12},{16,18},{18,... | collective-permute-start | bytes 1179656 | tf_op jit(solution)/shard_map/ppermute | solution.py:381
  15.4 14.8 %collective-permute-start.4 = (bf16[2,128,768]{2,1,0:T(8,128)(2,1)S(1)}, bf16[2,128,768]{2,1,0:T(8,128)(2,1)S(1)}, u32[]{:S(2)}, u32[]{:S(2)}) collective-permute-start(bf16[2,128,768]{2,1,0:T(8,128)(2,1)S(1)} %get-tuple-element.44.own_other_ref), channel_id=1, source_target_pairs={{2,4},{4,2},{6,8},{8,6},{10,12},{12,10},{14,16},{16,14},{18,20},{2... | collective-permute-start | bytes 1179656 | tf_op jit(solution)/shard_map/ppermute | solution.py:381
  32.2 3.2 %copy-start = (bf16[1,128,3072]{2,1,0:T(8,128)(2,1)S(1)}, bf16[1,128,3072]{2,1,0:T(8,128)(2,1)}, u32[]{:S(2)}) copy-start(bf16[1,128,3072]{2,1,0:T(8,128)(2,1)} %param.13) | copy-start | bytes 2359300
  32.2 3.2 %collective-permute-start.5 = (bf16[128,3072]{1,0:T(8,128)(2,1)S(1)}, bf16[128,3072]{1,0:T(8,128)(2,1)S(1)}, u32[]{:S(2)}, u32[]{:S(2)}) collective-permute-start(bf16[128,3072]{1,0:T(8,128)(2,1)S(1)} %get-tuple-element.50), channel_id=1, source_target_pairs={{0,1},{1,0},{2,3},{3,2},{4,5},{5,4},{6,7},{7,6},{8,9},{9,8},{10,11... | collective-permute-start | bytes 2359304 | tf_op jit(solution)/shard_map/ppermute | solution.py:29
  38.2 9.0 %collective-permute-start.6 = (bf16[128,3072]{1,0:T(8,128)(2,1)S(1)}, bf16[128,3072]{1,0:T(8,128)(2,1)S(1)}, u32[]{:S(2)}, u32[]{:S(2)}) collective-permute-start(bf16[128,3072]{1,0:T(8,128)(2,1)S(1)} %get-tuple-element.55.mine_ref), channel_id=1, source_target_pairs={{0,1},{1,0},{2,3},{3,2},{4,5},{5,4},{6,7},{7,6},{8,9},{9,8},{10,11... | collective-permute-start | bytes 2359304 | tf_op jit(solution)/shard_map/ppermute | solution.py:29
  38.7 21.0 %collective-permute-start.8 = (bf16[2,128,768]{2,1,0:T(8,128)(2,1)S(1)}, bf16[2,128,768]{2,1,0:T(8,128)(2,1)S(1)}, u32[]{:S(2)}, u32[]{:S(2)}) collective-permute-start(bf16[2,128,768]{2,1,0:T(8,128)(2,1)S(1)} %get-tuple-element.58.own_ref), channel_id=1, source_target_pairs={{2,4},{4,2},{6,8},{8,6},{10,12},{12,10},{14,16},{16,14},{18,20},{2... | collective-permute-start | bytes 1179656 | tf_op jit(solution)/shard_map/ppermute | solution.py:381
  47.2 12.5 %collective-permute-start.7 = (bf16[2,128,768]{2,1,0:T(8,128)(2,1)S(1)}, bf16[2,128,768]{2,1,0:T(8,128)(2,1)S(1)}, u32[]{:S(2)}, u32[]{:S(2)}) collective-permute-start(bf16[2,128,768]{2,1,0:T(8,128)(2,1)S(1)} %get-tuple-element.58.own_ref), channel_id=1, source_target_pairs={{0,2},{2,0},{4,6},{6,4},{8,10},{10,8},{12,14},{14,12},{16,18},{18,... | collective-permute-start | bytes 1179656 | tf_op jit(solution)/shard_map/ppermute | solution.py:381
  51.3 15.8 %collective-permute-start.10 = (bf16[2,128,768]{2,1,0:T(8,128)(2,1)S(1)}, bf16[2,128,768]{2,1,0:T(8,128)(2,1)S(1)}, u32[]{:S(2)}, u32[]{:S(2)}) collective-permute-start(bf16[2,128,768]{2,1,0:T(8,128)(2,1)S(1)} %shard_map.134.own_other_ref), channel_id=1, source_target_pairs={{2,4},{4,2},{6,8},{8,6},{10,12},{12,10},{14,16},{16,14},{18,20},{2... | collective-permute-start | bytes 1179656 | tf_op jit(solution)/shard_map/ppermute | solution.py:381
  52.1 15.7 %collective-permute-start.9 = (bf16[2,128,768]{2,1,0:T(8,128)(2,1)S(1)}, bf16[2,128,768]{2,1,0:T(8,128)(2,1)S(1)}, u32[]{:S(2)}, u32[]{:S(2)}) collective-permute-start(bf16[2,128,768]{2,1,0:T(8,128)(2,1)S(1)} %shard_map.134.own_other_ref), channel_id=1, source_target_pairs={{0,2},{2,0},{4,6},{6,4},{8,10},{10,8},{12,14},{14,12},{16,18},{18,... | collective-permute-start | bytes 1179656 | tf_op jit(solution)/shard_map/ppermute | solution.py:381
  69.7 2.7 %collective-permute-start.11 = (bf16[128,1536]{1,0:T(8,128)(2,1)S(1)}, bf16[128,1536]{1,0:T(8,128)(2,1)S(1)}, u32[]{:S(2)}, u32[]{:S(2)}) collective-permute-start(bf16[128,1536]{1,0:T(8,128)(2,1)S(1)} %get-tuple-element.63), channel_id=1, source_target_pairs={{0,1},{1,0},{2,3},{3,2},{4,5},{5,4},{6,7},{7,6},{8,9},{9,8},{10,11... | collective-permute-start | bytes 1179656 | tf_op jit(solution)/shard_map/ppermute | solution.py:29
  71.8 1.8 %collective-permute-start.13 = (bf16[128,1536]{1,0:T(8,128)(2,1)S(1)}, bf16[128,1536]{1,0:T(8,128)(2,1)S(1)}, u32[]{:S(2)}, u32[]{:S(2)}) collective-permute-start(bf16[128,1536]{1,0:T(8,128)(2,1)S(1)} %get-tuple-element.68), channel_id=1, source_target_pairs={{0,1},{1,0},{2,3},{3,2},{4,5},{5,4},{6,7},{7,6},{8,9},{9,8},{10,11... | collective-permute-start | bytes 1179656 | tf_op jit(solution)/shard_map/ppermute | solution.py:29
  72.6 16.1 %collective-permute-start.12 = (bf16[128,1536]{1,0:T(8,128)(2,1)S(1)}, bf16[128,1536]{1,0:T(8,128)(2,1)S(1)}, u32[]{:S(2)}, u32[]{:S(2)}) collective-permute-start(bf16[128,1536]{1,0:T(8,128)(2,1)S(1)} %shard_map.138), channel_id=1, source_target_pairs={{0,4},{2,6},{4,8},{6,10},{8,12},{10,14},{12,16},{14,18},{16,20},{1... | collective-permute-start | bytes 1179656 | tf_op jit(solution)/shard_map/ppermute | solution.py:435
  73.9 23.3 %collective-permute-start.14 = (bf16[128,1536]{1,0:T(8,128)(2,1)S(1)}, bf16[128,1536]{1,0:T(8,128)(2,1)S(1)}, u32[]{:S(2)}, u32[]{:S(2)}) collective-permute-start(bf16[128,1536]{1,0:T(8,128)(2,1)S(1)} %shard_map.140), channel_id=1, source_target_pairs={{0,4},{2,6},{4,8},{6,10},{8,12},{10,14},{12,16},{14,18},{16,20},{1... | collective-permute-start | bytes 1179656 | tf_op jit(solution)/shard_map/ppermute | solution.py:435
